TPU v7x, 32 devices: a whole 2x2x4 slice. The times are simulated.
32 devices in a mesh: dp: 16 (over z, x, core), mp: 2 (over y).
Axes of the slice: x: 2, y: 2, z: 4, core: 2. Of those that a mesh axis runs over, the one named last changes fastest.
Arguments:
- layer_input: bfloat16 [32, 512, 768], P('dp', 'mp'), may hold values from -6 to 6
- cotangent: bfloat16 [32, 512, 768], P('dp', 'mp'), may hold values from -6 to 6
- lengths: int32 [32, 2], P('dp'), may hold values from 1 to 256, as said below
- bucket: int32 [32], P('dp'), may hold values from 0 to 1
- w_qkv: bfloat16 [2, 3, 768, 768], P(None, None, 'dp', 'mp'), may hold values from -0.21875 to 0.21875
- bias_qv: bfloat16 [2, 2, 768], P(None, None, 'mp'), may hold values from -1.5 to 1.5
- w_out: bfloat16 [2, 768, 768], P(None, 'mp', 'dp'), may hold values from -1.75 to 1.75
- bias_out: bfloat16 [2, 2, 768], replicated, may hold values from -1.5 to 1.5
- ln_gain: bfloat16 [2, 2, 768], replicated, may hold values from 0.099609375 to 1.8984375
- ln_bias: bfloat16 [2, 2, 768], replicated, may hold values from -1.5 to 1.5
- w_up: bfloat16 [2, 768, 3072], P(None, 'dp', 'mp'), may hold values from -0.21875 to 0.21875
- bias_up: bfloat16 [2, 3072], P(None, 'mp'), may hold values from -1.5 to 1.5
- w_down: bfloat16 [2, 3072, 768], P(None, 'mp', 'dp'), may hold values from -0.109375 to 0.109375
Outputs:
- output: bfloat16 [32, 512, 768], P('dp', 'mp')
- input_grad: bfloat16 [32, 512, 768], P('dp', 'mp')
- grad_w_qkv: float32 [2, 3, 768, 768], P(None, None, 'dp', 'mp')
- grad_bias_qv: float32 [2, 2, 768], P(None, None, 'mp')
- grad_w_out: float32 [2, 768, 768], P(None, 'mp', 'dp')
- grad_bias_out: float32 [2, 2, 768], replicated
- grad_ln_gain: float32 [2, 2, 768], replicated
- grad_ln_bias: float32 [2, 2, 768], replicated
- grad_w_up: float32 [2, 768, 3072], P(None, 'dp', 'mp')
- grad_bias_up: float32 [2, 3072], P(None, 'mp')
- grad_w_down: float32 [2, 3072, 768], P(None, 'mp', 'dp')
Inputs may be any that keep to these rules, and one draw needn't show every extreme that they name: `lengths`: each entry is at most 256; in every draw some entry equals 256 and some equals 1. `bucket`: 1 marks a slot holding one item, 0 a slot holding two items.
All inputs are finite; a program needn't handle non-finite values.
Results may differ from a plain program's by a relative error of at most 0.025.
Values may be sent and summed in bfloat16 or wider, within the bound.
A program may use at most 256 MiB of HBM per device.

v0:
```python
import jax
import jax.numpy as jnp
from jax import lax
from jax.sharding import PartitionSpec as P

HEAD_DIM = 64
MICRO = 2


epsilon = 1e-12
masked_score = -1000000000.0


def gelu_exact(values):
    return jax.nn.gelu(values, approximate=False)


def build_mask(lengths, bucket, full_length):
    position = jnp.arange(full_length, dtype=jnp.int32)
    half_len = full_length // 2
    first_len = lengths[:, 0][:, None]
    second_len = lengths[:, 1][:, None]
    packed = (bucket == 0)[:, None]
    upper_half = (position >= half_len)[None, :]
    start_key = jnp.where(packed & upper_half, half_len, 0)
    end_key = jnp.where(
        packed, jnp.where(upper_half, half_len + second_len, first_len), first_len + second_len
    )
    key_pos = position[None, None, :]
    return (key_pos >= start_key[:, :, None]) & (key_pos < end_key[:, :, None])


def normalize(values):
    center = values - jnp.mean(values, axis=-1, keepdims=True)
    variance = jnp.mean(center * center, axis=-1, keepdims=True)
    inverse = lax.rsqrt(variance + epsilon)
    return (center * inverse, inverse)


def norm_back(grad_in, normed, inverse, gain_vec):
    scaled = grad_in * gain_vec
    return inverse * (
        scaled
        - jnp.mean(scaled, axis=-1, keepdims=True)
        - normed * jnp.mean(scaled * normed, axis=-1, keepdims=True)
    )


def gather_rows(values):
    return lax.all_gather(values, "mp", axis=1, tiled=True)


def sum_rows(values):
    return lax.psum_scatter(
        values.astype(jnp.bfloat16), "mp", scatter_dimension=1, tiled=True
    ).astype(jnp.float32)


def gather_grads(values):
    return lax.all_gather(values, "mp", axis=1, tiled=True)


def sum_grads(values):
    return lax.psum_scatter(
        values.astype(jnp.bfloat16), "mp", scatter_dimension=1, tiled=True
    ).astype(jnp.float32)


def attention_scores(queries, keys_low, key_valid):
    scores = (
        jnp.einsum("bqhe,bkhe->bhqk", queries, keys_low, preferred_element_type=jnp.float32) * 0.125
    )
    return jnp.where(key_valid[:, None], scores, masked_score)


def forward_layer(state_in, weights, vectors, key_valid):
    w_qkv, w_out, w_up, w_down = weights
    qv_bias, out_bias, gain_vec, shift_vec, up_bias = vectors
    batch_size = state_in.shape[0]
    full_x = gather_rows(state_in.astype(jnp.bfloat16))
    full_length = full_x.shape[1]
    local_width = w_qkv.shape[2]
    head_count = local_width // HEAD_DIM
    head_shape = (batch_size, full_length, head_count, HEAD_DIM)
    projected = jnp.einsum("bsd,tdc->tbsc", full_x, w_qkv, preferred_element_type=jnp.float32)
    queries = (projected[0] + qv_bias[0]).astype(jnp.bfloat16).reshape(head_shape)
    keys_low = projected[1].astype(jnp.bfloat16).reshape(head_shape)
    values_low = (projected[2] + qv_bias[1]).astype(jnp.bfloat16).reshape(head_shape)
    scores = attention_scores(queries, keys_low, key_valid)
    row_max = jnp.max(scores, axis=-1, keepdims=True)
    log_total = row_max + jnp.log(jnp.sum(jnp.exp(scores - row_max), axis=-1, keepdims=True))
    probs_low = jnp.exp(scores - log_total).astype(jnp.bfloat16)
    context = jnp.einsum(
        "bhqk,bkhe->bqhe", probs_low, values_low, preferred_element_type=jnp.float32
    )
    context = context.astype(jnp.bfloat16).reshape(batch_size, full_length, local_width)
    attn_out = sum_rows(
        jnp.einsum("bsc,cd->bsd", context, w_out, preferred_element_type=jnp.float32)
    )
    normed_one, inverse_one = normalize(state_in + attn_out + out_bias[0])
    hidden = normed_one * gain_vec[0] + shift_vec[0]
    full_hidden = gather_rows(hidden.astype(jnp.bfloat16))
    pre_active = (
        jnp.einsum("bsd,df->bsf", full_hidden, w_up, preferred_element_type=jnp.float32) + up_bias
    )
    active = gelu_exact(pre_active).astype(jnp.bfloat16)
    ffn_out = sum_rows(
        jnp.einsum("bsf,fd->bsd", active, w_down, preferred_element_type=jnp.float32)
    )
    normed_two, inverse_two = normalize(hidden + ffn_out + out_bias[1])
    result = normed_two * gain_vec[1] + shift_vec[1]
    saved_one = (
        full_x,
        queries,
        keys_low,
        values_low,
        log_total,
        context,
        normed_one,
        inverse_one,
        full_hidden,
        pre_active,
        active,
        normed_two,
        inverse_two,
    )
    return (result, saved_one)


def backward_layer(grad_in, saved_one, weights, vectors, key_valid):
    w_qkv, w_out, w_up, w_down = weights
    qv_bias, out_bias, gain_vec, shift_vec, up_bias = vectors
    (
        full_x,
        queries,
        keys_low,
        values_low,
        log_total,
        context,
        normed_one,
        inverse_one,
        full_hidden,
        pre_active,
        active,
        normed_two,
        inverse_two,
    ) = saved_one
    batch_size, full_length, head_count, _ = queries.shape
    local_width = head_count * HEAD_DIM
    flat_shape = (batch_size, full_length, local_width)
    gain_two = jnp.sum(grad_in * normed_two, axis=(0, 1))
    shift_two = jnp.sum(grad_in, axis=(0, 1))
    grad_second = norm_back(grad_in, normed_two, inverse_two, gain_vec[1])
    out_two = jnp.sum(grad_second, axis=(0, 1))
    full_second = gather_grads(grad_second.astype(jnp.bfloat16))
    grad_down = jnp.einsum("bsf,bsd->fd", active, full_second, preferred_element_type=jnp.float32)
    grad_active = jnp.einsum("bsd,fd->bsf", full_second, w_down, preferred_element_type=jnp.float32)
    grad_pre = jax.vjp(gelu_exact, pre_active)[1](grad_active)[0]
    up_grad = jnp.sum(grad_pre, axis=(0, 1))
    pre_low = grad_pre.astype(jnp.bfloat16)
    grad_up = jnp.einsum("bsd,bsf->df", full_hidden, pre_low, preferred_element_type=jnp.float32)
    grad_hidden = (
        sum_grads(jnp.einsum("bsf,df->bsd", pre_low, w_up, preferred_element_type=jnp.float32))
        + grad_second
    )
    gain_one = jnp.sum(grad_hidden * normed_one, axis=(0, 1))
    shift_one = jnp.sum(grad_hidden, axis=(0, 1))
    grad_first = norm_back(grad_hidden, normed_one, inverse_one, gain_vec[0])
    out_one = jnp.sum(grad_first, axis=(0, 1))
    full_first = gather_grads(grad_first.astype(jnp.bfloat16))
    grad_out = jnp.einsum("bsc,bsd->cd", context, full_first, preferred_element_type=jnp.float32)
    grad_context = jnp.einsum("bsd,cd->bsc", full_first, w_out, preferred_element_type=jnp.float32)
    grad_context = grad_context.astype(jnp.bfloat16).reshape(queries.shape)
    scores = attention_scores(queries, keys_low, key_valid)
    attn_probs = jnp.exp(scores - log_total)
    probs_low = attn_probs.astype(jnp.bfloat16)
    grad_probs = jnp.einsum(
        "bqhe,bkhe->bhqk", grad_context, values_low, preferred_element_type=jnp.float32
    )
    grad_value = jnp.einsum(
        "bhqk,bqhe->bkhe", probs_low, grad_context, preferred_element_type=jnp.float32
    )
    grad_scores = attn_probs * (
        grad_probs - jnp.sum(attn_probs * grad_probs, axis=-1, keepdims=True)
    )
    scores_low = jnp.where(key_valid[:, None], grad_scores, 0.0).astype(jnp.bfloat16)
    grad_query = (
        jnp.einsum("bhqk,bkhe->bqhe", scores_low, keys_low, preferred_element_type=jnp.float32)
        * 0.125
    )
    grad_key = (
        jnp.einsum("bhqk,bqhe->bkhe", scores_low, queries, preferred_element_type=jnp.float32)
        * 0.125
    )
    grad_query = grad_query.reshape(flat_shape)
    grad_key = grad_key.reshape(flat_shape)
    grad_value = grad_value.reshape(flat_shape)
    qv_grad = jnp.stack([jnp.sum(grad_query, axis=(0, 1)), jnp.sum(grad_value, axis=(0, 1))])
    grad_proj = jnp.stack([grad_query, grad_key, grad_value], axis=0).astype(jnp.bfloat16)
    grad_qkv = jnp.einsum("bsd,tbsc->tdc", full_x, grad_proj, preferred_element_type=jnp.float32)
    grad_prev = (
        sum_grads(jnp.einsum("tbsc,tdc->bsd", grad_proj, w_qkv, preferred_element_type=jnp.float32))
        + grad_first
    )
    matrices = (grad_qkv, grad_out, grad_up, grad_down)
    vector_set = (
        qv_grad,
        jnp.stack([out_one, out_two]),
        jnp.stack([gain_one, gain_two]),
        jnp.stack([shift_one, shift_two]),
        up_grad,
    )
    return (grad_prev, matrices, vector_set)


def per_device(
    layer_input,
    cotangent,
    lengths,
    bucket,
    w_qkv,
    bias_qv,
    w_out,
    bias_out,
    ln_gain,
    ln_bias,
    w_up,
    bias_up,
    w_down,
):
    layers = w_qkv.shape[0]
    slot_count, row_count, width = layer_input.shape
    per_batch = slot_count // MICRO
    full_length = row_count * lax.axis_size("mp")
    part_index = lax.axis_index("mp")
    local_width = w_qkv.shape[3]
    up_width = w_up.shape[2]
    vectors = [
        (
            bias_qv[layer_index].astype(jnp.float32),
            bias_out[layer_index].astype(jnp.float32),
            ln_gain[layer_index].astype(jnp.float32),
            ln_bias[layer_index].astype(jnp.float32),
            bias_up[layer_index].astype(jnp.float32),
        )
        for layer_index in range(layers)
    ]
    matrix_sums = [None] * layers
    vector_sums = [None] * layers
    outputs = []
    input_grads = []
    for batch_index in range(MICRO):
        weights = [
            (
                lax.all_gather(w_qkv[layer_index], "dp", axis=1, tiled=True),
                lax.all_gather(w_out[layer_index], "dp", axis=1, tiled=True),
                lax.all_gather(w_up[layer_index], "dp", axis=0, tiled=True),
                lax.all_gather(w_down[layer_index], "dp", axis=1, tiled=True),
            )
            for layer_index in range(layers)
        ]
        first_slot = batch_index * per_batch
        last_slot = first_slot + per_batch
        key_valid = build_mask(
            lengths[first_slot:last_slot], bucket[first_slot:last_slot], full_length
        )
        current = layer_input[first_slot:last_slot].astype(jnp.float32)
        kept_all = []
        for layer_index in range(layers):
            current, saved_one = forward_layer(
                current, weights[layer_index], vectors[layer_index], key_valid
            )
            kept_all.append(saved_one)
        outputs.append(current.astype(jnp.bfloat16))
        grad_now = cotangent[first_slot:last_slot].astype(jnp.float32)
        for layer_index in reversed(range(layers)):
            grad_now, matrices, vector_set = backward_layer(
                grad_now,
                kept_all[layer_index],
                weights[layer_index],
                vectors[layer_index],
                key_valid,
            )
            if matrix_sums[layer_index] is None:
                matrix_sums[layer_index] = matrices
                vector_sums[layer_index] = vector_set
            else:
                matrix_sums[layer_index] = jax.tree.map(jnp.add, matrix_sums[layer_index], matrices)
                vector_sums[layer_index] = jax.tree.map(
                    jnp.add, vector_sums[layer_index], vector_set
                )
        input_grads.append(grad_now.astype(jnp.bfloat16))
    qkv_stack = jnp.stack([matrix_sums[index_one][0] for index_one in range(layers)])
    out_stack = jnp.stack([matrix_sums[index_one][1] for index_one in range(layers)])
    up_stack = jnp.stack([matrix_sums[index_one][2] for index_one in range(layers)])
    down_stack = jnp.stack([matrix_sums[index_one][3] for index_one in range(layers)])
    grad_qkv, grad_out, grad_up, grad_down = (
        lax.psum_scatter(qkv_stack, "dp", scatter_dimension=2, tiled=True),
        lax.psum_scatter(out_stack, "dp", scatter_dimension=2, tiled=True),
        lax.psum_scatter(up_stack, "dp", scatter_dimension=1, tiled=True),
        lax.psum_scatter(down_stack, "dp", scatter_dimension=2, tiled=True),
    )
    qv_local = jnp.stack([vector_sums[index_one][0] for index_one in range(layers)])
    up_local = jnp.stack([vector_sums[index_one][4] for index_one in range(layers)])
    qv_full = lax.dynamic_update_slice(
        jnp.zeros((layers, 2, width), jnp.float32), qv_local, (0, 0, part_index * local_width)
    )
    up_full = lax.dynamic_update_slice(
        jnp.zeros((layers, up_width * lax.axis_size("mp")), jnp.float32),
        up_local,
        (0, part_index * up_width),
    )
    bias_stack = jnp.stack([vector_sums[index_one][1] for index_one in range(layers)])
    gain_stack = jnp.stack([vector_sums[index_one][2] for index_one in range(layers)])
    shift_stack = jnp.stack([vector_sums[index_one][3] for index_one in range(layers)])
    qv_total, bias_total, gain_total, shift_total, up_total = lax.psum(
        (qv_full, bias_stack, gain_stack, shift_stack, up_full), ("dp", "mp")
    )
    grad_qv = lax.dynamic_slice_in_dim(qv_total, part_index * local_width, local_width, 2)
    grad_bias_up = lax.dynamic_slice_in_dim(up_total, part_index * up_width, up_width, 1)
    return (
        jnp.concatenate(outputs, 0),
        jnp.concatenate(input_grads, 0),
        grad_qkv,
        grad_qv,
        grad_out,
        bias_total,
        gain_total,
        shift_total,
        grad_up,
        grad_bias_up,
        grad_down,
    )


def solution(mesh):
    in_specs = (
        P("dp", "mp", None),
        P("dp", "mp", None),
        P("dp", None),
        P("dp"),
        P(None, None, "dp", "mp"),
        P(None, None, "mp"),
        P(None, "mp", "dp"),
        P(),
        P(),
        P(),
        P(None, "dp", "mp"),
        P(None, "mp"),
        P(None, "mp", "dp"),
    )
    out_specs = (
        P("dp", "mp", None),
        P("dp", "mp", None),
        P(None, None, "dp", "mp"),
        P(None, None, "mp"),
        P(None, "mp", "dp"),
        P(),
        P(),
        P(),
        P(None, "dp", "mp"),
        P(None, "mp"),
        P(None, "mp", "dp"),
    )
    return jax.shard_map(
        per_device, mesh=mesh, in_specs=in_specs, out_specs=out_specs, check_vma=False
    )
```

profile of v0, /device:TPU:0, one launch (start us, length us, event | category | flops | bytes accessed | tf_op | source)
XLA Modules:
  0.0 1486.0 jit_solution(9868295935677100200)
XLA Ops:
  20.3 12.8 all_gather.81
  44.6 23.1 %all-gather.1 = bf16[1,384,768]{1,2,0:T(8,128)(2,1)S(1)} all-gather(bf16[1,384,48]{1,2,0:T(8,128)(2,1)S(1)} %get-tuple-element.190), channel_id=3, replica_groups=mesh['dp'=16,'mp'=2] {'dp'}, dimensions={2}, use_global_device_ids=true | all-gather | bytes 626688 | tf_op jit(solution)/shard_map/all_gather | solution.py:256
  98.0 19.1 %reduce-scatter.26.cloned.1.call-done = bf16[1,256,768]{2,1,0:T(8,128)(2,1)} async-done(((bf16[1,512,768]{2,1,0:T(8,128)(2,1)}), bf16[1,256,768]{2,1,0:T(8,128)(2,1)}) %reduce-scatter.26.cloned.1.call-update) | async-done | bytes 393232 | tf_op jit(solution)/shard_map/reduce_scatter | solution.py:54
  133.1 29.1 %all-gather.17.cloned.1.call-done = bf16[1,768,1536]{2,1,0:T(8,128)(2,1)} async-done(((bf16[1,48,1536]{2,1,0:T(8,128)(2,1)}), bf16[1,768,1536]{2,1,0:T(8,128)(2,1)}) %all-gather.17.cloned.1.call-update) | async-done | bytes 2359312 | tf_op jit(solution)/shard_map/all_gather | solution.py:257
  173.1 32.9 %all-gather.19.cloned.1.call-done = bf16[1,1536,768]{1,2,0:T(8,128)(2,1)} async-done(((bf16[1,1536,48]{1,2,0:T(8,128)(2,1)}), bf16[1,1536,768]{1,2,0:T(8,128)(2,1)}) %all-gather.19.cloned.1.call-update) | async-done | bytes 2359312 | tf_op jit(solution)/shard_map/all_gather | solution.py:258
  210.0 19.0 %all_gather.83 = bf16[1,512,768]{2,1,0:T(8,128)(2,1)S(1)} all-gather(bf16[1,256,768]{2,1,0:T(8,128)(2,1)S(1)} %get-tuple-element.156), channel_id=1, replica_groups=mesh['dp'=16,'mp'=2] {'mp'}, dimensions={1}, use_global_device_ids=true | all-gather | bytes 1179648 | tf_op jit(solution)/shard_map/all_gather | solution.py:50
  244.6 20.4 %all-gather.5 = bf16[1,384,768]{1,2,0:T(8,128)(2,1)} all-gather(bf16[1,384,48]{1,2,0:T(8,128)(2,1)S(1)} %get-tuple-element.189), channel_id=7, replica_groups=mesh['dp'=16,'mp'=2] {'dp'}, dimensions={2}, use_global_device_ids=true | all-gather | bytes 626688 | tf_op jit(solution)/shard_map/all_gather | solution.py:256
  268.4 12.8 all_gather.94
  281.2 21.6 %all-gather.21.cloned.1.call-done = bf16[1,3,768,384]{3,2,1,0:T(8,128)(2,1)} async-done(((bf16[1,3,48,384]{3,2,1,0:T(8,128)(2,1)}), bf16[1,3,768,384]{3,2,1,0:T(8,128)(2,1)}) %all-gather.21.cloned.1.call-update) | async-done | bytes 1769488 | tf_op jit(solution)/shard_map/all_gather | solution.py:255
  306.4 12.2 all_gather.86
  346.4 19.6 %reduce-scatter.22.cloned.1.call-done = bf16[1,256,768]{2,1,0:T(8,128)(2,1)} async-done(((bf16[1,512,768]{2,1,0:T(8,128)(2,1)}), bf16[1,256,768]{2,1,0:T(8,128)(2,1)}) %reduce-scatter.22.cloned.1.call-update) | async-done | bytes 393232 | tf_op jit(solution)/shard_map/reduce_scatter | solution.py:54
  380.9 29.8 %all-gather.23.cloned.1.call-done = bf16[1,768,1536]{2,1,0:T(8,128)(2,1)} async-done(((bf16[1,48,1536]{2,1,0:T(8,128)(2,1)}), bf16[1,768,1536]{2,1,0:T(8,128)(2,1)}) %all-gather.23.cloned.1.call-update) | async-done | bytes 2359312 | tf_op jit(solution)/shard_map/all_gather | solution.py:257
  421.9 32.1 %all-gather.25.cloned.1.call-done = bf16[1,1536,768]{1,2,0:T(8,128)(2,1)} async-done(((bf16[1,1536,48]{1,2,0:T(8,128)(2,1)}), bf16[1,1536,768]{1,2,0:T(8,128)(2,1)}) %all-gather.25.cloned.1.call-update) | async-done | bytes 2359312 | tf_op jit(solution)/shard_map/all_gather | solution.py:258
  458.5 18.3 %all_gather.89 = bf16[1,512,768]{2,1,0:T(8,128)(2,1)S(1)} all-gather(bf16[1,256,768]{2,1,0:T(8,128)(2,1)} %get-tuple-element.195), channel_id=1, replica_groups=mesh['dp'=16,'mp'=2] {'mp'}, dimensions={1}, use_global_device_ids=true | all-gather | bytes 1179648 | tf_op jit(solution)/shard_map/all_gather | solution.py:50
  492.0 15.2 %reduce-scatter.24.cloned.1.call-done = bf16[1,256,768]{2,1,0:T(8,128)(2,1)} async-done(((bf16[1,512,768]{2,1,0:T(8,128)(2,1)}), bf16[1,256,768]{2,1,0:T(8,128)(2,1)}) %reduce-scatter.24.cloned.1.call-update) | async-done | bytes 393232 | tf_op jit(solution)/shard_map/reduce_scatter | solution.py:54
  512.6 11.7 all_gather.100
  530.1 15.6 %all_gather.96 = bf16[1,512,768]{2,1,0:T(8,128)(2,1)S(1)} all-gather(bf16[1,256,768]{2,1,0:T(8,128)(2,1)} %get-tuple-element.124), channel_id=1, replica_groups=mesh['dp'=16,'mp'=2] {'mp'}, dimensions={1}, use_global_device_ids=true | all-gather | bytes 1179648 | tf_op jit(solution)/shard_map/all_gather | solution.py:60
  576.4 11.7 all_gather.101
  593.3 13.9 fusion.512
  607.1 13.5 fusion.327
  652.2 13.3 fusion.514
  730.6 15.8 %all_gather.98 = bf16[1,512,768]{2,1,0:T(8,128)(2,1)S(1)} all-gather(bf16[1,256,768]{2,1,0:T(8,128)(2,1)S(1)} %get-tuple-element.120), channel_id=1, replica_groups=mesh['dp'=16,'mp'=2] {'mp'}, dimensions={1}, use_global_device_ids=true | all-gather | bytes 1179648 | tf_op jit(solution)/shard_map/all_gather | solution.py:60
  778.2 11.7 all_gather.99
  794.8 13.2 fusion.510
  846.4 13.0 fusion.508
  877.4 15.0 %copy.105 = f32[2,1536,768]{1,0,2:T(2,128)} copy(f32[2,1536,768]{2,1,0:T(8,128)} %pad_maximum_fusion.1) | data formatting | bytes 18874368 | tf_op jit(solution)/shard_map/stack | solution.py:296
  921.1 13.6 copy.103
  950.8 31.9 %all-reduce.8.cloned.1.call-done = (f32[2,2,768]{2,1,0:T(2,128)}, f32[2,2,768]{2,1,0:T(2,128)}, f32[2,2,768]{2,1,0:T(2,128)}, f32[2,2,768]{2,1,0:T(2,128)}, f32[2,3072]{1,0:T(2,128)}) async-done(((f32[2,2,768]{2,1,0:T(2,128)}, f32[2,2,768]{2,1,0:T(2,128)}, f32[2,2,768]{2,1,0:T(2,128)}, f32[2,2,768]{2,1,0:T(2,128)}, f32[2,3072]{1,0:T(2,128)}), (f32[2,2,768]{2,1,0:T(2,128)}, f32[2,2,768]{2,1,0:T(2,128)}, ...) | async-done | bytes 73744 | tf_op jit(solution)/shard_map/psum | solution.py:316
  985.3 20.1 %reduce-scatter.40.cloned.1.call-done = bf16[1,256,768]{2,1,0:T(8,128)(2,1)} async-done(((bf16[1,512,768]{2,1,0:T(8,128)(2,1)}), bf16[1,256,768]{2,1,0:T(8,128)(2,1)}) %reduce-scatter.40.cloned.1.call-update) | async-done | bytes 393232 | tf_op jit(solution)/shard_map/reduce_scatter | solution.py:64
  1006.5 19.3 %reduce-scatter.48.cloned.1.call-done = bf16[1,256,768]{2,1,0:T(8,128)(2,1)} async-done(((bf16[1,512,768]{2,1,0:T(8,128)(2,1)}), bf16[1,256,768]{2,1,0:T(8,128)(2,1)}) %reduce-scatter.48.cloned.1.call-update) | async-done | bytes 393232 | tf_op jit(solution)/shard_map/reduce_scatter | solution.py:64
  1027.8 332.9 %all-reduce.10.cloned.1.call-done = (f32[2,3,768,384]{3,0,1,2:T(2,128)}, f32[2,384,768]{1,0,2:T(2,128)}, f32[2,1536,768]{1,0,2:T(2,128)}) async-done(((f32[2,3,768,384]{3,0,1,2:T(2,128)}, f32[2,384,768]{1,0,2:T(2,128)}, f32[2,1536,768]{1,0,2:T(2,128)}), (f32[2,3,768,384]{3,0,1,2:T(2,128)}, f32[2,384,768]{1,0,2:T(2,128)}, f32[2,1536,768]{1,0,2:T(2,128)})) %all-reduce.10.cloned.1.call-update) | async-done | bytes 18874384
  1366.4 111.1 %reduce-scatter.50.cloned.1.call-done = f32[2,48,1536]{2,1,0:T(8,128)} async-done(((f32[2,768,1536]{2,1,0:T(8,128)}), f32[2,48,1536]{2,1,0:T(8,128)}) %reduce-scatter.50.cloned.1.call-update) | async-done | bytes 589840 | tf_op jit(solution)/shard_map/reduce_scatter | solution.py:300
  (667 shorter events, 468.1 us)
Async XLA Ops:
  7.2 60.5 %all-gather.15.cloned.1.call-start = ((), (), s32[]{:S(2)}) async-start(), calls=%async_computation.34 | async-start | bytes 1880064 | tf_op jit(solution)/shard_map/all_gather | solution.py:255
  8.9 87.8 %reduce-scatter.18.cloned.1.call-start = ((), (), s32[]{:S(2)}) async-start(), calls=%async_computation.17 | async-start | bytes 1179648 | tf_op jit(solution)/shard_map/reduce_scatter | solution.py:54
  81.9 35.3 %reduce-scatter.26.cloned.1.call-start = ((), (), s32[]{:S(2)}) async-start(), calls=%async_computation.21 | async-start | bytes 1179648 | tf_op jit(solution)/shard_map/reduce_scatter | solution.py:54
  89.5 72.6 %all-gather.17.cloned.1.call-start = ((), (), s32[]{:S(2)}) async-start(), calls=%async_computation.35 | async-start | bytes 2506752 | tf_op jit(solution)/shard_map/all_gather | solution.py:257
  90.4 115.6 %all-gather.19.cloned.1.call-start = ((), (), s32[]{:S(2)}) async-start(), calls=%async_computation.36 | async-start | bytes 2506752 | tf_op jit(solution)/shard_map/all_gather | solution.py:258
  91.2 173.7 %reduce-scatter.28.cloned.1.call-start = ((), (), s32[]{:S(2)}) async-start(), calls=%async_computation.22 | async-start | bytes 1179648 | tf_op jit(solution)/shard_map/reduce_scatter | solution.py:54
  91.3 173.6 %copy-start.123 = (f32[768]{0:T(1024)}, f32[768]{0:T(1024)S(1)}, u32[]{:S(2)}) copy-start(f32[768]{0:T(1024)S(1)} %get-tuple-element.95) | copy-start | bytes 9220
  91.4 173.5 %copy-start.125 = (f32[768]{0:T(1024)}, f32[768]{0:T(1024)S(1)}, u32[]{:S(2)}) copy-start(f32[768]{0:T(1024)S(1)} %get-tuple-element.91) | copy-start | bytes 9220
  98.0 166.9 %copy-start.136 = (f32[256]{0:T(256)}, f32[256]{0:T(256)S(1)}, u32[]{:S(2)}) copy-start(f32[256]{0:T(256)S(1)} %broadcast_multiply_fusion.23) | copy-start | bytes 3076
  118.7 146.3 %copy-start.134 = (f32[256]{0:T(256)}, f32[256]{0:T(256)S(1)}, u32[]{:S(2)}) copy-start(f32[256]{0:T(256)S(1)} %broadcast_multiply_fusion.19) | copy-start | bytes 3076
  210.0 54.9 %reduce-scatter.20.cloned.1.call-start = ((), (), s32[]{:S(2)}) async-start(), calls=%async_computation.18 | async-start | bytes 1179648 | tf_op jit(solution)/shard_map/reduce_scatter | solution.py:54
  243.6 59.1 %all-gather.21.cloned.1.call-start = ((), (), s32[]{:S(2)}) async-start(), calls=%async_computation.37 | async-start | bytes 1880064 | tf_op jit(solution)/shard_map/all_gather | solution.py:255
  244.4 102.0 %reduce-scatter.30.cloned.1.call-start = ((), (), s32[]{:S(2)}) async-start(), calls=%async_computation.23 | async-start | bytes 1179648 | tf_op jit(solution)/shard_map/reduce_scatter | solution.py:54
  329.9 36.1 %reduce-scatter.22.cloned.1.call-start = ((), (), s32[]{:S(2)}) async-start(), calls=%async_computation.19 | async-start | bytes 1179648 | tf_op jit(solution)/shard_map/reduce_scatter | solution.py:54
  338.4 72.3 %all-gather.23.cloned.1.call-start = ((), (), s32[]{:S(2)}) async-start(), calls=%async_computation.38 | async-start | bytes 2506752 | tf_op jit(solution)/shard_map/all_gather | solution.py:257
  339.1 114.8 %all-gather.25.cloned.1.call-start = ((), (), s32[]{:S(2)}) async-start(), calls=%async_computation.39 | async-start | bytes 2506752 | tf_op jit(solution)/shard_map/all_gather | solution.py:258
  339.7 152.3 %reduce-scatter.32.cloned.1.call-start = ((), (), s32[]{:S(2)}) async-start(), calls=%async_computation.24 | async-start | bytes 1179648 | tf_op jit(solution)/shard_map/reduce_scatter | solution.py:54
  458.5 48.8 %reduce-scatter.24.cloned.1.call-start = ((), (), s32[]{:S(2)}) async-start(), calls=%async_computation.20 | async-start | bytes 1179648 | tf_op jit(solution)/shard_map/reduce_scatter | solution.py:54
  491.6 69.2 %reduce-scatter.42.cloned.1.call-start = ((), (), s32[]{:S(2)}) async-start(), calls=%async_computation.29 | async-start | bytes 1179648 | tf_op jit(solution)/shard_map/reduce_scatter | solution.py:64
  530.0 43.0 %reduce-scatter.34.cloned.1.call-start = ((), (), s32[]{:S(2)}) async-start(), calls=%async_computation.25 | async-start | bytes 1179648 | tf_op jit(solution)/shard_map/reduce_scatter | solution.py:64
  555.4 146.4 %reduce-scatter.44.cloned.1.call-start = ((), (), s32[]{:S(2)}) async-start(), calls=%async_computation.30 | async-start | bytes 1179648 | tf_op jit(solution)/shard_map/reduce_scatter | solution.py:64
  647.2 60.5 %reduce-scatter.36.cloned.1.call-start = ((), (), s32[]{:S(2)}) async-start(), calls=%async_computation.26 | async-start | bytes 1179648 | tf_op jit(solution)/shard_map/reduce_scatter | solution.py:64
  690.1 74.0 %reduce-scatter.46.cloned.1.call-start = ((), (), s32[]{:S(2)}) async-start(), calls=%async_computation.31 | async-start | bytes 1179648 | tf_op jit(solution)/shard_map/reduce_scatter | solution.py:64
  730.2 42.8 %reduce-scatter.38.cloned.1.call-start = ((), (), s32[]{:S(2)}) async-start(), calls=%async_computation.27 | async-start | bytes 1179648 | tf_op jit(solution)/shard_map/reduce_scatter | solution.py:64
  755.4 227.4 %all-reduce.8.cloned.1.call-start = ((), (), s32[]{:S(2)}) async-start(), calls=%async_computation.40 | async-start | bytes 147456 | tf_op jit(solution)/shard_map/psum | solution.py:316
  862.3 143.0 %reduce-scatter.40.cloned.1.call-start = ((), (), s32[]{:S(2)}) async-start(), calls=%async_computation.28 | async-start | bytes 1179648 | tf_op jit(solution)/shard_map/reduce_scatter | solution.py:64
  866.5 159.3 %reduce-scatter.48.cloned.1.call-start = ((), (), s32[]{:S(2)}) async-start(), calls=%async_computation.32 | async-start | bytes 1179648 | tf_op jit(solution)/shard_map/reduce_scatter | solution.py:64
  907.5 453.3 %all-reduce.10.cloned.1.call-start = ((), (), s32[]{:S(2)}) async-start(), calls=%async_computation.41 | async-start | bytes 37748736
  934.7 542.8 %reduce-scatter.50.cloned.1.call-start = ((), (), s32[]{:S(2)}) async-start(), calls=%async_computation.33 | async-start | bytes 10027008 | tf_op jit(solution)/shard_map/reduce_scatter | solution.py:300
  1026.9 450.6 %copy-start.149 = (f32[2,2,768]{2,1,0:T(2,128)S(1)}, f32[2,2,768]{2,1,0:T(2,128)}, u32[]{:S(2)}) copy-start(f32[2,2,768]{2,1,0:T(2,128)} %get-tuple-element.270) | copy-start | bytes 36868
  1026.9 451.2 %copy-start.148 = (f32[2,2,768]{2,1,0:T(2,128)S(1)}, f32[2,2,768]{2,1,0:T(2,128)}, u32[]{:S(2)}) copy-start(f32[2,2,768]{2,1,0:T(2,128)} %get-tuple-element.271) | copy-start | bytes 36868
  1026.9 451.8 %copy-start.147 = (f32[2,2,768]{2,1,0:T(2,128)S(1)}, f32[2,2,768]{2,1,0:T(2,128)}, u32[]{:S(2)}) copy-start(f32[2,2,768]{2,1,0:T(2,128)} %get-tuple-element.272) | copy-start | bytes 36868
  (165 other events, 1806.6 us)
Sparse Core Ops, SparseCore 0:
  10.9 43.3 all-gather.14
  82.0 14.7 reduce-scatter.17
  99.7 17.4 reduce-scatter.25
  119.9 42.2 all-gather.16
  164.9 41.0 all-gather.18
  210.1 21.8 reduce-scatter.27
  243.7 15.6 reduce-scatter.19
  262.4 40.3 all-gather.20
  330.0 16.3 reduce-scatter.29
  348.6 17.4 reduce-scatter.21
  368.3 42.3 all-gather.22
  412.8 41.0 all-gather.24
  458.6 21.5 reduce-scatter.31
  491.7 15.5 reduce-scatter.23
  530.1 20.2 reduce-scatter.41
  555.6 17.4 reduce-scatter.33
  647.3 17.4 reduce-scatter.43
  690.2 17.4 reduce-scatter.35
  730.3 20.4 reduce-scatter.45
  755.5 17.4 reduce-scatter.37
  862.4 120.2 all-reduce.7
  985.0 20.3 reduce-scatter.39
  1008.3 17.4 reduce-scatter.47
  1030.1 330.6 all-reduce.9
  1366.0 111.4 reduce-scatter.49
where the time goes:
time: 1500 us; the launch traced here: 1490 us
  waiting for transfers between devices  751 us (50%)
  matrix products  307 us (20%)
  blocking collectives  253 us (17%)
  local copies, waits for them, and re-layouts  88.6 us (6%)
  other arithmetic  61.2 us (4%)
  between operations  22.6 us (2%)
    unnamed x26, waiting for transfers between devices  335 us
    reduce_scatter x1, waiting for transfers between devices, per_device(): lax.psum_scatter(up_stack, 'dp', scatter_dimension=1, tiled=True)  111 us
    all_gather x8, blocking collectives, gather_rows(): return lax.all_gather(values, 'mp', axis=1, tiled=True)  109 us
    all_gather x8, blocking collectives, gather_grads(): return lax.all_gather(values, 'mp', axis=1, tiled=True)  100 us
    reduce_scatter x8, waiting for transfers between devices, sum_rows(): lax.psum_scatter(values.astype(jnp.bfloat16), 'mp', scatter_dimension=1,...  65.6 us
    all_gather x2, waiting for transfers between devices, per_device(): lax.all_gather(w_down[layer_index], 'dp', axis=1, tiled=True)  64.9 us
    reduce_scatter x8, waiting for transfers between devices, sum_grads(): lax.psum_scatter(values.astype(jnp.bfloat16), 'mp', scatter_dimension=1,...  61.8 us
    all_gather x2, waiting for transfers between devices, per_device(): lax.all_gather(w_up[layer_index], 'dp', axis=0, tiled=True)  58.9 us
  transfers between devices with their start and end apart: 25, of which 18 were waited for; matrix products, arithmetic and copies ran while one was open for 18% of the time, Pallas kernels for 0%

commit v1 on v0

v1 whole, which is shorter than its diff:
```python
import functools
import jax
import jax.numpy as jnp
from jax import lax
from jax.experimental import pallas as pl
from jax.experimental.pallas import tpu as pltpu
from jax.sharding import PartitionSpec as P

HEAD_DIM = 64
GROUPS = 16
MESH = pl.DeviceIdType.MESH


class Place:
    def __init__(self, fold):
        d = lax.axis_index("dp")
        self.fold = fold
        self.member = lax.rem(d, fold) if fold > 1 else 0
        g = d // fold if fold > 1 else d
        self.z = g // 4
        self.xc = lax.rem(g, 4)
        self.x = self.xc // 2
        self.c = lax.rem(self.xc, 2)
        self.y = lax.axis_index("mp")
    def dev(self, z, xc, y):
        return {"dp": (z * 4 + xc) * self.fold + self.member, "mp": y}

def gather_kernel(fold, nk, packed, w, lsem, zs, zr, xs, xr, ys, yr, fs, fr, cs, cr):
    p = Place(fold)
    z, xc, y = p.z, p.xc, p.y
    xo = (1 - p.x) * 2 + p.c
    co = p.x * 2 + (1 - p.c)
    yo = 1 - y
    barrier = pltpu.get_barrier_semaphore()
    peers = [p.dev(lax.rem(z + dz, 4), xc, y) for dz in (1, 2, 3)] + [p.dev(z, xo, y), p.dev(z, xc, yo), p.dev(z, co, y)]
    for d in peers:
        pl.semaphore_signal(barrier, inc=1, device_id=d, device_id_type=MESH)
    pl.semaphore_wait(barrier, 6)
    zj = [lax.rem(z + 4 - j, 4) for j in range(4)]
    def rc(src, dst, s, r, dev):
        return pltpu.make_async_remote_copy(src_ref=src, dst_ref=dst, send_sem=s, recv_sem=r, device_id=dev, device_id_type=MESH)
    sends = []
    def go(c):
        c.start(); sends.append(c)
    def own(k): return pltpu.make_async_copy(packed.at[k], w.at[k, y, z, xc], lsem.at[k])
    def zcopy(k, j): return rc(packed.at[k], w.at[k, y, z, xc], zs.at[k, j - 1], zr.at[k, j - 1], p.dev(lax.rem(z + j, 4), xc, y))
    def src(k, j): return packed.at[k] if j == 0 else w.at[k, y, zj[j], xc]
    def xcopy(k, j): return rc(src(k, j), w.at[k, y, zj[j], xc], xs.at[k, j], xr.at[k, j], p.dev(z, xo, y))
    def ycopy(k, j): return rc(src(k, j), w.at[k, y, zj[j], xc], ys.at[k, j], yr.at[k, j], p.dev(z, xc, yo))
    def fcopy(k, j):
        if j % 2 == 0:
            b = w.at[k, y, zj[j], xo]
            return rc(b, b, fs.at[k, j], fr.at[k, j], p.dev(z, xc, yo))
        b = w.at[k, yo, zj[j], xc]
        return rc(b, b, fs.at[k, j], fr.at[k, j], p.dev(z, xo, y))
    cols = [(y, xc), (y, xo), (yo, xc), (yo, xo)]
    def ccopy(k, i):
        cy, cx = cols[i]
        b = w.at[k, cy, :, cx]
        return rc(b, b, cs.at[k, i], cr.at[k, i], p.dev(z, co, y))
    def a(k):
        own(k).start()
        for j in (1, 2, 3): go(zcopy(k, j))
        go(xcopy(k, 0)); go(ycopy(k, 0))
    def b(k):
        for j in (1, 2, 3):
            zcopy(k, j).wait_recv()
            go(xcopy(k, j)); go(ycopy(k, j))
        own(k).wait()
        go(ccopy(k, 0))
    def c(k):
        for j in range(4):
            xcopy(k, j).wait_recv()
            if j % 2 == 0: go(fcopy(k, j))
            ycopy(k, j).wait_recv()
            if j % 2 == 1: go(fcopy(k, j))
        go(ccopy(k, 1)); go(ccopy(k, 2))
    def d(k):
        for j in range(4): fcopy(k, j).wait_recv()
        go(ccopy(k, 3))
    def e(k):
        for i in range(4): ccopy(k, i).wait_recv()
    a(0); a(1); b(0)
    for k in range(nk + 2):
        if k + 2 < nk: a(k + 2)
        if k + 1 < nk: b(k + 1)
        if k < nk: c(k)
        if 0 <= k - 1 < nk: d(k - 1)
        if 0 <= k - 2 < nk: e(k - 2)
    for s in sends: s.wait_send()

def gather(packed, fold=1, collective_id=1):
    nk, rows, cols = packed.shape
    D = pltpu.SemaphoreType.DMA
    return pl.pallas_call(
        functools.partial(gather_kernel, fold, nk),
        out_shape=jax.ShapeDtypeStruct((nk, 2, 4, 4, rows, cols), jnp.bfloat16),
        in_specs=[pl.BlockSpec(memory_space=pl.ANY)],
        out_specs=pl.BlockSpec(memory_space=pl.ANY),
        scratch_shapes=[D((nk,)), D((nk, 3)), D((nk, 3)), D((nk, 4)), D((nk, 4)), D((nk, 4)), D((nk, 4)), D((nk, 4)), D((nk, 4)), D((nk, 4)), D((nk, 4))],
        compiler_params=pltpu.CompilerParams(collective_id=collective_id, has_side_effects=True),
    )(packed)

def scatter_kernel(fold, nk, grads, out, own, rcb, rx, ry, rx2, ry2, rz, lsem, cs, cr, xs, xr, ys, yr, zs, zr):
    p = Place(fold)
    z, xc, y, x, c0 = p.z, p.xc, p.y, p.x, p.c
    xo = (1 - p.x) * 2 + p.c
    co = p.x * 2 + (1 - p.c)
    yo = 1 - y
    barrier = pltpu.get_barrier_semaphore()
    peers = [p.dev(lax.rem(z + dz, 4), xc, y) for dz in (1, 2, 3)] + [p.dev(z, xo, y), p.dev(z, xc, yo), p.dev(z, co, y)]
    for d in peers:
        pl.semaphore_signal(barrier, inc=1, device_id=d, device_id_type=MESH)
    pl.semaphore_wait(barrier, 6)
    def rc(src, dst, s, r, dev):
        return pltpu.make_async_remote_copy(src_ref=src, dst_ref=dst, send_sem=s, recv_sem=r, device_id=dev, device_id_type=MESH)
    sends = []
    def go(c):
        c.start(); sends.append(c)
    F = jnp.float32
    def load(k): return pltpu.make_async_copy(grads.at[k, :, :, :, c0], own.at[k], lsem.at[k])
    def ccopy(k): return rc(grads.at[k, :, :, :, 1 - c0], rcb.at[k], cs.at[k], cr.at[k], p.dev(z, co, y))
    def x1(k): return rc(own.at[k, :, 0:2, 1 - x], rx.at[k], xs.at[k, 0], xr.at[k, 0], p.dev(z, xo, y))
    def y1(k): return rc(own.at[k, 1 - y, 2:4], ry.at[k], ys.at[k, 0], yr.at[k, 0], p.dev(z, xc, yo))
    def y2(k): return rc(own.at[k, 1 - y, 0:2, x], ry2.at[k], ys.at[k, 1], yr.at[k, 1], p.dev(z, xc, yo))
    def x2(k): return rc(own.at[k, y, 2:4, 1 - x], rx2.at[k], xs.at[k, 1], xr.at[k, 1], p.dev(z, xo, y))
    def zc(k, j):
        zt = lax.rem(z + j, 4)
        return rc(own.at[k, y, zt, x], rz.at[k, j - 1], zs.at[k, j - 1], zr.at[k, j - 1], p.dev(zt, xc, y))
    def a(k):
        load(k).start(); go(ccopy(k))
    def b(k):
        load(k).wait(); ccopy(k).wait_recv()
        @pl.loop(0, 16)
        def _(i):
            yy, zz, xx = i // 8, lax.rem(i // 2, 4), lax.rem(i, 2)
            own[k, yy, zz, xx] = (own[k, yy, zz, xx].astype(F) + rcb[k, yy, zz, xx].astype(F)).astype(jnp.bfloat16)
        go(x1(k)); go(y1(k))
    def c(k):
        x1(k).wait_recv(); y1(k).wait_recv()
        @pl.loop(0, 4)
        def _(i):
            u, v = i // 2, lax.rem(i, 2)
            own[k, u, v, x] = (own[k, u, v, x].astype(F) + rx[k, u, v].astype(F)).astype(jnp.bfloat16)
            own[k, y, 2 + u, v] = (own[k, y, 2 + u, v].astype(F) + ry[k, u, v].astype(F)).astype(jnp.bfloat16)
        go(y2(k)); go(x2(k))
    def d(k):
        x2(k).wait_recv(); y2(k).wait_recv()
        @pl.loop(0, 2)
        def _(i):
            own[k, y, i, x] = (own[k, y, i, x].astype(F) + ry2[k, i].astype(F)).astype(jnp.bfloat16)
            own[k, y, 2 + i, x] = (own[k, y, 2 + i, x].astype(F) + rx2[k, i].astype(F)).astype(jnp.bfloat16)
        for j in (1, 2, 3): go(zc(k, j))
    def e(k):
        for j in (1, 2, 3): zc(k, j).wait_recv()
        out[k] = own[k, y, z, x].astype(F) + rz[k, 0].astype(F) + rz[k, 1].astype(F) + rz[k, 2].astype(F)
    a(0); a(1); b(0)
    for k in range(nk + 2):
        if k + 2 < nk: a(k + 2)
        if k + 1 < nk: b(k + 1)
        if k < nk: c(k)
        if 0 <= k - 1 < nk: d(k - 1)
        if 0 <= k - 2 < nk: e(k - 2)
    for s in sends: s.wait_send()

def scatter(grads, fold=1, collective_id=2):
    nk, _, _, _, _, rows, cols = grads.shape
    D = pltpu.SemaphoreType.DMA
    V = lambda *s: pltpu.VMEM(s + (rows, cols), jnp.bfloat16)
    return pl.pallas_call(
        functools.partial(scatter_kernel, fold, nk),
        out_shape=jax.ShapeDtypeStruct((nk, rows, cols), jnp.float32),
        in_specs=[pl.BlockSpec(memory_space=pl.ANY)],
        out_specs=pl.BlockSpec(memory_space=pltpu.VMEM),
        scratch_shapes=[V(nk, 2, 4, 2), V(nk, 2, 4, 2), V(nk, 2, 2), V(nk, 2, 2), V(nk, 2), V(nk, 2), V(nk, 3),
            D((nk,)), D((nk,)), D((nk,)), D((nk, 2)), D((nk, 2)), D((nk, 2)), D((nk, 2)), D((nk, 3)), D((nk, 3))],
        compiler_params=pltpu.CompilerParams(collective_id=collective_id, has_side_effects=True, vmem_limit_bytes=60 * 2**20),
    )(grads)


epsilon = 1e-12
masked_score = -1000000000.0


def gelu_exact(values):
    return jax.nn.gelu(values, approximate=False)


def build_mask(lengths, bucket, full_length):
    position = jnp.arange(full_length, dtype=jnp.int32)
    half_len = full_length // 2
    first_len = lengths[:, 0][:, None]
    second_len = lengths[:, 1][:, None]
    packed = (bucket == 0)[:, None]
    upper_half = (position >= half_len)[None, :]
    start_key = jnp.where(packed & upper_half, half_len, 0)
    end_key = jnp.where(
        packed, jnp.where(upper_half, half_len + second_len, first_len), first_len + second_len
    )
    key_pos = position[None, None, :]
    return (key_pos >= start_key[:, :, None]) & (key_pos < end_key[:, :, None])


def normalize(values):
    center = values - jnp.mean(values, axis=-1, keepdims=True)
    variance = jnp.mean(center * center, axis=-1, keepdims=True)
    inverse = lax.rsqrt(variance + epsilon)
    return (center * inverse, inverse)


def norm_back(grad_in, normed, inverse, gain_vec):
    scaled = grad_in * gain_vec
    return inverse * (
        scaled
        - jnp.mean(scaled, axis=-1, keepdims=True)
        - normed * jnp.mean(scaled * normed, axis=-1, keepdims=True)
    )


def attention_scores(queries, keys_low, key_valid):
    scores = (
        jnp.einsum("bqhe,bkhe->bhqk", queries, keys_low, preferred_element_type=jnp.float32) * 0.125
    )
    return jnp.where(key_valid[:, None], scores, masked_score)


def forward_layer(state_in, weights, vectors, key_valid):
    w_qkv, w_out, w_up, w_down = weights
    qv_bias, out_bias, gain_vec, shift_vec, up_bias = vectors
    batch_size = state_in.shape[0]
    full_x = state_in.astype(jnp.bfloat16)
    full_length = full_x.shape[1]
    local_width = w_qkv.shape[2]
    head_count = local_width // HEAD_DIM
    head_shape = (batch_size, full_length, head_count, HEAD_DIM)
    projected = jnp.einsum("bsd,tdc->tbsc", full_x, w_qkv, preferred_element_type=jnp.float32)
    queries = (projected[0] + qv_bias[0]).astype(jnp.bfloat16).reshape(head_shape)
    keys_low = projected[1].astype(jnp.bfloat16).reshape(head_shape)
    values_low = (projected[2] + qv_bias[1]).astype(jnp.bfloat16).reshape(head_shape)
    scores = attention_scores(queries, keys_low, key_valid)
    row_max = jnp.max(scores, axis=-1, keepdims=True)
    log_total = row_max + jnp.log(jnp.sum(jnp.exp(scores - row_max), axis=-1, keepdims=True))
    probs_low = jnp.exp(scores - log_total).astype(jnp.bfloat16)
    context = jnp.einsum(
        "bhqk,bkhe->bqhe", probs_low, values_low, preferred_element_type=jnp.float32
    )
    context = context.astype(jnp.bfloat16).reshape(batch_size, full_length, local_width)
    attn_out = (
        jnp.einsum("bsc,cd->bsd", context, w_out, preferred_element_type=jnp.float32)
    )
    normed_one, inverse_one = normalize(state_in + attn_out + out_bias[0])
    hidden = normed_one * gain_vec[0] + shift_vec[0]
    full_hidden = hidden.astype(jnp.bfloat16)
    pre_active = (
        jnp.einsum("bsd,df->bsf", full_hidden, w_up, preferred_element_type=jnp.float32) + up_bias
    )
    active = gelu_exact(pre_active).astype(jnp.bfloat16)
    ffn_out = (
        jnp.einsum("bsf,fd->bsd", active, w_down, preferred_element_type=jnp.float32)
    )
    normed_two, inverse_two = normalize(hidden + ffn_out + out_bias[1])
    result = normed_two * gain_vec[1] + shift_vec[1]
    saved_one = (
        full_x,
        queries,
        keys_low,
        values_low,
        log_total,
        context,
        normed_one,
        inverse_one,
        full_hidden,
        pre_active,
        active,
        normed_two,
        inverse_two,
    )
    return (result, saved_one)


def backward_layer(grad_in, saved_one, weights, vectors, key_valid):
    w_qkv, w_out, w_up, w_down = weights
    qv_bias, out_bias, gain_vec, shift_vec, up_bias = vectors
    (
        full_x,
        queries,
        keys_low,
        values_low,
        log_total,
        context,
        normed_one,
        inverse_one,
        full_hidden,
        pre_active,
        active,
        normed_two,
        inverse_two,
    ) = saved_one
    batch_size, full_length, head_count, _ = queries.shape
    local_width = head_count * HEAD_DIM
    flat_shape = (batch_size, full_length, local_width)
    gain_two = jnp.sum(grad_in * normed_two, axis=(0, 1))
    shift_two = jnp.sum(grad_in, axis=(0, 1))
    grad_second = norm_back(grad_in, normed_two, inverse_two, gain_vec[1])
    out_two = jnp.sum(grad_second, axis=(0, 1))
    full_second = grad_second.astype(jnp.bfloat16)
    grad_down = jnp.einsum("bsf,bsd->fd", active, full_second, preferred_element_type=jnp.float32)
    grad_active = jnp.einsum("bsd,fd->bsf", full_second, w_down, preferred_element_type=jnp.float32)
    grad_pre = jax.vjp(gelu_exact, pre_active)[1](grad_active)[0]
    up_grad = jnp.sum(grad_pre, axis=(0, 1))
    pre_low = grad_pre.astype(jnp.bfloat16)
    grad_up = jnp.einsum("bsd,bsf->df", full_hidden, pre_low, preferred_element_type=jnp.float32)
    grad_hidden = (
        (jnp.einsum("bsf,df->bsd", pre_low, w_up, preferred_element_type=jnp.float32))
        + grad_second
    )
    gain_one = jnp.sum(grad_hidden * normed_one, axis=(0, 1))
    shift_one = jnp.sum(grad_hidden, axis=(0, 1))
    grad_first = norm_back(grad_hidden, normed_one, inverse_one, gain_vec[0])
    out_one = jnp.sum(grad_first, axis=(0, 1))
    full_first = grad_first.astype(jnp.bfloat16)
    grad_out = jnp.einsum("bsc,bsd->cd", context, full_first, preferred_element_type=jnp.float32)
    grad_context = jnp.einsum("bsd,cd->bsc", full_first, w_out, preferred_element_type=jnp.float32)
    grad_context = grad_context.astype(jnp.bfloat16).reshape(queries.shape)
    scores = attention_scores(queries, keys_low, key_valid)
    attn_probs = jnp.exp(scores - log_total)
    probs_low = attn_probs.astype(jnp.bfloat16)
    grad_probs = jnp.einsum(
        "bqhe,bkhe->bhqk", grad_context, values_low, preferred_element_type=jnp.float32
    )
    grad_value = jnp.einsum(
        "bhqk,bqhe->bkhe", probs_low, grad_context, preferred_element_type=jnp.float32
    )
    grad_scores = attn_probs * (
        grad_probs - jnp.sum(attn_probs * grad_probs, axis=-1, keepdims=True)
    )
    scores_low = jnp.where(key_valid[:, None], grad_scores, 0.0).astype(jnp.bfloat16)
    grad_query = (
        jnp.einsum("bhqk,bkhe->bqhe", scores_low, keys_low, preferred_element_type=jnp.float32)
        * 0.125
    )
    grad_key = (
        jnp.einsum("bhqk,bqhe->bkhe", scores_low, queries, preferred_element_type=jnp.float32)
        * 0.125
    )
    grad_query = grad_query.reshape(flat_shape)
    grad_key = grad_key.reshape(flat_shape)
    grad_value = grad_value.reshape(flat_shape)
    qv_grad = jnp.stack([jnp.sum(grad_query, axis=(0, 1)), jnp.sum(grad_value, axis=(0, 1))])
    grad_proj = jnp.stack([grad_query, grad_key, grad_value], axis=0).astype(jnp.bfloat16)
    grad_qkv = jnp.einsum("bsd,tbsc->tdc", full_x, grad_proj, preferred_element_type=jnp.float32)
    grad_prev = (
        (jnp.einsum("tbsc,tdc->bsd", grad_proj, w_qkv, preferred_element_type=jnp.float32))
        + grad_first
    )
    matrices = (grad_qkv, grad_out, grad_up, grad_down)
    vector_set = (
        qv_grad,
        jnp.stack([out_one, out_two]),
        jnp.stack([gain_one, gain_two]),
        jnp.stack([shift_one, shift_two]),
        up_grad,
    )
    return (grad_prev, matrices, vector_set)


def full_weights(chunks, layer):
    a, b, c = (chunks[3 * layer + i].reshape(2, 768, 1536) for i in range(3))
    w_qkv = a[:, :, :1152].reshape(2, 768, 3, 384).transpose(2, 1, 0, 3).reshape(3, 768, 768)
    w_out = a[:, :, 1152:].transpose(0, 2, 1).reshape(768, 768)
    w_up = b.transpose(1, 0, 2).reshape(768, 3072)
    w_down = c.transpose(0, 2, 1).reshape(3072, 768)
    return w_qkv, w_out, w_up, w_down


def chunk_grads(matrices):
    g_qkv, g_out, g_up, g_down = (m.astype(jnp.bfloat16) for m in matrices)
    a = jnp.concatenate([
        g_qkv.reshape(3, 768, 2, 384).transpose(2, 1, 0, 3).reshape(2, 768, 1152),
        g_out.reshape(2, 384, 768).transpose(0, 2, 1)], axis=2)
    b = g_up.reshape(768, 2, 1536).transpose(1, 0, 2)
    c = g_down.reshape(2, 1536, 768).transpose(0, 2, 1)
    return [a, b, c]


def swap_rows(values):
    m = lax.axis_index("mp")
    keep = lax.dynamic_index_in_dim(values, m, 0, keepdims=False)
    send = lax.dynamic_index_in_dim(values, 1 - m, 0, keepdims=False)
    got = lax.ppermute(send, "mp", [(0, 1), (1, 0)])
    first = jnp.where(m == 0, keep, got)
    return jnp.concatenate([first, jnp.where(m == 0, got, keep)], 0)[None]


def swap_slots(values):
    m = lax.axis_index("mp")
    halves = values.reshape(2, values.shape[1] // 2, values.shape[2])
    keep = lax.dynamic_index_in_dim(halves, m, 0, keepdims=False)
    send = lax.dynamic_index_in_dim(halves, 1 - m, 0, keepdims=False)
    got = lax.ppermute(send, "mp", [(0, 1), (1, 0)])
    first = jnp.where(m == 0, keep, got)
    return jnp.stack([first, jnp.where(m == 0, got, keep)], 0)


def per_device(layer_input, cotangent, lengths, bucket, w_qkv, bias_qv, w_out, bias_out,
               ln_gain, ln_bias, w_up, bias_up, w_down):
    layers = w_qkv.shape[0]
    dp = lax.axis_size("dp")
    fold = dp // GROUPS
    part = lax.axis_index("mp")
    width = layer_input.shape[2]
    members = [[g * fold + i for i in range(fold)] for g in range(GROUPS)]
    packed = []
    for l in range(layers):
        packed.append(jnp.concatenate([w_qkv[l, 0], w_qkv[l, 1], w_qkv[l, 2], w_out[l].T], 1))
        packed.append(w_up[l])
        packed.append(w_down[l].T)
    packed = jnp.stack(packed)
    if fold > 1:
        packed = lax.all_gather(packed, "dp", axis=1, tiled=True, axis_index_groups=members)
    chunks = gather(packed, fold)
    weights = [full_weights(chunks, l) for l in range(layers)]
    full_qv = lax.all_gather(bias_qv, "mp", axis=2, tiled=True).astype(jnp.float32)
    full_up = lax.all_gather(bias_up, "mp", axis=1, tiled=True).astype(jnp.float32)
    vectors = [(full_qv[l], bias_out[l].astype(jnp.float32), ln_gain[l].astype(jnp.float32),
                ln_bias[l].astype(jnp.float32), full_up[l]) for l in range(layers)]
    current = swap_rows(layer_input).astype(jnp.float32)
    full_length = current.shape[1]
    mine = lambda v: lax.dynamic_slice_in_dim(v, part, 1, 0)
    key_valid = build_mask(mine(lengths), mine(bucket), full_length)
    kept = []
    for l in range(layers):
        current, saved = forward_layer(current, weights[l], vectors[l], key_valid)
        kept.append(saved)
    output = swap_slots(current.astype(jnp.bfloat16))
    grad_now = swap_rows(cotangent).astype(jnp.float32)
    sums = [None] * layers
    vecs = [None] * layers
    for l in reversed(range(layers)):
        grad_now, matrices, vecs[l] = backward_layer(grad_now, kept[l], weights[l], vectors[l], key_valid)
        sums[l] = chunk_grads(matrices)
    input_grad = swap_slots(grad_now.astype(jnp.bfloat16))
    grads = jnp.stack([g for l in range(layers) for g in sums[l]])
    grads = grads.reshape(3 * layers, 2, 4, 2, 2, 48, 1536)
    shards = scatter(grads, fold)
    if fold > 1:
        shards = lax.psum_scatter(shards, "dp", scatter_dimension=1, tiled=True, axis_index_groups=members)
    rows = shards.shape[1]
    shards = shards.reshape(layers, 3, rows, 1536)
    a, b, c = shards[:, 0], shards[:, 1], shards[:, 2]
    grad_qkv = a[:, :, :1152].reshape(layers, rows, 3, 384).transpose(0, 2, 1, 3)
    grad_out = a[:, :, 1152:].transpose(0, 2, 1)
    grad_down = c.transpose(0, 2, 1)
    stacked = [jnp.stack([vecs[l][i] for l in range(layers)]) for i in range(5)]
    qv, bias, gain, shift, up = lax.psum(tuple(stacked), ("dp", "mp"))
    half = width // 2
    qv = lax.dynamic_slice_in_dim(qv, part * half, half, 2)
    up = lax.dynamic_slice_in_dim(up, part * w_up.shape[2], w_up.shape[2], 1)
    return output, input_grad, grad_qkv, qv, grad_out, bias, gain, shift, b, up, grad_down


def solution(mesh):
    in_specs = (
        P("dp", "mp", None),
        P("dp", "mp", None),
        P("dp", None),
        P("dp"),
        P(None, None, "dp", "mp"),
        P(None, None, "mp"),
        P(None, "mp", "dp"),
        P(),
        P(),
        P(),
        P(None, "dp", "mp"),
        P(None, "mp"),
        P(None, "mp", "dp"),
    )
    out_specs = (
        P("dp", "mp", None),
        P("dp", "mp", None),
        P(None, None, "dp", "mp"),
        P(None, None, "mp"),
        P(None, "mp", "dp"),
        P(),
        P(),
        P(),
        P(None, "dp", "mp"),
        P(None, "mp"),
        P(None, "mp", "dp"),
    )
    return jax.shard_map(
        per_device, mesh=mesh, in_specs=in_specs, out_specs=out_specs, check_vma=False
    )
```

time: 1500 us -> 949 us (0.63)
  waiting for transfers between devices: 751 us -> 120 us
  Pallas kernels: 0 us -> 277 us
  blocking collectives: 253 us -> 16.9 us
  local copies, waits for them, and re-layouts: 88.6 us -> 210 us
  matrix products: 307 us -> 255 us
  other arithmetic: 61.2 us -> 36 us
    unnamed x26 -> x1, waiting for transfers between devices: 335 us -> 0.02 us
    pallas_call x0 -> x2, Pallas kernels: none -> 277 us  [the longest x1 150 us: scatter(): pl.pallas_call(functools.partial(scatter_kernel, fold, nk), out_shape=jax...]
    reduce_scatter x17 -> x0, waiting for transfers between devices: 238 us -> none  [the longest x1 111 us: per_device(): lax.psum_scatter(up_stack, 'dp', scatter_dimension=1, tiled=True)]
    all_gather x18 -> x2, blocking collectives: 253 us -> 16.9 us  [the longest x1 12.3 us: per_device(): lax.all_gather(bias_qv, 'mp', axis=2, tiled=True).astype(jnp.float32)]
    all_gather x6 -> x0, waiting for transfers between devices: 145 us -> none  [the longest x2 64.9 us: per_device(): lax.all_gather(w_down[layer_index], 'dp', axis=1, tiled=True)]
    psum x1, waiting for transfers between devices: 31.9 us -> 120 us  [per_device(): qv, bias, gain, shift, up = lax.psum(tuple(stacked), ('dp', 'mp'))]
    reshape x0 -> x9, local copies, waits for them, and re-layouts: none -> 42.8 us  [the longest x2 16.4 us: chunk_grads(): g_qkv.reshape(3, 768, 2, 384).transpose(2, 1, 0, 3).reshape(2, 768, 1152)]
    slice x6 -> x7, local copies, waits for them, and re-layouts: 5.63 us -> 29.5 us  [the longest x1 20.9 us: full_weights(): a, b, c = (chunks[3 * layer + i].reshape(2, 768, 1536) for i in range(3))]
  transfers between devices with their start and end apart: 25 -> 5, of which waited for: 18 -> 1; matrix products, arithmetic and copies ran while one was open for 18% -> 25% of each run, Pallas kernels for 0% -> 30%
where the time goes in v1:
time: 949 us; the launch traced here: 939 us
  Pallas kernels  277 us (29%)
  matrix products  255 us (27%)
  local copies, waits for them, and re-layouts  210 us (22%)
  waiting for transfers between devices  120 us (13%)
  other arithmetic  36 us (4%)
  between operations  18.6 us (2%)
  blocking collectives  16.9 us (2%)
    pallas_call x1, Pallas kernels, scatter(): pl.pallas_call(functools.partial(scatter_kernel, fold, nk), out_shape=jax...  150 us
    pallas_call x1, Pallas kernels, gather(): pl.pallas_call(functools.partial(gather_kernel, fold, nk), out_shape=jax....  127 us
    psum x1, waiting for transfers between devices, per_device(): qv, bias, gain, shift, up = lax.psum(tuple(stacked), ('dp', 'mp'))  120 us
    dot_general x2, matrix products, backward_layer(): jnp.einsum('bhqk,bkhe->bqhe', scores_low, keys_low, preferred_element_typ...  41.7 us
    dot_general x2, matrix products, backward_layer(): jnp.einsum('bhqk,bqhe->bkhe', scores_low, queries, preferred_element_type...  41.1 us
    dot_general x2, matrix products, forward_layer(): jnp.einsum('bsd,df->bsf', full_hidden, w_up, preferred_element_type=jnp.f...  39.4 us
    unnamed x280, local copies, waits for them, and re-layouts  39.2 us
    another operation x4, local copies, waits for them, and re-layouts, full_weights(): a, b, c = (chunks[3 * layer + i].reshape(2, 768, 1536) for i in range(3))  27.2 us
  transfers between devices with their start and end apart: 5, of which 1 were waited for; matrix products, arithmetic and copies ran while one was open for 25% of the time, Pallas kernels for 30%

profile of v1, /device:TPU:0, one launch (start us, length us, event | category | flops | bytes accessed | tf_op | source)
XLA Modules:
  0.0 938.5 jit_solution(6447197207400674636)
XLA Ops:
  17.5 12.3 %all_gather.6 = bf16[2,2,768]{2,1,0:T(2,128)(2,1)S(1)} all-gather(bf16[2,2,384]{2,1,0:T(2,128)(2,1)} %param.18), channel_id=1, replica_groups=mesh['dp'=16,'mp'=2] {'mp'}, dimensions={2}, use_global_device_ids=true | all-gather | bytes 9216 | tf_op jit(solution)/shard_map/all_gather | solution.py:423
  45.4 127.3 %shard_map.212 = bf16[6,2,4,4,48,1536]{5,4,3,2,1,0:T(8,128)(2,1)} custom-call(bf16[6,48,1536]{2,1,0:T(8,128)(2,1)} %copy-done.34), custom_call_target="tpu_custom_call" | custom-call | tf_op jit(solution)/shard_map/pallas_call | solution.py:95
  172.6 20.9 %fusion.184 = (bf16[1,2,4,4,48,1536]{5,4,3,2,1,0:T(8,128)(2,1)}, bf16[1,2,4,4,48,1536]{5,4,3,2,1,0:T(8,128)(2,1)}, bf16[1,2,4,4,48,1536]{5,4,3,2,1,0:T(8,128)(2,...) fusion(bf16[6,2,4,4,48,1536]{5,4,3,2,1,0:T(8,128)(2,1)} %shard_, ...), kind=kLoop, calls=%fused_computation.324 | loop fusion | bytes 56623104 | tf_op jit(solution)/shard_map/slice | solution.py:368
  208.1 6.6 copy.71
  214.7 6.7 copy.70
  221.4 5.8 copy.116
  242.1 7.1 copy.65
  249.2 6.9 copy.64
  274.7 20.0 %multiply_convert_fusion.1 = (bf16[512,3072]{1,0:T(8,128)(2,1)S(1)}, f32[512,3072]{1,0:T(8,128)}, f32[512,3072]{1,0:T(8,128)}) fusion(f32[3072]{0:T(1024)S(1)} %bitcast.399, bf16[768,3072]{0,1:T(8,128)(2,1)S(1)} %bitcast.342, f32[512,768]{1,0:T(8,128)S(1)} %get-tuple-element.72, f32[768]{0:T(1024)S(1)} %get-tuple-element.51, ...), kind=kOutput, calls=%fused_computation.47 | convolution fusion | flops 2521694208 | bytes 22042624 | tf_op jit(solution)/shard_map/bsd,df->bsf/dot_general | solution.py:255
  316.3 19.4 %multiply_convert_fusion = (bf16[512,3072]{1,0:T(8,128)(2,1)S(1)}, f32[512,3072]{1,0:T(8,128)}, f32[512,3072]{1,0:T(8,128)}) fusion(f32[3072]{0:T(1024)S(1)} %bitcast.402, bf16[768,3072]{0,1:T(8,128)(2,1)S(1)} %bitcast.354, f32[512,768]{1,0:T(8,128)S(1)} %get-tuple-element.121, f32[768]{0:T(1024)S(1)} %copy-done.102, f32[768]{0:T(1024)S(1)} %get-tuple-element.146, ...), kind=kOutput, calls=%fused_computation.32 | convolution fusion | flops 2521694208 | bytes 22042624 | tf_op jit(solution)/shard_map/bsd,df->bsf/dot_general | solution.py:255
  341.2 9.7 %fusion.196 = (f32[3072]{0:T(1024)}, bf16[512,3072]{1,0:T(8,128)(2,1)}) fusion(f32[512,3072]{1,0:T(8,128)} %get-tuple-element.68, bf16[3072,768]{1,0:T(8,128)(2,1)S(1)} %bitcast.361, f32[512,768]{1,0:T(8,128)S(1)} %get-tuple-element.66, f32[512,3072]{1,0:T(8,128)} %get-tuple-element.122, f32[3072]{0:T(1024)S(1)} %bitcast.403), kind=kOutput, calls=%fused_computation.332 | convolution fusion | flops 2441475072 | bytes 22044672 | tf_op jit(solution)/shard_map/bsd,fd->bsf/dot_general | solution.py:308
  373.1 9.4 %bitcast_convert_fusion = (bf16[1,512,12,64]{1,3,2,0:T(8,128)(2,1)}, f32[12,64,512]{2,1,0:T(8,128)}) fusion(bf16[512,12,64]{0,2,1:T(8,128)(2,1)} %bitcast.376, f32[12,512,512]{1,2,0:T(8,128)} %copy-done.3, f32[12,512]{1,0:T(8,128)S(1)} %log_add_fusion, pred[512,512]{0,1:T(8,128)(4,1)S(1)} %fusion.99), kind=kOutput, calls=%fused_computation.104 | convolution fusion | flops 415629312 | bytes 16015360 | tf_op jit(solution)/shard_map/bhqk,bqhe->bkhe/dot_general | solution.py:331
  382.5 6.8 fusion.123
  389.3 20.4 %multiply_convert_fusion.3 = bf16[12,64,512]{2,1,0:T(8,128)(2,1)} fusion(f32[12,512,512]{1,2,0:T(8,128)} %fusion.123, f32[12,512,512]{1,2,0:T(8,128)} %copy-done.3, f32[12,512]{1,0:T(8,128)S(1)} %log_add_fusion, pred[512,512]{0,1:T(8,128)(4,1)S(1)} %fusion.99, f32[512,12,64]{0,2,1:T(8,128)S(1)} %bitcast.331, f32[12,64]{1,0:T(8,128)S(1)} %copy-done.60), kind=kOutput, calls=%fused_computation.125 | convolution fusion | flops 438835712 | bytes 27814912 | tf_op jit(solution)/shard_map/bhqk,bqhe->bkhe/dot_general | solution.py:343
  409.7 20.8 %bitcast_convert_fusion.1 = (bf16[1,512,12,64]{1,3,2,0:T(8,128)(2,1)}, f32[12,64,512]{2,1,0:T(8,128)}) fusion(bf16[512,12,64]{0,2,1:T(8,128)(2,1)S(1)} %bitcast.375, f32[12,512,512]{1,2,0:T(8,128)} %fusion.123, f32[12,512,512]{1,2,0:T(8,128)} %copy-done.3, f32[12,512]{1,0:T(8,128)S(1)} %log_add_fusion, pred[512,512]{0,1:T(8,128)(4,1)S(1)} %fusion.99), kind=kOutput, calls=%fused_computation.106 | convolution fusion | flops 438049280 | bytes 28598272 | tf_op jit(solution)/shard_map/bhqk,bkhe->bqhe/dot_general | solution.py:339
  437.6 5.6 multiply_reduce_fusion.3
  453.7 9.7 %fusion.197 = (f32[3072]{0:T(1024)}, bf16[512,3072]{1,0:T(8,128)(2,1)}) fusion(f32[512,3072]{1,0:T(8,128)} %get-tuple-element.70, bf16[3072,768]{1,0:T(8,128)(2,1)S(1)} %bitcast.351, f32[512,768]{1,0:T(8,128)S(1)} %get-tuple-element.62, f32[512,3072]{1,0:T(8,128)} %get-tuple-element.115, f32[3072]{0:T(1024)S(1)} %bitcast.400), kind=kOutput, calls=%fused_computation.333 | convolution fusion | flops 2441475072 | bytes 22044672 | tf_op jit(solution)/shard_map/bsd,fd->bsf/dot_general | solution.py:308
  463.5 5.2 multiply_reduce_fusion.4
  478.7 7.8 bitcast_convert_fusion.2
  486.5 8.0 fusion.121
  494.5 20.7 %multiply_convert_fusion.2 = bf16[12,64,512]{2,1,0:T(8,128)(2,1)} fusion(f32[12,512,512]{1,2,0:T(8,128)} %fusion.121, f32[12,512,512]{1,2,0:T(8,128)} %copy-done.2, f32[12,512]{1,0:T(8,128)S(1)} %copy-done.65, pred[512,512]{0,1:T(8,128)(4,1)S(1)} %fusion.99, f32[512,12,64]{0,2,1:T(8,128)S(1)} %bitcast.327, f32[12,64]{1,0:T(8,128)S(1)} %copy-done.59), kind=kOutput, calls=%fused_computation.117 | convolution fusion | flops 438835712 | bytes 27814912 | tf_op jit(solution)/shard_map/bhqk,bqhe->bkhe/dot_general | solution.py:343
  515.1 21.0 %bitcast_convert_fusion.3 = (bf16[1,512,12,64]{1,3,2,0:T(8,128)(2,1)}, f32[12,64,512]{2,1,0:T(8,128)}) fusion(bf16[512,12,64]{0,2,1:T(8,128)(2,1)} %bitcast.373, f32[12,512,512]{1,2,0:T(8,128)} %fusion.121, f32[12,512,512]{1,2,0:T(8,128)} %copy-done.2, f32[12,512]{1,0:T(8,128)S(1)} %copy-done.65, pred[512,512]{0,1:T(8,128)(4,1)S(1)} %fusion.99), kind=kOutput, calls=%fused_computation.110 | convolution fusion | flops 438049280 | bytes 28598272 | tf_op jit(solution)/shard_map/bhqk,bkhe->bqhe/dot_general | solution.py:339
  539.9 5.5 fusion.79
  560.4 6.8 copy.97
  569.2 6.7 copy.92
  585.4 8.2 copy.94
  593.6 7.9 concatenate.66
  606.1 8.2 copy.89
  614.3 9.6 %concatenate.63 = bf16[1,2,4,2,2,48,1152]{6,5,4,3,2,1,0:T(8,128)(2,1)} reshape(bf16[2,768,3,384]{3,2,1,0:T(4,128)(2,1)} %bitcast.322) | data formatting | bytes 7077888 | tf_op jit(solution)/shard_map/concatenate | solution.py:378
  623.9 5.2 maximum_dynamic-update-slice_fusion.1
  645.6 150.1 %shard_map.213 = f32[6,48,1536]{2,1,0:T(8,128)} custom-call(bf16[6,2,4,2,2,48,1536]{6,5,4,3,2,1,0:T(8,128)(2,1)} %constant_dynamic-update-slice_fusion.grads), custom_call_target="tpu_custom_call" | custom-call | tf_op jit(solution)/shard_map/pallas_call | solution.py:170
  804.1 119.8 %all-reduce.3.cloned.1.call-done = (f32[2,2,768]{2,1,0:T(2,128)}, f32[2,2,768]{2,1,0:T(2,128)}, f32[2,2,768]{2,1,0:T(2,128)}, f32[2,2,768]{2,1,0:T(2,128)}, f32[2,3072]{1,0:T(2,128)}) async-done(((f32[2,2,768]{2,1,0:T(2,128)}, f32[2,2,768]{2,1,0:T(2,128)}, f32[2,2,768]{2,1,0:T(2,128)}, f32[2,2,768]{2,1,0:T(2,128)}, f32[2,3072]{1,0:T(2,128)}), (f32[2,2,768]{2,1,0:T(2,128)}, f32[2,2,768]{2,1,0:T(2,128)}, ...) | async-done | bytes 73744 | tf_op jit(solution)/shard_map/psum | solution.py:455
  (447 shorter events, 213.9 us)
Async XLA Ops:
  7.2 916.8 %all-reduce.3.cloned.1.call-start = ((), (), s32[]{:S(2)}) async-start(), calls=%async_computation | async-start | bytes 147456 | tf_op jit(solution)/shard_map/psum | solution.py:455
  9.0 291.7 %collective-permute-start.2 = (bf16[256,768]{1,0:T(8,128)(2,1)}, bf16[256,768]{1,0:T(8,128)(2,1)}, u32[]{:S(2)}, u32[]{:S(2)}) collective-permute-start(bf16[256,768]{1,0:T(8,128)(2,1)} %dynamic-slice_bitcast_fusion.1), channel_id=1, source_target_pairs={{0,1},{1,0},{2,3},{3,2},{4,5},{5,4},{6,7},{7,6},{8,9},{9,8},{10,11... | collective-permute-start | bytes 1179656 | tf_op jit(solution)/shard_map/ppermute | solution.py:390
  13.7 242.7 %collective-permute-start = (bf16[256,768]{1,0:T(8,128)(2,1)}, bf16[256,768]{1,0:T(8,128)(2,1)}, u32[]{:S(2)}, u32[]{:S(2)}) collective-permute-start(bf16[256,768]{1,0:T(8,128)(2,1)} %dynamic-slice_bitcast_fusion.3), channel_id=1, source_target_pairs={{0,1},{1,0},{2,3},{3,2},{4,5},{5,4},{6,7},{7,6},{8,9},{9,8},{10,11... | collective-permute-start | bytes 1179656 | tf_op jit(solution)/shard_map/ppermute | solution.py:390
  206.7 55.7 %copy-start.58 = (f32[12,64]{1,0:T(8,128)}, f32[12,64]{1,0:T(8,128)S(1)}, u32[]{:S(2)}) copy-start(f32[12,64]{1,0:T(8,128)S(1)} %add.295) | copy-start | bytes 9220
  242.1 31.2 %copy-start.35 = (bf16[2,768,384]{1,2,0:T(8,128)(2,1)}, bf16[2,768,384]{1,2,0:T(8,128)(2,1)S(1)}, u32[]{:S(2)}) copy-start(bf16[2,768,384]{1,2,0:T(8,128)(2,1)S(1)} %copy.115) | copy-start | bytes 3538948
  256.1 38.6 %copy-start.70 = (f32[768]{0:T(1024)}, f32[768]{0:T(1024)S(1)}, u32[]{:S(2)}) copy-start(f32[768]{0:T(1024)S(1)} %get-tuple-element.144) | copy-start | bytes 9220
  256.1 38.6 %copy-start.100 = (f32[768]{0:T(1024)}, f32[768]{0:T(1024)S(1)}, u32[]{:S(2)}) copy-start(f32[768]{0:T(1024)S(1)} %get-tuple-element.51) | copy-start | bytes 9220
  273.4 21.4 %slice-start.10 = ((s8[4718592]{0:T(1024)(128)(4,1)}), s8[4194304]{0:T(1024)(128)(4,1)S(1)}, s32[]{:S(2)}) async-start(s8[4718592]{0:T(1024)(128)(4,1)} %bitcast.346), calls=%async_computation.11 | async-start | bytes 8388608
  314.8 21.0 %copy-start.41 = (bf16[12,64,512]{2,1,0:T(8,128)(2,1)}, bf16[12,64,512]{2,1,0:T(8,128)(2,1)S(1)}, u32[]{:S(2)}) copy-start(bf16[12,64,512]{2,1,0:T(8,128)(2,1)S(1)} %convolution_convert_fusion.10) | copy-start | bytes 2359300
  515.1 21.0 %copy-start.43 = (bf16[1,512,12,64]{1,3,2,0:T(8,128)(2,1)S(1)}, bf16[1,512,12,64]{1,3,2,0:T(8,128)(2,1)}, u32[]{:S(2)}) copy-start(bf16[1,512,12,64]{1,3,2,0:T(8,128)(2,1)} %get-tuple-element.132) | copy-start | bytes 2359300
  515.1 23.5 %copy-start.45 = (bf16[12,64,512]{2,1,0:T(8,128)(2,1)S(1)}, bf16[12,64,512]{2,1,0:T(8,128)(2,1)}, u32[]{:S(2)}) copy-start(bf16[12,64,512]{2,1,0:T(8,128)(2,1)} %multiply_convert_fusion.2) | copy-start | bytes 2359300
  558.9 367.7 %collective-permute-start.1 = (bf16[256,768]{1,0:T(8,128)(2,1)}, bf16[256,768]{1,0:T(8,128)(2,1)}, u32[]{:S(2)}, u32[]{:S(2)}) collective-permute-start(bf16[256,768]{1,0:T(8,128)(2,1)} %dynamic-slice_bitcast_fusion.2), channel_id=1, source_target_pairs={{0,1},{1,0},{2,3},{3,2},{4,5},{5,4},{6,7},{7,6},{8,9},{9,8},{10,11... | collective-permute-start | bytes 1179656 | tf_op jit(solution)/shard_map/ppermute | solution.py:400
  645.4 153.6 %copy-start.77 = (f32[1,768]{1,0:T(1,128)S(1)}, f32[1,768]{1,0:T(1,128)}, u32[]{:S(2)}) copy-start(f32[1,768]{1,0:T(1,128)} %stack.231) | copy-start | bytes 9220
  645.4 153.6 %copy-start.78 = (f32[1,768]{1,0:T(1,128)S(1)}, f32[1,768]{1,0:T(1,128)}, u32[]{:S(2)}) copy-start(f32[1,768]{1,0:T(1,128)} %stack.223) | copy-start | bytes 9220
  645.4 153.6 %copy-start.79 = (f32[1,768]{1,0:T(1,128)S(1)}, f32[1,768]{1,0:T(1,128)}, u32[]{:S(2)}) copy-start(f32[1,768]{1,0:T(1,128)} %stack.222) | copy-start | bytes 9220
  645.4 153.6 %copy-start.80 = (f32[1,768]{1,0:T(1,128)S(1)}, f32[1,768]{1,0:T(1,128)}, u32[]{:S(2)}) copy-start(f32[1,768]{1,0:T(1,128)} %stack.240) | copy-start | bytes 9220
  645.4 153.6 %copy-start.89 = (f32[3072]{0:T(1024)S(1)}, f32[3072]{0:T(1024)}, u32[]{:S(2)}) copy-start(f32[3072]{0:T(1024)} %get-tuple-element.136) | copy-start | bytes 36868
  645.5 153.6 %copy-start.91 = (f32[3072]{0:T(1024)S(1)}, f32[3072]{0:T(1024)}, u32[]{:S(2)}) copy-start(f32[3072]{0:T(1024)} %get-tuple-element.138) | copy-start | bytes 36868
  645.5 154.3 %copy-start.82 = (f32[1,768]{1,0:T(1,128)S(1)}, f32[1,768]{1,0:T(1,128)}, u32[]{:S(2)}) copy-start(f32[1,768]{1,0:T(1,128)} %stack.228) | copy-start | bytes 9220
  645.5 154.3 %copy-start.86 = (f32[1,768]{1,0:T(1,128)S(1)}, f32[1,768]{1,0:T(1,128)}, u32[]{:S(2)}) copy-start(f32[1,768]{1,0:T(1,128)} %stack.227) | copy-start | bytes 9220
  645.5 154.9 %copy-start.81 = (f32[1,768]{1,0:T(1,128)S(1)}, f32[1,768]{1,0:T(1,128)}, u32[]{:S(2)}) copy-start(f32[1,768]{1,0:T(1,128)} %stack.219) | copy-start | bytes 9220
  645.5 154.9 %copy-start.83 = (f32[1,768]{1,0:T(1,128)S(1)}, f32[1,768]{1,0:T(1,128)}, u32[]{:S(2)}) copy-start(f32[1,768]{1,0:T(1,128)} %stack.218) | copy-start | bytes 9220
  645.5 155.5 %copy-start.84 = (f32[1,768]{1,0:T(1,128)S(1)}, f32[1,768]{1,0:T(1,128)}, u32[]{:S(2)}) copy-start(f32[1,768]{1,0:T(1,128)} %stack.236) | copy-start | bytes 9220
  645.5 155.5 %copy-start.85 = (f32[1,768]{1,0:T(1,128)S(1)}, f32[1,768]{1,0:T(1,128)}, u32[]{:S(2)}) copy-start(f32[1,768]{1,0:T(1,128)} %stack.237) | copy-start | bytes 9220
  645.5 156.1 %copy-start.92 = (f32[1,768]{1,0:T(1,128)S(1)}, f32[1,768]{1,0:T(1,128)}, u32[]{:S(2)}) copy-start(f32[1,768]{1,0:T(1,128)} %stack.214) | copy-start | bytes 9220
  645.5 156.1 %copy-start.93 = (f32[1,768]{1,0:T(1,128)S(1)}, f32[1,768]{1,0:T(1,128)}, u32[]{:S(2)}) copy-start(f32[1,768]{1,0:T(1,128)} %stack.213) | copy-start | bytes 9220
  645.5 156.1 %copy-start.94 = (f32[1,768]{1,0:T(1,128)S(1)}, f32[1,768]{1,0:T(1,128)}, u32[]{:S(2)}) copy-start(f32[1,768]{1,0:T(1,128)} %stack.210) | copy-start | bytes 9220
  645.6 156.1 %copy-start.95 = (f32[1,768]{1,0:T(1,128)S(1)}, f32[1,768]{1,0:T(1,128)}, u32[]{:S(2)}) copy-start(f32[1,768]{1,0:T(1,128)} %stack.209) | copy-start | bytes 9220
  645.6 156.7 %copy-start.52 = (bf16[512,768]{1,0:T(8,128)(2,1)S(1)}, bf16[512,768]{1,0:T(8,128)(2,1)}, u32[]{:S(2)}) copy-start(bf16[512,768]{1,0:T(8,128)(2,1)} %fusion.79) | copy-start | bytes 2359300
  795.6 131.0 %copy-start.31 = (bf16[512,768]{1,0:T(8,128)(2,1)S(1)}, bf16[512,768]{1,0:T(8,128)(2,1)}, u32[]{:S(2)}) copy-start(bf16[512,768]{1,0:T(8,128)(2,1)} %get-tuple-element.86) | copy-start | bytes 2359300
  802.3 129.2 %copy-start.1 = (s32[2,2]{1,0:T(2,128)S(1)}, s32[2,2]{1,0:T(2,128)}, u32[]{:S(2)}) copy-start(s32[2,2]{1,0:T(2,128)} %param.15) | copy-start | bytes 52
  802.4 126.2 %collective-permute-start.3 = (bf16[256,768]{1,0:T(8,128)(2,1)S(1)}, bf16[256,768]{1,0:T(8,128)(2,1)S(1)}, u32[]{:S(2)}, u32[]{:S(2)}) collective-permute-start(bf16[256,768]{1,0:T(8,128)(2,1)S(1)} %dynamic-slice_bitcast_fusion), channel_id=1, source_target_pairs={{0,1},{1,0},{2,3},{3,2},{4,5},{5,4},{6,7},{7,6},{8,9},{9,8},{10,11... | collective-permute-start | bytes 1179656 | tf_op jit(solution)/shard_map/ppermute | solution.py:400
  (106 other events, 704.5 us)
Sparse Core Ops, SparseCore 0:
  802.4 121.4 all-reduce.2

commit v2 on v0

v2 whole, which is shorter than its diff:
```python
import functools

import jax
import jax.numpy as jnp
from jax import lax
from jax.experimental import pallas as pl
from jax.experimental.pallas import tpu as pltpu
from jax.sharding import PartitionSpec as P

F32 = jnp.float32
BF16 = jnp.bfloat16
S = 512
D = 768
HALF = 384
UNITS = 1536
GROUPS = 16
EPS = 1e-12
MESH = pl.DeviceIdType.MESH
NN = (((1,), (0,)), ((), ()))
NT = (((1,), (1,)), ((), ()))
TN = (((0,), (0,)), ((), ()))
ANY = pl.BlockSpec(memory_space=pl.ANY)
VMEM = pl.BlockSpec(memory_space=pltpu.VMEM)
SMEM = pl.BlockSpec(memory_space=pltpu.SMEM)


def dot(a, b, dims=NN):
    return lax.dot_general(a, b, dims, preferred_element_type=F32)


def at(start, size):
    return pl.ds(pl.multiple_of(start, size), size)


def remote(src, dst, send_sem, recv_sem, device):
    return pltpu.make_async_remote_copy(
        src_ref=src, dst_ref=dst, send_sem=send_sem, recv_sem=recv_sem,
        device_id=device, device_id_type=MESH)


class Place:
    def __init__(self, fold):
        d = lax.axis_index("dp")
        self.fold = fold
        self.member = lax.rem(d, fold) if fold > 1 else 0
        g = d // fold if fold > 1 else d
        self.z = g // 4
        self.xc = lax.rem(g, 4)
        self.x = self.xc // 2
        self.c = lax.rem(self.xc, 2)
        self.y = lax.axis_index("mp")
        self.xo = (1 - self.x) * 2 + self.c
        self.co = self.x * 2 + (1 - self.c)
        self.yo = 1 - self.y
        self.to_z = [None] + [self.device(lax.rem(self.z + j, 4), self.xc, self.y) for j in (1, 2, 3)]
        self.to_x = self.device(self.z, self.xo, self.y)
        self.to_y = self.device(self.z, self.xc, self.yo)
        self.to_c = self.device(self.z, self.co, self.y)

    def device(self, z, xc, y):
        return {"dp": (z * 4 + xc) * self.fold + self.member, "mp": y}

    def greet(self):
        barrier = pltpu.get_barrier_semaphore()
        for device in (*self.to_z[1:], self.to_x, self.to_y, self.to_c):
            pl.semaphore_signal(barrier, inc=1, device_id=device, device_id_type=MESH)
        pl.semaphore_wait(barrier, 6)


class Gather:
    def __init__(self, place, packed, w, lsem, zs, zr, xs, xr, ys, yr, fs, fr, cs, cr):
        self.p, self.packed, self.w, self.lsem = place, packed, w, lsem
        self.sems = (zs, zr, xs, xr, ys, yr, fs, fr, cs, cr)
        self.zj = [lax.rem(place.z + 4 - j, 4) for j in range(4)]
        self.sends = []

    def go(self, copy):
        copy.start()
        self.sends.append(copy)

    def own(self, k):
        p = self.p
        return pltpu.make_async_copy(self.packed.at[k], self.w.at[k, p.y, p.z, p.xc], self.lsem.at[k])

    def src(self, k, j):
        p = self.p
        return self.packed.at[k] if j == 0 else self.w.at[k, p.y, self.zj[j], p.xc]

    def zcopy(self, k, j):
        p, (zs, zr, *_) = self.p, self.sems
        return remote(self.packed.at[k], self.w.at[k, p.y, p.z, p.xc], zs.at[k, j - 1], zr.at[k, j - 1], p.to_z[j])

    def xcopy(self, k, j):
        p, (_, _, xs, xr, *_) = self.p, self.sems
        return remote(self.src(k, j), self.w.at[k, p.y, self.zj[j], p.xc], xs.at[k, j], xr.at[k, j], p.to_x)

    def ycopy(self, k, j):
        p, (_, _, _, _, ys, yr, *_) = self.p, self.sems
        return remote(self.src(k, j), self.w.at[k, p.y, self.zj[j], p.xc], ys.at[k, j], yr.at[k, j], p.to_y)

    def fcopy(self, k, j):
        p, (*_, fs, fr, _, _) = self.p, self.sems
        if j % 2 == 0:
            block, to = self.w.at[k, p.y, self.zj[j], p.xo], p.to_y
        else:
            block, to = self.w.at[k, p.yo, self.zj[j], p.xc], p.to_x
        return remote(block, block, fs.at[k, j], fr.at[k, j], to)

    def ccopy(self, k, i):
        p, (*_, cs, cr) = self.p, self.sems
        y, xc = ((p.y, p.xc), (p.y, p.xo), (p.yo, p.xc), (p.yo, p.xo))[i]
        block = self.w.at[k, y, :, xc]
        return remote(block, block, cs.at[k, i], cr.at[k, i], p.to_c)

    def start(self, k):
        self.own(k).start()
        for j in (1, 2, 3):
            self.go(self.zcopy(k, j))
        self.go(self.xcopy(k, 0))
        self.go(self.ycopy(k, 0))

    def spread(self, k):
        for j in (1, 2, 3):
            self.zcopy(k, j).wait_recv()
            self.go(self.xcopy(k, j))
            self.go(self.ycopy(k, j))
        self.own(k).wait()
        self.go(self.ccopy(k, 0))

    def forward(self, k):
        for j in range(4):
            self.xcopy(k, j).wait_recv()
            if j % 2 == 0:
                self.go(self.fcopy(k, j))
            self.ycopy(k, j).wait_recv()
            if j % 2 == 1:
                self.go(self.fcopy(k, j))
        self.go(self.ccopy(k, 1))
        self.go(self.ccopy(k, 2))

    def share(self, k):
        for j in range(4):
            self.fcopy(k, j).wait_recv()
        self.go(self.ccopy(k, 3))

    def arrive(self, k):
        for i in range(4):
            self.ccopy(k, i).wait_recv()

    def finish(self):
        for copy in self.sends:
            copy.wait_send()

    @staticmethod
    def scratch(n):
        dma = pltpu.SemaphoreType.DMA
        return [dma((n,)), dma((n, 3)), dma((n, 3))] + [dma((n, 4))] * 8


def columns(w, y, cols):
    v = w[y, :, :, :, cols]
    return v.reshape(D, v.shape[-1])


def bounds(lengths, bucket, m):
    l0, l1, one = lengths[m, 0], lengths[m, 1], bucket[m] == 1
    half = S // 2
    return jnp.where(one, l0 + l1, l0), jnp.where(one, 0, half), jnp.where(one, l0 + l1, half + l1)


def key_bias(limits):
    first_end, second_start, second_end = limits
    k = lax.broadcasted_iota(jnp.int32, (S, 128), 0)
    lo = jnp.where(k < first_end, 0.0, -1e9)
    hi = jnp.where((k >= second_start) & (k < second_end), 0.0, -1e9)
    return lo, hi


def with_mask(q2, k2, half, bias):
    lane = lax.broadcasted_iota(jnp.int32, (S, 128), 1)
    low = lax.broadcasted_iota(jnp.int32, (S, 128), 0) < S // 2
    own = (lane // 64) == half
    o = 64 * (1 - half)
    one = lambda pick: jnp.where(pick, 1.0, 0.0)
    qa = jnp.where(lane == o, one(low), jnp.where(lane == o + 1, one(~low), 0.0))
    ka = jnp.where(lane == o, bias[0], jnp.where(lane == o + 1, bias[1], 0.0))
    qm = jnp.where(own, q2.astype(F32) * 0.125, qa).astype(BF16)
    km = jnp.where(own, k2.astype(F32), ka).astype(BF16)
    return qm, km


def head_pair(pair):
    y, r = pair // 3, lax.rem(pair, 3)
    return y, [at(o + 128 * r, 128) for o in (0, HALF, 2 * HALF)]


def attend(qkv, ctx, lse, limits, pair):
    y, (qc, kc, vc) = head_pair(pair)
    q2, k2, v2 = qkv[y, :, qc], qkv[y, :, kc], qkv[y, :, vc]
    bias = key_bias(limits)
    v2t = v2.T
    parts = []
    for half in range(2):
        qm, km = with_mask(q2, k2, half, bias)
        st = dot(km, qm, NT)
        top = jnp.max(st, axis=0, keepdims=True)
        e = jnp.exp(st - top)
        total = jnp.sum(e, axis=0, keepdims=True)
        lse[pair * 2 + half] = top + jnp.log(total)
        ct = dot(v2t[64 * half:64 * half + 64], e.astype(BF16))
        parts.append(ct * (1.0 / total))
    ctx[y, :, qc] = jnp.concatenate(parts, 0).T.astype(BF16)


def normalize(h, rows, gain, shift, n, r):
    v = h[rows, :]
    c = v - jnp.mean(v, axis=-1, keepdims=True)
    inverse = lax.rsqrt(jnp.mean(c * c, axis=-1, keepdims=True) + EPS)
    normed = c * inverse
    n[rows, :] = normed
    r[rows, :] = jnp.broadcast_to(inverse, (inverse.shape[0], 128))
    return normed * gain + shift


def gelu_parts(u):
    cdf = 0.5 * (1.0 + lax.erf(u * 0.7071067811865476))
    return u * cdf, cdf + u * (jnp.exp(-0.5 * u * u) * 0.3989422804014327)


def forward_kernel(fold, layers, packed, xin, cot, vec, glob, lengths, bucket,
                   w, cotf, out, xrt_o, qkv_o, lse_o, ctx_o, n1_o, r1_o, y1t_o, act_o, dg_o, n2_o, r2_o,
                   wv, xh, vecf, x, xr, xrt, qkv, lse, ctx, h, n1, r1, y1, y1r, y1t, act, dg, n2, r2, outv,
                   wsem, esem, ssem, *gsems):
    p = Place(fold)
    m = p.y
    g = Gather(p, packed, w, *gsems)
    parts = 3 * layers
    saves = {}
    names = ("xrt", "qkv", "lse", "ctx", "n1", "r1", "y1t", "act", "dg", "n2", "r2")

    def load(k):
        return pltpu.make_async_copy(w.at[k], wv.at[k % 3], wsem.at[k])

    def save(i, l, src, dst):
        if i in saves:
            saves.pop(i).wait()
        saves[i] = pltpu.make_async_copy(src, dst.at[l], ssem.at[names.index(i), l])
        saves[i].start()

    def before(*names):
        for i in names:
            if i in saves:
                saves.pop(i).wait()

    own_x = pltpu.make_async_copy(xin.at[m], xh.at[m], esem.at[0])
    swap_x = remote(xin.at[1 - m], xh.at[m], esem.at[1], esem.at[2], p.to_y)
    own_c = pltpu.make_async_copy(cot.at[m], cotf.at[m], esem.at[3])
    swap_c = remote(cot.at[1 - m], cotf.at[m], esem.at[4], esem.at[5], p.to_y)
    own_v = pltpu.make_async_copy(vec, vecf.at[m], esem.at[6])
    swap_v = remote(vec, vecf.at[m], esem.at[7], esem.at[8], p.to_y)
    limits = bounds(lengths, bucket, m)

    def row(i):
        return glob[i:i + 1, :]

    def stage_a(l):
        wa = wv.at[3 * l % 3]
        before("xrt", "qkv", "lse", "ctx", "n1", "r1", "y1t")
        xrt[...] = xr[...].T
        save("xrt", l, xrt, xrt_o)
        for y in range(2):
            for t in range(3):
                cols = slice(HALF * t, HALF * t + HALF)
                v = dot(xr[...], columns(wa, y, cols))
                if t != 1:
                    v = v + vecf[y, 2 + l:3 + l, HALF * (t // 2):HALF * (t // 2) + HALF]
                qkv[y, :, cols] = v.astype(BF16)
        save("qkv", l, qkv, qkv_o)

    def stage_att(l, first, last):
        pl.loop(first, last)(lambda i: attend(qkv, ctx, lse, limits, i))

    def stage_out(l):
        wa = wv.at[3 * l % 3]
        save("lse", l, lse, lse_o)
        save("ctx", l, ctx, ctx_o)
        wo = [columns(wa, y, slice(3 * HALF, 4 * HALF)) for y in range(2)]
        h[...] = x[...] + row(6 * l) + dot(ctx[0], wo[0], NT) + dot(ctx[1], wo[1], NT)

        @pl.loop(0, 4)
        def _(i):
            rows = at(128 * i, 128)
            o = normalize(h, rows, row(6 * l + 2), row(6 * l + 4), n1, r1)
            y1[rows, :] = o
            y1r[rows, :] = o.astype(BF16)
        y1t[...] = y1r[...].T
        save("n1", l, n1, n1_o)
        save("r1", l, r1, r1_o)
        save("y1t", l, y1t, y1t_o)

    def stage_b(l):
        wb = wv.at[(3 * l + 1) % 3]
        before("act", "dg", "n2", "r2")
        for y in range(2):
            @pl.loop(0, 3)
            def _(i):
                cols = at(512 * i, 512)
                u = dot(y1r[...], columns(wb, y, cols)) + vecf[y, l:l + 1, cols]
                a, d = gelu_parts(u)
                act[y, :, cols] = a.astype(BF16)
                dg[y, :, cols] = d.astype(BF16)
        save("act", l, act, act_o)
        save("dg", l, dg, dg_o)

    def stage_c(l):
        wc = wv.at[(3 * l + 2) % 3]
        full = slice(0, UNITS)
        h[...] = (y1[...] + row(6 * l + 1) + dot(act[0], columns(wc, 0, full), NT)
                  + dot(act[1], columns(wc, 1, full), NT))

        @pl.loop(0, 4)
        def _(i):
            rows = at(128 * i, 128)
            o = normalize(h, rows, row(6 * l + 3), row(6 * l + 5), n2, r2)
            x[rows, :] = o
            xr[rows, :] = o.astype(BF16)
        save("n2", l, n2, n2_o)
        save("r2", l, r2, r2_o)

    def compute(k):
        l, kind = k // 3, k % 3
        load(k).wait()
        if kind == 0:
            stage_a(l)
            stage_att(l, 0, 6)
            stage_out(l)
        elif kind == 1:
            stage_b(l)
        else:
            stage_c(l)

    own_x.start()
    own_v.start()
    own_c.start()
    p.greet()
    g.start(0)
    swap_v.start()
    swap_x.start()
    g.start(1)
    g.spread(0)
    for k in range(parts + 2):
        if k + 2 < parts:
            g.start(k + 2)
        if k + 1 < parts:
            g.spread(k + 1)
        if k == 1:
            swap_c.start()
        if k < parts:
            g.forward(k)
        if 0 <= k - 1 < parts:
            g.share(k - 1)
        if 0 <= k - 2 < parts:
            g.arrive(k - 2)
            load(k - 2).start()
            if k == 2:
                own_x.wait()
                swap_x.wait()
                own_v.wait()
                swap_v.wait()
                for i in range(2):
                    rows = slice(256 * i, 256 * i + 256)
                    xr[rows, :] = xh[i]
                    x[rows, :] = xh[i].astype(F32)
            compute(k - 2)
    own_c.wait()
    swap_c.wait()
    last = pltpu.make_async_copy(xr, out, esem.at[9])
    last.start()
    g.finish()
    for copy in saves.values():
        copy.wait()
    last.wait()


def forward(packed, xin, cot, vec, glob, lengths, bucket, layers, fold):
    n = 3 * layers
    dma = pltpu.SemaphoreType.DMA
    saved = [((D, S), BF16), ((2, S, 3 * HALF), BF16), ((12, 1, S), F32), ((2, S, HALF), BF16), ((S, D), F32), ((S, 128), F32),
             ((D, S), BF16), ((2, S, UNITS), BF16), ((2, S, UNITS), BF16), ((S, D), F32), ((S, 128), F32)]
    shape = jax.ShapeDtypeStruct
    vm = pltpu.VMEM
    return pl.pallas_call(
        functools.partial(forward_kernel, fold, layers),
        out_shape=[shape((n, 2, 4, 4, 48, UNITS), BF16), shape((2, S // 2, D), BF16), shape((S, D), BF16)]
        + [shape((layers, *s), d) for s, d in saved],
        in_specs=[ANY, ANY, ANY, ANY, VMEM, SMEM, SMEM],
        out_specs=[ANY] * (3 + len(saved)),
        scratch_shapes=[
            vm((3, 2, 4, 4, 48, UNITS), BF16), vm((2, S // 2, D), BF16), vm((2, 8, UNITS), F32), vm((S, D), F32),
            vm((S, D), BF16), vm((D, S), BF16), vm((2, S, 3 * HALF), BF16), vm((12, 1, S), F32), vm((2, S, HALF), BF16),
            vm((S, D), F32), vm((S, D), F32), vm((S, 128), F32), vm((S, D), F32), vm((S, D), BF16), vm((D, S), BF16),
            vm((2, S, UNITS), BF16), vm((2, S, UNITS), BF16), vm((S, D), F32), vm((S, 128), F32),
            vm((S, D), BF16), dma((n,)), dma((10,)), dma((11, layers)), *Gather.scratch(n)],
        compiler_params=pltpu.CompilerParams(collective_id=1, has_side_effects=True, vmem_limit_bytes=60 * 2**20),
    )(packed, xin, cot, vec, glob, lengths, bucket)


class Reduce:
    def __init__(self, place, total, slots, held, out, rc, rx, ry, rx2, ry2, rz, cs, cr, xs, xr, ys, yr, zs, zr, free):
        self.p, self.total, self.slots = place, total, slots
        self.held, self.out, self.buffers = held, out, (rc, rx, ry, rx2, ry2, rz)
        self.sems = (cs, cr, xs, xr, ys, yr, zs, zr)
        self.free = free
        self.sends = {}
        self.at = {}
        self.fresh = None

    def slot(self, u):
        for copy in self.sends.pop(u - self.slots, ()):
            copy.wait_send()
        return self.held.at[u % self.slots]

    def go(self, u, copy):
        copy.start()
        self.sends.setdefault(u, []).append(copy)

    def copies(self, u, kind, j=0):
        p, s = self.p, u % self.slots
        h = self.held.at[s]
        rc, rx, ry, rx2, ry2, rz = self.buffers
        cs, cr, xs, xr, ys, yr, zs, zr = self.sems
        if kind == "c":
            return remote(h.at[:, :, :, 1 - p.c], rc.at[s], cs.at[s], cr.at[s], p.to_c)
        if kind == "x1":
            return remote(h.at[:, 0:2, 1 - p.x, p.c], rx.at[s], xs.at[s, 0], xr.at[s, 0], p.to_x)
        if kind == "y1":
            return remote(h.at[p.yo, 2:4, :, p.c], ry.at[s], ys.at[s, 0], yr.at[s, 0], p.to_y)
        if kind == "y2":
            return remote(h.at[p.yo, 0:2, p.x, p.c], ry2.at[s], ys.at[s, 1], yr.at[s, 1], p.to_y)
        if kind == "x2":
            return remote(h.at[p.y, 2:4, 1 - p.x, p.c], rx2.at[s], xs.at[s, 1], xr.at[s, 1], p.to_x)
        to = lax.rem(p.z + j, 4)
        return remote(h.at[p.y, to, p.x, p.c], rz.at[s, j - 1], zs.at[s, j - 1], zr.at[s, j - 1], p.to_z[j])

    def peers(self):
        p = self.p
        return (p.to_c, p.to_x, p.to_y, p.to_z[1], p.to_z[2], p.to_z[3])

    def submit(self, u):
        if u >= self.slots:
            for i in range(6):
                pl.semaphore_wait(self.free.at[i], 1)
        self.go(u, self.copies(u, "c"))
        self.at[u] = 0
        self.fresh = u

    def stage(self, i, u):
        p, s = self.p, u % self.slots
        h = self.held.at[s]
        rc, rx, ry, rx2, ry2, rz = (b.at[s] for b in self.buffers)
        wait = lambda kind, j=0: self.copies(u, kind, j).wait_recv()
        if i == 1:
            wait("c")

            @pl.loop(0, 16)
            def _(n):
                y, z, x = n // 8, lax.rem(n // 2, 4), lax.rem(n, 2)
                h[y, z, x, p.c] = h[y, z, x, p.c] + rc[y, z, x]
            self.go(u, self.copies(u, "x1"))
            self.go(u, self.copies(u, "y1"))
        elif i == 2:
            wait("x1")
            wait("y1")

            @pl.loop(0, 4)
            def _(n):
                a, b = n // 2, lax.rem(n, 2)
                h[a, b, p.x, p.c] = h[a, b, p.x, p.c] + rx[a, b]
                h[p.y, 2 + a, b, p.c] = h[p.y, 2 + a, b, p.c] + ry[a, b]
            self.go(u, self.copies(u, "y2"))
            self.go(u, self.copies(u, "x2"))
        elif i == 3:
            wait("x2")
            wait("y2")

            @pl.loop(0, 2)
            def _(n):
                h[p.y, n, p.x, p.c] = h[p.y, n, p.x, p.c] + ry2[n]
                h[p.y, 2 + n, p.x, p.c] = h[p.y, 2 + n, p.x, p.c] + rx2[n]
            for j in (1, 2, 3):
                self.go(u, self.copies(u, "z", j))
        else:
            for j in (1, 2, 3):
                wait("z", j)
            f = lambda v: v.astype(F32)
            self.out[u] = f(h[p.y, p.z, p.x, p.c]) + f(rz[0]) + f(rz[1]) + f(rz[2])
            if u + self.slots < self.total:
                for i, device in zip((0, 1, 2, 5, 4, 3), self.peers()):
                    pl.semaphore_signal(self.free.at[i], inc=1, device_id=device, device_id_type=MESH)

    def pump(self):
        for u in sorted(self.at, reverse=True):
            if u == self.fresh:
                continue
            self.at[u] += 1
            self.stage(self.at[u], u)
            if self.at[u] == 4:
                del self.at[u]
        self.fresh = None

    def finish(self):
        for copies in self.sends.values():
            for copy in copies:
                copy.wait_send()

    @staticmethod
    def scratch(n, part):
        dma = pltpu.SemaphoreType.DMA
        v = lambda *s: pltpu.VMEM((n, *s, 48, part), BF16)
        return [v(2, 4, 2, 2)], [v(2, 4, 2), v(2, 2), v(2, 2), v(2), v(2), v(3), dma((n,)), dma((n,))] + [dma((n, 2))] * 4 + [
            dma((n, 3))] * 2 + [pltpu.SemaphoreType.REGULAR((6,))]


class Total:
    def __init__(self, place, v, got, zall, sems):
        self.p, self.v, self.got, self.zall = place, v, got, zall
        self.send, self.recv = sems
        self.last = []

    def copy(self, i):
        p = self.p
        if i < 3:
            return remote(self.v.at[i], self.got.at[i], self.send.at[i], self.recv.at[i], (p.to_c, p.to_x, p.to_y)[i])
        return remote(self.v.at[3], self.zall.at[p.z], self.send.at[i], self.recv.at[i], p.to_z[i - 2])

    def step(self, i, out=None):
        if 1 <= i <= 3:
            self.copy(i - 1).wait_recv()
            self.v[i] = self.v[i - 1] + self.got[i - 1]
        if i < 3:
            self.copy(i).start()
        elif i == 3:
            for j in (3, 4, 5):
                self.copy(j).start()
            self.zall[self.p.z] = self.v[3]
        else:
            for j in (3, 4, 5):
                self.copy(j).wait_recv()
            z = self.zall
            out[...] = (z[0] + z[1]) + (z[2] + z[3])
            for j in range(6):
                self.copy(j).wait_send()

    @staticmethod
    def scratch(rows):
        dma = pltpu.SemaphoreType.DMA
        v = lambda n: pltpu.VMEM((n, rows, D), F32)
        return [v(4), v(3), v(4), dma((6,)), dma((6,))]


def attend_back(qkv, lse, gc, gqkv, sums, limits, pair):
    y, (qc, kc, vc) = head_pair(pair)
    q2, k2, v2, c2 = qkv[y, :, qc], qkv[y, :, kc], qkv[y, :, vc], gc[y, :, qc]
    bias = key_bias(limits)
    lane = lax.broadcasted_iota(jnp.int32, (S, 128), 1)
    k2t = k2.T
    gq, gk, gv = [], [], []
    for half in range(2):
        qm, km = with_mask(q2, k2, half, bias)
        st = dot(km, qm, NT)
        probs = jnp.exp(st - lse[pair * 2 + half])
        vm = jnp.where((lane // 64) == half, v2, jnp.zeros_like(v2))
        gp = dot(vm, c2, NT)
        prod = probs * gp
        total = jnp.sum(prod, axis=0, keepdims=True)
        gs = (prod - probs * total).astype(BF16)
        gv.append(dot(probs.astype(BF16), c2))
        gk.append(dot(gs, q2))
        gq.append(dot(k2t[64 * half:64 * half + 64], gs))
    pick = lambda v: jnp.where(lane < 64, v[0], v[1])
    gqt = jnp.concatenate(gq, 0).T * 0.125
    gkt = pick(gk) * 0.125
    gvt = pick(gv)
    gqkv[y, :, qc] = gqt.astype(BF16)
    gqkv[y, :, kc] = gkt.astype(BF16)
    gqkv[y, :, vc] = gvt.astype(BF16)
    sums[y, 0, :, qc] = jnp.sum(gqt, axis=0, keepdims=True)
    sums[y, 1, :, qc] = jnp.sum(gvt, axis=0, keepdims=True)


def norm_back(g, rows, gain, n, r):
    v = g[rows, :]
    normed, inverse = n[rows, :], r[rows, 0:1]
    e = v * gain
    gh = inverse * (e - jnp.mean(e, axis=-1, keepdims=True) - normed * jnp.mean(e * normed, axis=-1, keepdims=True))
    add = lambda t: jnp.sum(t, axis=0, keepdims=True)
    return gh, add(v * normed), add(v), add(gh)


SLOTS = 5
PART = UNITS // 2
ROWS = 24


def backward_kernel(fold, layers, w, cotf, outx, glob, lengths, bucket,
                    xrt_o, qkv_o, lse_o, ctx_o, n1_o, r1_o, y1t_o, act_o, dg_o, n2_o, r2_o,
                    output, ingrad, shards, vout, vlate,
                    wv, g, gh, n, r, low, lowt, act, dg, y1t, ctx, qkv, lse, xrt, gc, gqkv, sums, gin,
                    wsem, lsem, esem, *rest):
    p = Place(fold)
    m = p.y
    red = Reduce(p, 6 * layers, SLOTS, rest[0], shards, *rest[1:16])
    early = Total(p, *rest[16:19], rest[19:21])
    late = Total(p, *rest[21:24], rest[24:26])
    limits = bounds(lengths, bucket, m)
    order = [3 * l + t for l in reversed(range(layers)) for t in (2, 1, 0)]
    full = slice(0, UNITS)

    def row(i):
        return glob[i:i + 1, :]

    def weights(i):
        return pltpu.make_async_copy(w.at[order[i]], wv.at[i % 2], wsem.at[i % 2])

    table = {"n2": (n2_o, n), "r2": (r2_o, r), "act": (act_o, act), "dg": (dg_o, dg), "y1t": (y1t_o, y1t),
             "n1": (n1_o, n), "r1": (r1_o, r), "ctx": (ctx_o, ctx), "qkv": (qkv_o, qkv), "lse": (lse_o, lse),
             "xrt": (xrt_o, xrt)}
    loads = {}

    def begin(l, *names):
        for i in names:
            src, dst = table[i]
            loads[i] = pltpu.make_async_copy(src.at[l], dst, lsem.at[list(table).index(i)])
            loads[i].start()

    def need(*names):
        for i in names:
            loads.pop(i).wait()

    def add(line, value):
        early.v[0, line:line + 1, :] = early.v[0, line:line + 1, :] + value

    def norm_stage(l, which):
        base = 12 * (layers - 1 - l)

        @pl.loop(0, 4)
        def _(i):
            rows = at(128 * i, 128)
            v, a, b, c = norm_back(g, rows, row(6 * l + 2 + which), n, r)
            gh[rows, :] = v
            low[rows, :] = v.astype(BF16)
            add(base + which, a)
            add(base + 2 + which, b)
            add(base + 4 + which, c)
        lowt[...] = low[...].T

    def tiles(u, left, right, start, width, to):
        s = red.slot(u)
        for y in range(2):
            @pl.loop(0, width // HALF)
            def _(i):
                v = dot(left[...], right[y, :, at(start + HALF * i, HALF)]).astype(BF16)
                s[y, :, :, :, :, at(to + HALF * i, HALF)] = v.reshape(4, 2, 2, 48, HALF)

    def submit(u):
        red.submit(u)
        red.pump()

    def layer(l, u, i):
        base = 12 * (layers - 1 - l)
        last = l == 0
        need("n2", "r2")
        norm_stage(l, 1)
        begin(l, "n1", "r1")
        need("act")
        for half in range(2):
            tiles(u + half, lowt, act, PART * half, PART, 0)
            submit(u + half)
        if not last:
            begin(l - 1, "act")
        weights(i).wait()
        wc = wv.at[i % 2]
        need("dg", "y1t")
        for half in range(2):
            for y in range(2):
                @pl.loop(0, 2)
                def _(j):
                    cols = at(PART * half + HALF * j, HALF)
                    gi = dot(low[...], columns(wc, y, cols)) * dg[y, :, cols].astype(F32)
                    dg[y, :, cols] = gi.astype(BF16)
                    line = base + 6 + 2 * y + half
                    early.v[0, line:line + 1, at(HALF * j, HALF)] = jnp.sum(gi, axis=0, keepdims=True)
            tiles(u + 2 + half, y1t, dg, PART * half, PART, 0)
            submit(u + 2 + half)
        if i + 2 < 3 * layers:
            weights(i + 2).start()
        weights(i + 1).wait()
        wb = wv.at[(i + 1) % 2]
        g[...] = gh[...] + dot(dg[0], columns(wb, 0, full), NT) + dot(dg[1], columns(wb, 1, full), NT)
        if i + 3 < 3 * layers:
            weights(i + 3).start()
        if not last:
            begin(l - 1, "dg", "y1t")
        need("n1", "r1")
        norm_stage(l, 0)
        red.pump()
        need("ctx")
        tiles(u + 4, lowt, ctx, 0, HALF, HALF)
        weights(i + 2).wait()
        wa = wv.at[(i + 2) % 2]
        for y in range(2):
            gc[y] = dot(low[...], columns(wa, y, slice(3 * HALF, 4 * HALF))).astype(BF16)
        if not last:
            begin(l - 1, "n2", "r2", "ctx")
        else:
            early.step(0)
        need("qkv", "lse", "xrt")
        pl.loop(0, 3)(lambda j: attend_back(qkv, lse, gc, gqkv, sums, limits, j))
        red.pump()
        if last:
            early.step(1)
        pl.loop(3, 6)(lambda j: attend_back(qkv, lse, gc, gqkv, sums, limits, j))
        if last:
            early.step(2)
        for y in range(2):
            for t in range(2):
                where = slice(HALF * y, HALF * y + HALF)
                if last:
                    late.v[0, t:t + 1, where] = sums[y, t]
                else:
                    early.v[0, base + 10 + t:base + 11 + t, where] = sums[y, t]
        tiles(u + 4, xrt, gqkv, 2 * HALF, HALF, 0)
        submit(u + 4)
        tiles(u + 5, xrt, gqkv, 0, 2 * HALF, 0)
        submit(u + 5)
        wqkv = [columns(wa, y, slice(0, 3 * HALF)) for y in range(2)]
        if last:
            early.step(3)
            late.step(0)
            for j in range(2):
                rows = at((S // 2) * (1 - m if j == 0 else m), S // 2)
                v = gh[rows, :] + dot(gqkv[0, rows, :], wqkv[0], NT) + dot(gqkv[1, rows, :], wqkv[1], NT)
                gin[j] = v.astype(BF16)
                if j == 0:
                    swap_g.start()
            own_g.start()
        else:
            g[...] = gh[...] + dot(gqkv[0], wqkv[0], NT) + dot(gqkv[1], wqkv[1], NT)
            begin(l - 1, "qkv", "lse", "xrt")
            if i + 4 < 3 * layers:
                weights(i + 4).start()

    own_o = pltpu.make_async_copy(outx.at[m], output.at[m], esem.at[0])
    swap_o = remote(outx.at[1 - m], output.at[m], esem.at[1], esem.at[2], p.to_y)
    own_g = pltpu.make_async_copy(gin.at[1], ingrad.at[m], esem.at[3])
    swap_g = remote(gin.at[0], ingrad.at[m], esem.at[4], esem.at[5], p.to_y)
    top = layers - 1
    cload = pltpu.make_async_copy(cotf, low, esem.at[6])
    cload.start()
    begin(top, "n2", "r2", "act")
    weights(0).start()
    begin(top, "dg", "y1t")
    weights(1).start()
    begin(top, "ctx", "qkv", "lse", "xrt")
    early.v[0] = jnp.zeros((ROWS, D), F32)
    late.v[0] = jnp.zeros((8, D), F32)
    cload.wait()
    g[...] = low[...].astype(F32)
    own_o.start()
    p.greet()
    swap_o.start()
    for j, l in enumerate(reversed(range(layers))):
        layer(l, 6 * j, 3 * j)
    early.step(4, vout)
    for step in range(1, 5):
        if red.at:
            red.pump()
        late.step(step, vlate)
    while red.at:
        red.pump()
    red.finish()
    own_o.wait()
    swap_o.wait()
    own_g.wait()
    swap_g.wait()


def backward(w, cotf, outx, glob, lengths, bucket, saved, layers, fold):
    n = 6 * layers
    dma = pltpu.SemaphoreType.DMA
    shape = jax.ShapeDtypeStruct
    vm = pltpu.VMEM
    first, rest = Reduce.scratch(SLOTS, PART)
    return pl.pallas_call(
        functools.partial(backward_kernel, fold, layers),
        out_shape=[shape((2, S // 2, D), BF16), shape((2, S // 2, D), BF16), shape((n, 48, PART), F32),
                   shape((ROWS, D), F32), shape((8, D), F32)],
        in_specs=[ANY, ANY, ANY, VMEM, SMEM, SMEM] + [ANY] * 11,
        out_specs=[ANY, ANY, VMEM, VMEM, VMEM],
        scratch_shapes=[
            vm((2, 2, 4, 4, 48, UNITS), BF16), vm((S, D), F32), vm((S, D), F32), vm((S, D), F32), vm((S, 128), F32),
            vm((S, D), BF16), vm((D, S), BF16), vm((2, S, UNITS), BF16), vm((2, S, UNITS), BF16), vm((D, S), BF16),
            vm((2, S, HALF), BF16), vm((2, S, 3 * HALF), BF16), vm((12, 1, S), F32), vm((D, S), BF16), vm((2, S, HALF), BF16),
            vm((2, S, 3 * HALF), BF16), vm((2, 2, 1, HALF), F32), vm((2, S // 2, D), BF16),
            dma((2,)), dma((11,)), dma((7,)), *first, *rest, *Total.scratch(ROWS), *Total.scratch(8)],
        compiler_params=pltpu.CompilerParams(collective_id=2, has_side_effects=True, vmem_limit_bytes=62 * 2**20),
    )(w, cotf, outx, glob, lengths, bucket, *saved)


def pack(w_qkv, w_out, w_up, w_down):
    parts = []
    for l in range(w_qkv.shape[0]):
        parts.append(jnp.concatenate([w_qkv[l, 0], w_qkv[l, 1], w_qkv[l, 2], w_out[l].T], 1))
        parts.append(w_up[l])
        parts.append(w_down[l].T)
    return jnp.stack(parts)


def per_device(layer_input, cotangent, lengths, bucket, w_qkv, bias_qv, w_out, bias_out, ln_gain, ln_bias, w_up, bias_up, w_down):
    layers = w_qkv.shape[0]
    fold = lax.axis_size("dp") // GROUPS
    members = [[g * fold + i for i in range(fold)] for g in range(GROUPS)]
    packed = pack(w_qkv, w_out, w_up, w_down)
    if fold > 1:
        packed = lax.all_gather(packed, "dp", axis=1, tiled=True, axis_index_groups=members)
    qv = jnp.pad(bias_qv.reshape(layers, 2 * HALF), ((0, 0), (0, UNITS - 2 * HALF)))
    vec = jnp.concatenate([bias_up, qv], 0).astype(F32)
    vec = jnp.pad(vec, ((0, 8 - vec.shape[0]), (0, 0)))
    glob = jnp.concatenate([bias_out, ln_gain, ln_bias], 1).astype(F32).reshape(6 * layers, D)
    glob = jnp.pad(glob, ((0, 16 - 6 * layers), (0, 0)))
    w, cotf, out, *saved = forward(packed, layer_input, cotangent, vec, glob, lengths, bucket, layers, fold)
    output, ingrad, shards, early, late = backward(
        w, cotf.reshape(S, D), out.reshape(2, S // 2, D), glob, lengths, bucket, saved, layers, fold)
    if fold > 1:
        shards = lax.psum_scatter(shards, "dp", scatter_dimension=1, tiled=True, axis_index_groups=members)
        early, late = lax.psum((early, late), "dp", axis_index_groups=members)
    rows = shards.shape[1]
    part = lax.axis_index("mp")
    shards = jnp.flip(shards.reshape(layers, 6, rows, PART), 0)
    down, up, vo, qk = shards[:, 0:2], shards[:, 2:4], shards[:, 4], shards[:, 5]
    grad_qkv = jnp.stack([qk[..., :HALF], qk[..., HALF:], vo[..., :HALF]], 1)
    grad_out = vo[..., HALF:].transpose(0, 2, 1)
    grad_up = up.transpose(0, 2, 1, 3).reshape(layers, rows, UNITS)
    grad_down = down.transpose(0, 1, 3, 2).reshape(layers, UNITS, rows)
    vecs = jnp.flip(early.reshape(layers, 12, D), 0)
    gain, shift, bias = vecs[:, 0:2], vecs[:, 2:4], vecs[:, 4:6]
    grad_bias_up = lax.dynamic_slice_in_dim(vecs[:, 6:10].reshape(layers, 2, UNITS), part, 1, 1)[:, 0]
    qv = jnp.concatenate([late[None, 0:2], vecs[1:, 10:12]], 0)
    qv = lax.dynamic_slice_in_dim(qv, part * HALF, HALF, 2)
    return output, ingrad, grad_qkv, qv, grad_out, bias, gain, shift, grad_up, grad_bias_up, grad_down


def solution(mesh):
    in_specs = (
        P("dp", "mp", None),
        P("dp", "mp", None),
        P("dp", None),
        P("dp"),
        P(None, None, "dp", "mp"),
        P(None, None, "mp"),
        P(None, "mp", "dp"),
        P(),
        P(),
        P(),
        P(None, "dp", "mp"),
        P(None, "mp"),
        P(None, "mp", "dp"),
    )
    out_specs = (
        P("dp", "mp", None),
        P("dp", "mp", None),
        P(None, None, "dp", "mp"),
        P(None, None, "mp"),
        P(None, "mp", "dp"),
        P(),
        P(),
        P(),
        P(None, "dp", "mp"),
        P(None, "mp"),
        P(None, "mp", "dp"),
    )
    return jax.shard_map(
        per_device, mesh=mesh, in_specs=in_specs, out_specs=out_specs, check_vma=False
    )
```

time: 1500 us -> 377 us (0.25)
  waiting for transfers between devices: 751 us -> 0 us
  Pallas kernels: 0 us -> 352 us
  matrix products: 307 us -> 0 us
  blocking collectives: 253 us -> 0 us
  local copies, waits for them, and re-layouts: 88.6 us -> 17 us
  other arithmetic: 61.2 us -> 3.49 us
  between operations: 22.6 us -> 0.99 us
    pallas_call x0 -> x2, Pallas kernels: none -> 352 us  [the longest x1 181 us: backward(): pl.pallas_call(functools.partial(backward_kernel, fold, layers), out_shap...]
    unnamed x26 -> x0, waiting for transfers between devices: 335 us -> none
    dot_general x72 -> x0, matrix products: 307 us -> none  [the longest x4 53.4 us: backward_layer(): jnp.einsum('bhqk,bkhe->bqhe', scores_low, keys_low, preferred_element_typ...]
    all_gather x18 -> x0, blocking collectives: 253 us -> none  [the longest x8 109 us: gather_rows(): return lax.all_gather(values, 'mp', axis=1, tiled=True)]
    reduce_scatter x17 -> x0, waiting for transfers between devices: 238 us -> none  [the longest x1 111 us: per_device(): lax.psum_scatter(up_stack, 'dp', scatter_dimension=1, tiled=True)]
    all_gather x6 -> x0, waiting for transfers between devices: 145 us -> none  [the longest x2 64.9 us: per_device(): lax.all_gather(w_down[layer_index], 'dp', axis=1, tiled=True)]
    another operation x47 -> x2, local copies, waits for them, and re-layouts: 44.7 us -> 0.94 us  [the longest x1 0.92 us: pack(): return jnp.stack(parts)]
    psum x1 -> x0, waiting for transfers between devices: 31.9 us -> none  [per_device(): lax.psum((qv_full, bias_stack, gain_stack, shift_stack, up_full), ('dp',...]
  transfers between devices with their start and end apart: 25 -> 0, of which waited for: 18 -> 0; matrix products, arithmetic and copies ran while one was open for 18% -> 0% of each run, Pallas kernels for 0% -> 0%
where the time goes in v2:
time: 377 us; the launch traced here: 374 us
  Pallas kernels  352 us (93%)
  local copies, waits for them, and re-layouts  17 us (5%)
    pallas_call x1, Pallas kernels, backward(): pl.pallas_call(functools.partial(backward_kernel, fold, layers), out_shap...  181 us
    pallas_call x1, Pallas kernels, forward(): pl.pallas_call(functools.partial(forward_kernel, fold, layers), out_shape...  171 us
    unnamed x18, local copies, waits for them, and re-layouts  7.8 us

profile of v2, /device:TPU:0, one launch (start us, length us, event | category | flops | bytes accessed | tf_op | source)
XLA Modules:
  0.0 373.6 jit_solution(1797651318081133487)
XLA Ops:
  0.6 0.9 slice_bitcast_fusion.9
  1.5 0.8 slice_bitcast_fusion.6
  2.3 0.9 slice_dynamic-update-slice_fusion.1
  3.3 0.9 bitcast_dynamic-update-slice_fusion.1
  4.2 0.9 slice_dynamic-update-slice_fusion
  5.2 0.9 bitcast_dynamic-update-slice_fusion.packed
  6.1 0.0 copy-start
  6.1 0.9 pad_maximum_fusion.1
  7.0 0.6 pad_convert_fusion.glob
  7.6 0.7 copy.39
  8.3 0.7 fusion.3
  9.0 0.6 pad_convert_fusion.1.vec
  9.6 0.0 copy-done
  9.6 171.4 %shard_map.212 = (bf16[6,2,4,4,48,1536]{5,4,3,2,1,0:T(8,128)(2,1)}, bf16[2,256,768]{2,1,0:T(8,128)(2,1)}, bf16[512,768]{1,0:T(8,128)(2,1)}, bf16[2,768,512]{2,1,...) custom-call(bf16[6,48,1536]{2,1,0:T(8,128)(2,1)} %copy-done, ...), custom_call_target="tpu_custom_call" | custom-call | tf_op jit(solution)/shard_map/pallas_call | solution.py:392
  181.0 180.8 %shard_map.213 = (bf16[2,256,768]{2,1,0:T(8,128)(2,1)}, bf16[2,256,768]{2,1,0:T(8,128)(2,1)}, f32[12,48,768]{2,1,0:T(8,128)}, f32[24,768]{1,0:T(8,128)}, f32[8,768]{1,0:T(8,128)}) custom-call(bf16[6,2,4,4,48,1536]{5,4,3,2,1,0:T(8,128)(2,1)} %get-tuple-element.30.w, bf16[512,768]{1,0:T(8,128)(2,1)} %bitcast.76, bf16[2,256,768]{2,1,0:T(8,128)(2,1)} %bitcast.77, ...), custom_call_target="tpu_custom_call" | custom-call | tf_op jit(solution)/shard_map/pallas_call | solution.py:794
  361.9 0.0 copy-start.3
  361.9 1.4 fusion.5
  363.2 0.1 reverse_bitcast_fusion
  363.3 0.9 copy.37
  364.2 0.9 copy.38
  365.1 0.8 slice_bitcast_fusion.14
  365.9 0.6 fusion.4
  366.5 1.1 slice_bitcast_fusion.1
  367.7 0.7 slice_bitcast_fusion.2
  368.4 0.8 copy.33
  369.3 0.6 copy.41
  369.9 0.6 slice.126
  370.5 0.6 slice.128
  371.1 0.6 slice.130
  371.7 0.9 copy.49
  372.6 0.0 copy-done.1
  372.6 0.9 copy.50
  (17 shorter events, 0.2 us)
Async XLA Ops:
  6.1 3.6 copy-start
  361.9 3.2 copy-start.3
  365.1 6.6 %copy-start.2 = (bf16[2,256,768]{2,1,0:T(8,128)(2,1)S(1)}, bf16[2,256,768]{2,1,0:T(8,128)(2,1)}, u32[]{:S(2)}) copy-start(bf16[2,256,768]{2,1,0:T(8,128)(2,1)} %get-tuple-element.105) | copy-start | bytes 2359300
  367.6 5.0 %copy-start.1 = (bf16[2,256,768]{2,1,0:T(8,128)(2,1)S(1)}, bf16[2,256,768]{2,1,0:T(8,128)(2,1)}, u32[]{:S(2)}) copy-start(bf16[2,256,768]{2,1,0:T(8,128)(2,1)} %get-tuple-element.106) | copy-start | bytes 2359300

commit v3 on v2

v3 whole, which is shorter than its diff:
```python
import functools

import jax
import jax.numpy as jnp
from jax import lax
from jax.experimental import pallas as pl
from jax.experimental.pallas import tpu as pltpu
from jax.sharding import PartitionSpec as P

F32 = jnp.float32
BF16 = jnp.bfloat16
S = 512
D = 768
HALF = 384
UNITS = 1536
GROUPS = 16
EPS = 1e-12
MESH = pl.DeviceIdType.MESH
NN = (((1,), (0,)), ((), ()))
NT = (((1,), (1,)), ((), ()))
TN = (((0,), (0,)), ((), ()))
ANY = pl.BlockSpec(memory_space=pl.ANY)
VMEM = pl.BlockSpec(memory_space=pltpu.VMEM)
SMEM = pl.BlockSpec(memory_space=pltpu.SMEM)


def dot(a, b, dims=NN):
    return lax.dot_general(a, b, dims, preferred_element_type=F32)


def at(start, size):
    return pl.ds(pl.multiple_of(start, size), size)


def remote(src, dst, send_sem, recv_sem, device):
    return pltpu.make_async_remote_copy(
        src_ref=src, dst_ref=dst, send_sem=send_sem, recv_sem=recv_sem,
        device_id=device, device_id_type=MESH)


class Place:
    def __init__(self, fold):
        d = lax.axis_index("dp")
        self.fold = fold
        self.member = lax.rem(d, fold) if fold > 1 else 0
        g = d // fold if fold > 1 else d
        self.z = g // 4
        self.xc = lax.rem(g, 4)
        self.x = self.xc // 2
        self.c = lax.rem(self.xc, 2)
        self.y = lax.axis_index("mp")
        self.xo = (1 - self.x) * 2 + self.c
        self.co = self.x * 2 + (1 - self.c)
        self.yo = 1 - self.y
        self.to_z = [None] + [self.device(lax.rem(self.z + j, 4), self.xc, self.y) for j in (1, 2, 3)]
        self.to_x = self.device(self.z, self.xo, self.y)
        self.to_y = self.device(self.z, self.xc, self.yo)
        self.to_c = self.device(self.z, self.co, self.y)

    def device(self, z, xc, y):
        return {"dp": (z * 4 + xc) * self.fold + self.member, "mp": y}

    def greet(self):
        barrier = pltpu.get_barrier_semaphore()
        for device in (*self.to_z[1:], self.to_x, self.to_y, self.to_c):
            pl.semaphore_signal(barrier, inc=1, device_id=device, device_id_type=MESH)
        pl.semaphore_wait(barrier, 6)


class Gather:
    def __init__(self, place, packed, w, turned, via_x, lsem, zs, zr, xs, xr, ys, yr, fs, fr, cs, cr, qs, qr):
        self.p, self.packed, self.w, self.turned, self.via_x = place, packed, w, turned, via_x
        self.sems = dict(z=(zs, zr), x=(xs, xr), y=(ys, yr), f=(fs, fr), c=(cs, cr), q=(qs, qr))
        self.lsem = lsem
        z = place.z
        low = z < 2
        self.order = [z, jnp.where(low, 1 - z, 5 - z), jnp.where(low, 2, 1), jnp.where(low, 3, 0)]
        self.inner = (z == 1) | (z == 2)
        self.partner = place.device(z + 1 - 2 * lax.rem(z, 2), place.xc, place.y)
        self.across = place.device(3 - z, place.xc, place.y)
        self.sends, self.inner_sends, self.waited = [], [], set()

    def go(self, make):
        make().start()
        self.sends.append(make)

    def go_inner(self, make):
        pl.when(self.inner)(lambda: make().start())
        self.inner_sends.append(make)

    def copy(self, kind, k, i, j, src, dst, device):
        send, recv = self.sems[kind]
        return remote(src, dst, send.at[k, i], recv.at[k, j], device)

    def block(self, k, j=0, other_x=False, other_y=False):
        p = self.p
        return self.w.at[k, p.yo if other_y else p.y, self.order[j], 1 - p.x if other_x else p.x, p.c]

    def source(self, k, j):
        return self.packed.at[k] if j == 0 else self.block(k, j)

    def own(self, k):
        return pltpu.make_async_copy(self.packed.at[k], self.block(k), self.lsem.at[k])

    def load(self, k, j):
        return self.w.at[k, :, self.order[j], :, self.p.c] if k == self.turned else self.block(k, j)

    def line(self, k, i):
        j, slot, device = ((0, 1, self.partner), (0, 2, self.across), (1, 3, self.across), (2, 2, self.partner),
                           (3, 3, self.partner))[i]
        src = dst = self.load(k, j)
        if j == 0 and k != self.turned:
            src = self.packed.at[k]
        return self.copy("z", k, i, slot, src, dst, device)

    def line_start(self, k):
        self.go(lambda: self.line(k, 0))
        self.go_inner(lambda: self.line(k, 1))

    def line_wait(self, k, j):
        self.copy("z", k, 0, j, self.load(k, j), self.load(k, j), self.partner).wait_recv()
        self.go_inner(lambda: self.line(k, j + 1))

    def to_x(self, k, j):
        return self.copy("x", k, j, j, self.source(k, j), self.block(k, j), self.p.to_x)

    def to_y(self, k, j):
        return self.copy("y", k, j, j, self.source(k, j), self.block(k, j), self.p.to_y)

    def diagonal(self, k, j):
        x = self.via_x(k, j)
        block = self.block(k, j, other_x=not x, other_y=x)
        return self.copy("f", k, j, j, block, block, self.p.to_x if x else self.p.to_y)

    def to_core(self, k, i):
        p = self.p
        if k == self.turned:
            block = self.load(k, i)
        else:
            y, x = ((p.y, p.x), (p.y, 1 - p.x), (p.yo, p.x), (p.yo, 1 - p.x))[i]
            block = self.w.at[k, y, :, x, p.c]
        return self.copy("c", k, i, i, block, block, p.to_c)

    def start(self, k):
        self.own(k).start()
        self.line_start(k)
        self.go(lambda: self.to_x(k, 0))
        self.go(lambda: self.to_y(k, 0))

    def spread(self, k, j):
        self.go(lambda: self.to_x(k, j))
        self.go(lambda: self.to_y(k, j))
        if j == 3:
            self.own(k).wait()
            self.go(lambda: self.to_core(k, 0))

    def seen(self, kind, k, j):
        if (kind, k, j) not in self.waited:
            self.waited.add((kind, k, j))
            (self.to_x if kind == "x" else self.to_y)(k, j).wait_recv()

    def forward(self, k, j):
        self.seen("y" if self.via_x(k, j) else "x", k, j)
        self.go(lambda: self.diagonal(k, j))

    def side(self, k, kind):
        for j in range(4):
            self.seen(kind, k, j)
        self.go(lambda: self.to_core(k, 1 if kind == "x" else 2))

    def share(self, k):
        for j in range(4):
            self.diagonal(k, j).wait_recv()
        self.go(lambda: self.to_core(k, 3))

    def arrive(self, k):
        for i in range(4):
            self.to_core(k, i).wait_recv()

    def turned_copy(self, i):
        p, k = self.p, self.turned
        if i < 2:
            return self.copy("q", 0, i, i, self.packed.at[k], self.block(k), (p.to_x, p.to_y)[i])
        half = slice(UNITS // 2 * (i - 2), UNITS // 2 * (i - 1))
        block = self.block(k, other_x=i == 2, other_y=i == 3).at[:, half]
        return self.copy("q", 0, i, i, block, block, (p.to_y, p.to_x)[i - 2])

    def turned_start(self):
        self.own(self.turned).start()
        self.go(lambda: self.turned_copy(0))
        self.go(lambda: self.turned_copy(1))

    def turned_forward(self, i):
        self.turned_copy(i).wait_recv()
        self.go(lambda: self.turned_copy(2 + i))

    def turned_line(self, j):
        k = self.turned
        if j == 0:
            self.own(k).wait()
            self.turned_copy(2).wait_recv()
            self.turned_copy(3).wait_recv()
            self.line_start(k)
        else:
            self.line_wait(k, j)
        self.go(lambda: self.to_core(k, j))

    def finish(self):
        for make in self.sends:
            make().wait_send()
        for make in self.inner_sends:
            pl.when(self.inner)(lambda: make().wait_send())

    @staticmethod
    def scratch(n):
        dma = pltpu.SemaphoreType.DMA
        return [dma((n,)), dma((n, 5)), dma((n, 4))] + [dma((n, 4))] * 8 + [dma((1, 4))] * 2


def columns(w, y, cols):
    v = w[y, :, :, :, :, cols]
    return v.reshape(D, v.shape[-1])


def bounds(lengths, bucket, m):
    l0, l1, one = lengths[m, 0], lengths[m, 1], bucket[m] == 1
    half = S // 2
    return jnp.where(one, l0 + l1, l0), jnp.where(one, 0, half), jnp.where(one, l0 + l1, half + l1)


def key_bias(limits):
    first_end, second_start, second_end = limits
    k = lax.broadcasted_iota(jnp.int32, (S, 128), 0)
    lo = jnp.where(k < first_end, 0.0, -1e9)
    hi = jnp.where((k >= second_start) & (k < second_end), 0.0, -1e9)
    return lo, hi


def with_mask(q2, k2, half, bias):
    lane = lax.broadcasted_iota(jnp.int32, (S, 128), 1)
    low = lax.broadcasted_iota(jnp.int32, (S, 128), 0) < S // 2
    own = (lane // 64) == half
    o = 64 * (1 - half)
    one = lambda pick: jnp.where(pick, 1.0, 0.0)
    qa = jnp.where(lane == o, one(low), jnp.where(lane == o + 1, one(~low), 0.0))
    ka = jnp.where(lane == o, bias[0], jnp.where(lane == o + 1, bias[1], 0.0))
    qm = jnp.where(own, q2.astype(F32) * 0.125, qa).astype(BF16)
    km = jnp.where(own, k2.astype(F32), ka).astype(BF16)
    return qm, km


def head_pair(pair):
    y, r = pair // 3, lax.rem(pair, 3)
    return y, [at(o + 128 * r, 128) for o in (0, HALF, 2 * HALF)]


def attend(qkv, ctx, lse, limits, pair):
    y, (qc, kc, vc) = head_pair(pair)
    q2, k2, v2 = qkv[y, :, qc], qkv[y, :, kc], qkv[y, :, vc]
    bias = key_bias(limits)
    v2t = v2.T
    parts = []
    for half in range(2):
        qm, km = with_mask(q2, k2, half, bias)
        st = dot(km, qm, NT)
        top = jnp.max(st, axis=0, keepdims=True)
        e = jnp.exp(st - top)
        total = jnp.sum(e, axis=0, keepdims=True)
        lse[pair * 2 + half] = top + jnp.log(total)
        ct = dot(v2t[64 * half:64 * half + 64], e.astype(BF16))
        parts.append(ct * (1.0 / total))
    ctx[y, :, qc] = jnp.concatenate(parts, 0).T.astype(BF16)


def normalize(h, rows, gain, shift, n, r):
    v = h[rows, :]
    c = v - jnp.mean(v, axis=-1, keepdims=True)
    inverse = lax.rsqrt(jnp.mean(c * c, axis=-1, keepdims=True) + EPS)
    normed = c * inverse
    n[rows, :] = normed
    r[rows, :] = jnp.broadcast_to(inverse, (inverse.shape[0], 128))
    return normed * gain + shift


def gelu_parts(u):
    cdf = 0.5 * (1.0 + lax.erf(u * 0.7071067811865476))
    return u * cdf, cdf + u * (jnp.exp(-0.5 * u * u) * 0.3989422804014327)


PLAN = (
    ("TS",), ("S", 0), ("S", 4), ("TF", 0), ("L", 0, 1), ("S", 2), ("L", 4, 1), ("L", 2, 1), ("S", 1), ("L", 0, 2),
    ("XY", 0, 1), ("XY", 0, 2), ("L", 2, 2), ("L", 0, 3), ("XY", 0, 3), ("F", 0, 0), ("L", 1, 1), ("L", 1, 2), ("S", 5),
    ("L", 2, 3), ("XY", 2, 2), ("CY", 0), ("F", 0, 1), ("F", 0, 2), ("L", 1, 3), ("F", 0, 3), ("TF", 1), ("L", 4, 2),
    ("CX", 0), ("SX",), ("L", 5, 1), ("L", 5, 2), ("XY", 1, 3), ("XY", 1, 1), ("XY", 1, 2), ("SH", 0), ("F", 2, 2),
    ("TL", 0), ("F", 1, 3), ("AR", 0), ("F", 1, 0), ("XY", 2, 1), ("CX", 1), ("XY", 2, 3), ("L", 4, 3), ("F", 1, 1),
    ("CY", 1), ("F", 1, 2), ("XY", 4, 3), ("L", 5, 3), ("F", 2, 3), ("SH", 1), ("F", 2, 0), ("TL", 1), ("CX", 2),
    ("TL", 2), ("F", 2, 1), ("XY", 4, 1), ("AR", 1), ("F", 4, 0), ("CY", 2), ("XY", 4, 2), ("SH", 2), ("XY", 5, 2),
    ("XY", 5, 1), ("XY", 5, 3), ("F", 4, 1), ("TL", 3), ("CY", 4), ("F", 4, 2), ("AR", 2), ("CX", 4), ("F", 5, 2),
    ("F", 5, 1), ("AR", 3), ("CX", 5), ("F", 5, 0), ("F", 4, 3), ("CY", 5), ("F", 5, 3), ("SH", 4), ("SC",), ("SH", 5),
    ("AR", 4), ("AR", 5),
)
TURNED = 3
VIA_X = ((1, 0, 0, 1), (0, 1, 1, 0), (1, 1, 1, 0), (0, 1, 0, 1), (0, 0, 1, 0), (1, 1, 1, 0))


def forward_kernel(fold, layers, packed, xin, cot, vec, glob, lengths, bucket,
                   w, cotf, out, xr_o, qkv_o, lse_o, ctx_o, n1_o, r1_o, y1r_o, act_o, dg_o, n2_o, r2_o,
                   wv, xh, vecf, x, xr, qkv, lse, ctx, h, n1, r1, y1, y1r, act, dg, n2, r2,
                   wsem, esem, ssem, *gsems):
    p = Place(fold)
    m = p.y
    parts = 3 * layers
    assert parts == len(VIA_X)
    g = Gather(p, packed, w, TURNED, lambda k, j: VIA_X[k][j], *gsems)
    saves = {}
    names = ("xr", "qkv", "lse", "ctx", "n1", "r1", "y1r", "act", "dg", "n2", "r2")

    def load(k):
        return pltpu.make_async_copy(w.at[k], wv.at[k], wsem.at[k])

    def save(i, l, src, dst):
        if i in saves:
            saves.pop(i).wait()
        saves[i] = pltpu.make_async_copy(src, dst.at[l], ssem.at[names.index(i), l])
        saves[i].start()

    def before(*names):
        for i in names:
            if i in saves:
                saves.pop(i).wait()

    own_x = pltpu.make_async_copy(xin.at[m], xh.at[m], esem.at[0])
    swap_x = remote(xin.at[1 - m], xh.at[m], esem.at[1], esem.at[2], p.to_y)
    own_c = pltpu.make_async_copy(cot.at[m], cotf.at[m], esem.at[3])
    swap_c = remote(cot.at[1 - m], cotf.at[m], esem.at[4], esem.at[5], p.to_y)
    own_v = pltpu.make_async_copy(vec, vecf.at[m], esem.at[6])
    swap_v = remote(vec, vecf.at[m], esem.at[7], esem.at[8], p.to_y)
    limits = bounds(lengths, bucket, m)

    def row(i):
        return glob[i:i + 1, :]

    def stage_a(l, y):
        wa = wv.at[3 * l]
        if y == 0:
            before("xr", "qkv", "lse", "ctx", "n1", "r1", "y1r")
            save("xr", l, xr, xr_o)
        for t in range(3):
            cols = slice(HALF * t, HALF * t + HALF)
            v = dot(xr[...], columns(wa, y, cols))
            if t != 1:
                v = v + vecf[y, 2 + l:3 + l, HALF * (t // 2):HALF * (t // 2) + HALF]
            qkv[y, :, cols] = v.astype(BF16)
        if y == 1:
            save("qkv", l, qkv, qkv_o)

    def stage_out(l):
        wa = wv.at[3 * l]
        save("lse", l, lse, lse_o)
        save("ctx", l, ctx, ctx_o)
        wo = [columns(wa, y, slice(3 * HALF, 4 * HALF)) for y in range(2)]
        h[...] = x[...] + row(6 * l) + dot(ctx[0], wo[0], NT) + dot(ctx[1], wo[1], NT)

        @pl.loop(0, 2)
        def _(i):
            rows = at(256 * i, 256)
            o = normalize(h, rows, row(6 * l + 2), row(6 * l + 4), n1, r1)
            y1[rows, :] = o
            y1r[rows, :] = o.astype(BF16)
        save("n1", l, n1, n1_o)
        save("r1", l, r1, r1_o)
        save("y1r", l, y1r, y1r_o)

    def stage_b(l, y, i):
        wb = wv.at[3 * l + 1]
        if y == 0 and i == 0:
            before("act", "dg", "n2", "r2")
        cols = slice(768 * i, 768 * i + 768)
        u = dot(y1r[...], columns(wb, y, cols)) + vecf[y, l:l + 1, cols]
        a, d = gelu_parts(u)
        act[y, :, cols] = a.astype(BF16)
        dg[y, :, cols] = d.astype(BF16)
        if y == 1 and i == 1:
            save("act", l, act, act_o)
            save("dg", l, dg, dg_o)

    def stage_c(l):
        wc = wv.at[3 * l + 2]
        before("xr")
        full = slice(0, UNITS)
        h[...] = (y1[...] + row(6 * l + 1) + dot(act[0], columns(wc, 0, full), NT)
                  + dot(act[1], columns(wc, 1, full), NT))

        @pl.loop(0, 2)
        def _(i):
            rows = at(256 * i, 256)
            o = normalize(h, rows, row(6 * l + 3), row(6 * l + 5), n2, r2)
            x[rows, :] = o
            xr[rows, :] = o.astype(BF16)
        save("n2", l, n2, n2_o)
        save("r2", l, r2, r2_o)

    pending, here, used = [], set(), [0]

    def ready(k):
        l, kind = k // 3, k % 3
        pending.append(lambda: load(k).wait())
        if k == 0:
            pending.append(first)
        if kind == 0:
            pending.append(lambda: stage_a(l, 0))
            pending.append(lambda: stage_a(l, 1))
            pending.append((6, lambda j: attend(qkv, ctx, lse, limits, j)))
            pending.append(lambda: stage_out(l))
        elif kind == 1:
            for y in range(2):
                for i in range(2):
                    pending.append(lambda y=y, i=i: stage_b(l, y, i))
        else:
            pending.append(lambda: stage_c(l))

    def first():
        own_x.wait()
        swap_x.wait()
        own_v.wait()
        swap_v.wait()
        for i in range(2):
            rows = slice(256 * i, 256 * i + 256)
            xr[rows, :] = xh[i]
            x[rows, :] = xh[i].astype(F32)

    def run(steps):
        steps = list(steps)
        while steps or pending:
            piece = pending.pop(0) if pending else None
            if isinstance(piece, tuple):
                inside, steps = steps[:piece[0]], steps[piece[0]:]

                @pl.loop(0, piece[0])
                def _(j):
                    piece[1](j)
                    for i, step in enumerate(inside):
                        pl.when(j == i)(step)
            else:
                if piece is not None:
                    piece()
                if steps:
                    steps.pop(0)()

    def arrived(k):
        g.arrive(k)
        load(k).start()
        here.add(k)
        while used[0] in here:
            ready(used[0])
            used[0] += 1

    steps = {
        "S": g.start, "L": g.line_wait, "XY": g.spread, "F": g.forward, "CX": lambda k: g.side(k, "x"),
        "CY": lambda k: g.side(k, "y"), "SH": g.share, "AR": arrived, "TS": g.turned_start, "TF": g.turned_forward,
        "TL": g.turned_line, "SX": lambda: (swap_v.start(), swap_x.start()), "SC": lambda: swap_c.start()}
    plan = [lambda t=t: steps[t[0]](*t[1:]) for t in PLAN]

    own_x.start()
    own_v.start()
    own_c.start()
    p.greet()
    run(plan)
    own_c.wait()
    swap_c.wait()
    last = pltpu.make_async_copy(xr, out, esem.at[9])
    last.start()
    g.finish()
    for copy in saves.values():
        copy.wait()
    last.wait()


def forward(packed, xin, cot, vec, glob, lengths, bucket, layers, fold):
    n = 3 * layers
    dma = pltpu.SemaphoreType.DMA
    saved = [((S, D), BF16), ((2, S, 3 * HALF), BF16), ((12, 1, S), F32), ((2, S, HALF), BF16), ((S, D), F32), ((S, 128), F32),
             ((S, D), BF16), ((2, S, UNITS), BF16), ((2, S, UNITS), BF16), ((S, D), F32), ((S, 128), F32)]
    shape = jax.ShapeDtypeStruct
    vm = pltpu.VMEM
    return pl.pallas_call(
        functools.partial(forward_kernel, fold, layers),
        out_shape=[shape((n, 2, 4, 2, 2, 48, UNITS), BF16), shape((2, S // 2, D), BF16), shape((S, D), BF16)]
        + [shape((layers, *s), d) for s, d in saved],
        in_specs=[ANY, ANY, ANY, ANY, VMEM, SMEM, SMEM],
        out_specs=[ANY] * (3 + len(saved)),
        scratch_shapes=[
            vm((n, 2, 4, 2, 2, 48, UNITS), BF16), vm((2, S // 2, D), BF16), vm((2, 8, UNITS), F32), vm((S, D), F32),
            vm((S, D), BF16), vm((2, S, 3 * HALF), BF16), vm((12, 1, S), F32), vm((2, S, HALF), BF16),
            vm((S, D), F32), vm((S, D), F32), vm((S, 128), F32), vm((S, D), F32), vm((S, D), BF16),
            vm((2, S, UNITS), BF16), vm((2, S, UNITS), BF16), vm((S, D), F32), vm((S, 128), F32),
            dma((n,)), dma((10,)), dma((11, layers)), *Gather.scratch(n)],
        compiler_params=pltpu.CompilerParams(collective_id=1, has_side_effects=True, vmem_limit_bytes=60 * 2**20),
    )(packed, xin, cot, vec, glob, lengths, bucket)


class Reduce:
    def __init__(self, place, total, slots, split, held, out, rc, rx, ry, rx2, ry2, rz, cs, cr, xs, xr, ys, yr, zs, zr, free):
        self.p, self.total, self.slots, self.split = place, total, slots, split
        self.held, self.out, self.buffers = held, out, (rc, rx, ry, rx2, ry2, rz)
        self.sems = (cs, cr, xs, xr, ys, yr, zs, zr)
        self.free = free
        self.sends = {}

    def slot(self, u):
        for args in self.sends.pop(u - self.slots, ()):
            self.copy(u - self.slots, *args).wait_send()
        return self.held.at[u % self.slots]

    def go(self, u, *args):
        self.copy(u, *args).start()
        self.sends.setdefault(u, []).append(args)

    def got(self, u, *args):
        self.copy(u, *args).wait_recv()

    def copy(self, u, kind, j=0):
        p, s, n = self.p, u % self.slots, self.split[u]
        h = self.held.at[s]
        rc, rx, ry, rx2, ry2, rz = self.buffers
        cs, cr, xs, xr, ys, yr, zs, zr = self.sems
        if kind == "c":
            return remote(h.at[:, :, :, 1 - p.c], rc.at[s], cs.at[s], cr.at[s], p.to_c)
        if kind == "x1":
            return remote(h.at[:, 0:n, 1 - p.x, p.c], rx.at[s, :, 0:n], xs.at[s, 0], xr.at[s, 0], p.to_x)
        if kind == "y1":
            return remote(h.at[p.yo, n:4, :, p.c], ry.at[s, 0:4 - n], ys.at[s, 0], yr.at[s, 0], p.to_y)
        if kind == "y2":
            return remote(h.at[p.yo, 0:n, p.x, p.c], ry2.at[s, 0:n], ys.at[s, 1], yr.at[s, 1], p.to_y)
        if kind == "x2":
            return remote(h.at[p.y, n:4, 1 - p.x, p.c], rx2.at[s, 0:4 - n], xs.at[s, 1], xr.at[s, 1], p.to_x)
        to = lax.rem(p.z + j, 4)
        return remote(h.at[p.y, to, p.x, p.c], rz.at[s, j - 1], zs.at[s, j - 1], zr.at[s, j - 1], p.to_z[j])

    def submit(self, u):
        if u >= self.slots:
            for i in range(6):
                pl.semaphore_wait(self.free.at[i], 1)
        self.go(u, "c")

    def cores(self, u):
        p, h, rc = self.p, self.held.at[u % self.slots], self.buffers[0].at[u % self.slots]
        self.got(u, "c")

        @pl.loop(0, 4)
        def _(z):
            for y in range(2):
                for x in range(2):
                    h[y, z, x, p.c] = h[y, z, x, p.c] + rc[y, z, x]
        self.go(u, "x1")
        self.go(u, "y1")

    def after_x(self, u):
        p, h, rx, n = self.p, self.held.at[u % self.slots], self.buffers[1].at[u % self.slots], self.split[u]
        self.got(u, "x1")
        for y in range(2):
            for z in range(n):
                h[y, z, p.x, p.c] = h[y, z, p.x, p.c] + rx[y, z]
        self.go(u, "y2")

    def after_y(self, u):
        p, h, ry, n = self.p, self.held.at[u % self.slots], self.buffers[2].at[u % self.slots], self.split[u]
        self.got(u, "y1")
        for z in range(n, 4):
            for x in range(2):
                h[p.y, z, x, p.c] = h[p.y, z, x, p.c] + ry[z - n, x]
        self.go(u, "x2")

    def plane(self, u):
        p, h, n = self.p, self.held.at[u % self.slots], self.split[u]
        _, _, _, rx2, ry2, _ = (b.at[u % self.slots] for b in self.buffers)
        self.got(u, "x2")
        self.got(u, "y2")
        for z in range(4):
            h[p.y, z, p.x, p.c] = h[p.y, z, p.x, p.c] + (ry2[z] if z < n else rx2[z - n])
        for j in (1, 2, 3):
            self.go(u, "z", j)

    def line(self, u):
        p, h, rz = self.p, self.held.at[u % self.slots], self.buffers[5].at[u % self.slots]
        for j in (1, 2, 3):
            self.got(u, "z", j)
        f = lambda v: v.astype(F32)
        self.out[u] = f(h[p.y, p.z, p.x, p.c]) + f(rz[0]) + f(rz[1]) + f(rz[2])
        if u + self.slots < self.total:
            for i, device in zip((0, 1, 2, 5, 4, 3), (p.to_c, p.to_x, p.to_y, *p.to_z[1:])):
                pl.semaphore_signal(self.free.at[i], inc=1, device_id=device, device_id_type=MESH)

    def finish(self):
        for u, sent in self.sends.items():
            for args in sent:
                self.copy(u, *args).wait_send()

    @staticmethod
    def scratch(n, part):
        dma = pltpu.SemaphoreType.DMA
        v = lambda *s: pltpu.VMEM((n, *s, 48, part), BF16)
        return [v(2, 4, 2, 2)], [v(2, 4, 2), v(2, 3), v(2, 2), v(2), v(3), v(3), dma((n,)), dma((n,))] + [dma((n, 2))] * 4 + [
            dma((n, 3))] * 2 + [pltpu.SemaphoreType.REGULAR((6,))]


class Total:
    def __init__(self, place, v, got, zall, sems):
        self.p, self.v, self.got, self.zall = place, v, got, zall
        self.send, self.recv = sems
        self.last = []

    def copy(self, i):
        p = self.p
        if i < 3:
            return remote(self.v.at[i], self.got.at[i], self.send.at[i], self.recv.at[i], (p.to_c, p.to_x, p.to_y)[i])
        return remote(self.v.at[3], self.zall.at[p.z], self.send.at[i], self.recv.at[i], p.to_z[i - 2])

    def step(self, i, out=None):
        if 1 <= i <= 3:
            self.copy(i - 1).wait_recv()
            self.v[i] = self.v[i - 1] + self.got[i - 1]
        if i < 3:
            self.copy(i).start()
        elif i == 3:
            for j in (3, 4, 5):
                self.copy(j).start()
            self.zall[self.p.z] = self.v[3]
        else:
            for j in (3, 4, 5):
                self.copy(j).wait_recv()
            z = self.zall
            out[...] = (z[0] + z[1]) + (z[2] + z[3])
            for j in range(6):
                self.copy(j).wait_send()

    @staticmethod
    def scratch(rows):
        dma = pltpu.SemaphoreType.DMA
        v = lambda n: pltpu.VMEM((n, rows, D), F32)
        return [v(4), v(3), v(4), dma((6,)), dma((6,))]


def attend_back(qkv, lse, gc, gqkv, sums, limits, pair):
    y, (qc, kc, vc) = head_pair(pair)
    q2, k2, v2, c2 = qkv[y, :, qc], qkv[y, :, kc], qkv[y, :, vc], gc[y, :, qc]
    bias = key_bias(limits)
    lane = lax.broadcasted_iota(jnp.int32, (S, 128), 1)
    k2t = k2.T
    gq, gk, gv = [], [], []
    for half in range(2):
        qm, km = with_mask(q2, k2, half, bias)
        st = dot(km, qm, NT)
        probs = jnp.exp(st - lse[pair * 2 + half])
        vm = jnp.where((lane // 64) == half, v2, jnp.zeros_like(v2))
        gp = dot(vm, c2, NT)
        prod = probs * gp
        total = jnp.sum(prod, axis=0, keepdims=True)
        gs = (prod - probs * total).astype(BF16)
        gv.append(dot(probs.astype(BF16), c2))
        gk.append(dot(gs, q2))
        gq.append(dot(k2t[64 * half:64 * half + 64], gs))
    pick = lambda v: jnp.where(lane < 64, v[0], v[1])
    gqt = jnp.concatenate(gq, 0).T * 0.125
    gkt = pick(gk) * 0.125
    gvt = pick(gv)
    gqkv[y, :, qc] = gqt.astype(BF16)
    gqkv[y, :, kc] = gkt.astype(BF16)
    gqkv[y, :, vc] = gvt.astype(BF16)
    sums[y, 0, :, qc] = jnp.sum(gqt, axis=0, keepdims=True)
    sums[y, 1, :, qc] = jnp.sum(gvt, axis=0, keepdims=True)


def norm_back(g, rows, gain, n, r):
    v = g[rows, :]
    normed, inverse = n[rows, :], r[rows, 0:1]
    e = v * gain
    gh = inverse * (e - jnp.mean(e, axis=-1, keepdims=True) - normed * jnp.mean(e * normed, axis=-1, keepdims=True))
    add = lambda t: jnp.sum(t, axis=0, keepdims=True)
    return gh, add(v * normed), add(v), add(gh)


BACKWARD = (
    ("SO",), ("n2", 0), ("t", 0), ("SUB", 0), ("t", 1), ("ST1", 0), ("g", 0, 0), ("SUB", 1), ("t", 2), ("ST1", 1),
    ("g", 0, 1), ("SUB", 2), ("t", 3), ("ST1", 2), ("gy", 0), ("ST2Y", 0), ("n1", 0), ("ST2X", 0), ("to", 4),
    ("SUB", 3), ("ST2Y", 1), ("gc", 0), ("ST1", 3), ("a", 0, 0), ("a", 0, 1), ("a", 0, 2), ("ST3", 0), ("a", 0, 3),
    ("ST2X", 1), ("a", 0, 4), ("ST2X", 2), ("ST2Y", 2), ("a", 0, 5), ("ST4", 0), ("tv", 4), ("ST3", 1), ("SUB", 4),
    ("ST2X", 3), ("ST2Y", 3), ("t", 5), ("ST3", 2), ("SUB", 5), ("ST1", 4), ("ST1", 5), ("gx", 0), ("n2", 1),
    ("ST4", 1), ("ST2Y", 4), ("t", 6), ("ST3", 3), ("ST2X", 4), ("ST4", 2), ("t", 7), ("SUB", 7), ("ST2X", 5),
    ("ST2Y", 5), ("g", 1, 0), ("ST1", 7), ("ST3", 4), ("ST4", 3), ("SUB", 6), ("ST1", 6), ("t", 8), ("SUB", 8),
    ("g", 1, 1), ("ST3", 5), ("ST4", 4), ("t", 9), ("ST2Y", 7), ("ST2X", 7), ("gy", 1), ("n1", 1), ("ST2Y", 6),
    ("ST4", 5), ("ST2X", 6), ("E", 0), ("SUB", 9), ("to", 10), ("E", 1), ("gc", 1), ("ST1", 8), ("ST3", 7), ("a", 1, 0),
    ("a", 1, 1), ("ST3", 6), ("E", 2), ("ST1", 9), ("a", 1, 2), ("a", 1, 3), ("E", 3), ("ST2Y", 8), ("a", 1, 4),
    ("ST2X", 8), ("a", 1, 5), ("tv", 10), ("V", 0), ("ST2X", 9), ("V", 1), ("ST4", 6), ("SUB", 10), ("ST2Y", 9),
    ("V", 2), ("ST3", 8), ("ST1", 10), ("t", 11), ("V", 3), ("SUB", 11), ("gx", 1), ("ST1", 11), ("ST2Y", 10),
    ("ST3", 9), ("ST2X", 10), ("ST2X", 11), ("ST3", 10), ("E", 4), ("ST2Y", 11), ("ST4", 9), ("ST3", 11), ("ST4", 8),
    ("ST4", 7), ("ST4", 10), ("V", 4), ("ST4", 11),
)
SPLIT = (3, 2, 2, 2, 2, 2, 2, 2, 2, 2, 2, 2)
SLOTS = 5
PART = UNITS // 2
ROWS = 24


def backward_kernel(fold, layers, w, cotf, outx, glob, lengths, bucket,
                    xr_o, qkv_o, lse_o, ctx_o, n1_o, r1_o, y1r_o, act_o, dg_o, n2_o, r2_o,
                    output, ingrad, shards, vout, vlate,
                    wv, g, gh, n, r, low, act, dg, y1r, ctx, qkv, lse, xr, gc, gqkv, sums,
                    wsem, lsem, esem, *rest):
    p = Place(fold)
    m = p.y
    red = Reduce(p, 6 * layers, SLOTS, SPLIT, rest[0], shards, *rest[1:16])
    early = Total(p, *rest[16:19], rest[19:21])
    late = Total(p, *rest[21:24], rest[24:26])
    limits = bounds(lengths, bucket, m)
    order = [3 * l + t for l in reversed(range(layers)) for t in (2, 1, 0)]
    full = slice(0, UNITS)

    def row(i):
        return glob[i:i + 1, :]

    def weights(i):
        return pltpu.make_async_copy(w.at[order[i]], wv.at[i % 2], wsem.at[i % 2])

    table = {"n2": (n2_o, n), "r2": (r2_o, r), "act": (act_o, act), "dg": (dg_o, dg), "y1r": (y1r_o, y1r),
             "n1": (n1_o, n), "r1": (r1_o, r), "ctx": (ctx_o, ctx), "qkv": (qkv_o, qkv), "lse": (lse_o, lse),
             "xr": (xr_o, xr)}
    loads = {}

    def begin(l, *names):
        for i in names:
            src, dst = table[i]
            loads[i] = pltpu.make_async_copy(src.at[l], dst, lsem.at[list(table).index(i)])
            loads[i].start()

    def need(*names):
        for i in names:
            loads.pop(i).wait()

    def add(line, value):
        early.v[0, line:line + 1, :] = early.v[0, line:line + 1, :] + value

    def norm_stage(l, which):
        base = 12 * (layers - 1 - l)

        @pl.loop(0, 4)
        def _(i):
            rows = at(128 * i, 128)
            v, a, b, c = norm_back(g, rows, row(6 * l + 2 + which), n, r)
            gh[rows, :] = v
            low[rows, :] = v.astype(BF16)
            add(base + which, a)
            add(base + 2 + which, b)
            add(base + 4 + which, c)

    def tiles(u, left, right, start, width, to):
        s = red.slot(u)
        for y in range(2):
            v = dot(left[...], right[y, :, start:start + width], TN).astype(BF16)
            s[y, :, :, :, :, to:to + width] = v.reshape(4, 2, 2, 48, width)

    def norm_two(i):
        l = layers - 1 - i
        need("n2", "r2")
        norm_stage(l, 1)
        begin(l, "n1", "r1")

    def gradient(u):
        l, kind = layers - 1 - u // 6, u % 6
        if kind < 2:
            if kind == 0:
                need("act")
            tiles(u, low, act, PART * kind, PART, 0)
            if kind == 1 and l:
                begin(l - 1, "act")
        elif kind < 4:
            if kind == 2:
                need("y1r")
            tiles(u, y1r, dg, PART * (kind - 2), PART, 0)
        else:
            tiles(u, xr, gqkv, 0, 2 * HALF, 0)

    def gradient_out(u):
        need("ctx")
        tiles(u, low, ctx, 0, HALF, HALF)

    def gradient_value(u):
        need("xr")
        tiles(u, xr, gqkv, 2 * HALF, HALF, 0)

    def units(i, half):
        if half == 0:
            weights(3 * i).wait()
            need("dg")
        wc = wv.at[3 * i % 2]
        for y in range(2):
            cols = slice(PART * half, PART * half + PART)
            gi = dot(low[...], columns(wc, y, cols)) * dg[y, :, cols].astype(F32)
            dg[y, :, cols] = gi.astype(BF16)
            line = 12 * i + 6 + 2 * y + half
            early.v[0, line:line + 1, :] = jnp.sum(gi, axis=0, keepdims=True)
        if half == 1 and 3 * i + 2 < 3 * layers:
            weights(3 * i + 2).start()

    def hidden(i):
        weights(3 * i + 1).wait()
        wb = wv.at[(3 * i + 1) % 2]
        g[...] = gh[...] + dot(dg[0], columns(wb, 0, full), NT) + dot(dg[1], columns(wb, 1, full), NT)
        if 3 * i + 3 < 3 * layers:
            weights(3 * i + 3).start()
        l = layers - 1 - i
        if l:
            begin(l - 1, "dg", "y1r")

    def norm_one(i):
        l = layers - 1 - i
        need("n1", "r1")
        norm_stage(l, 0)
        if l:
            begin(l - 1, "n2", "r2")

    def context(i):
        l = layers - 1 - i
        weights(3 * i + 2).wait()
        wa = wv.at[(3 * i + 2) % 2]
        for y in range(2):
            gc[y] = dot(low[...], columns(wa, y, slice(3 * HALF, 4 * HALF))).astype(BF16)
        if l:
            begin(l - 1, "ctx")
        need("qkv", "lse")

    def attention(i, inside):
        @pl.loop(0, 6)
        def _(j):
            attend_back(qkv, lse, gc, gqkv, sums, limits, j)
            for turn, todo in enumerate(inside):
                if todo:
                    @pl.when(j == turn)
                    def _():
                        for t in todo:
                            steps[t[0]](*t[1:])
        for y in range(2):
            for t in range(2):
                where = slice(HALF * y, HALF * y + HALF)
                if i == layers - 1:
                    late.v[0, t:t + 1, where] = sums[y, t]
                else:
                    early.v[0, 12 * i + 10 + t:12 * i + 11 + t, where] = sums[y, t]

    def state(i):
        l = layers - 1 - i
        wa = wv.at[(3 * i + 2) % 2]
        wqkv = [columns(wa, y, slice(0, 3 * HALF)) for y in range(2)]
        if l:
            g[...] = gh[...] + dot(gqkv[0], wqkv[0], NT) + dot(gqkv[1], wqkv[1], NT)
            begin(l - 1, "qkv", "lse", "xr")
            weights(3 * i + 4).start()
        else:
            for j in range(2):
                rows = at((S // 2) * (1 - m if j == 0 else m), S // 2)
                v = gh[rows, :] + dot(gqkv[0, rows, :], wqkv[0], NT) + dot(gqkv[1, rows, :], wqkv[1], NT)
                low[rows, :] = v.astype(BF16)
                (swap_g if j == 0 else own_g).start()

    steps = {
        "n2": norm_two, "t": gradient, "to": gradient_out, "tv": gradient_value, "g": units, "gy": hidden, "n1": norm_one,
        "gc": context, "gx": state, "SUB": red.submit, "ST1": red.cores, "ST2X": red.after_x, "ST2Y": red.after_y,
        "ST3": red.plane, "ST4": red.line, "E": lambda i: early.step(i, vout), "V": lambda i: late.step(i, vlate),
        "SO": lambda: swap_o.start()}
    own_o = pltpu.make_async_copy(outx.at[m], output.at[m], esem.at[0])
    swap_o = remote(outx.at[1 - m], output.at[m], esem.at[1], esem.at[2], p.to_y)
    half = lambda i: low.at[at((S // 2) * i, S // 2), :]
    own_g = pltpu.make_async_copy(half(m), ingrad.at[m], esem.at[3])
    swap_g = remote(half(1 - m), ingrad.at[m], esem.at[4], esem.at[5], p.to_y)
    top = layers - 1
    cload = pltpu.make_async_copy(cotf, low, esem.at[6])
    cload.start()
    begin(top, "n2", "r2", "act")
    weights(0).start()
    begin(top, "dg", "y1r")
    weights(1).start()
    begin(top, "ctx", "qkv", "lse", "xr")
    early.v[0] = jnp.zeros((ROWS, D), F32)
    late.v[0] = jnp.zeros((8, D), F32)
    cload.wait()
    g[...] = low[...].astype(F32)
    own_o.start()
    p.greet()
    plan = list(BACKWARD)
    while plan:
        t = plan.pop(0)
        if t[0] != "a":
            steps[t[0]](*t[1:])
            continue
        inside = [[] for _ in range(6)]
        while (t[0], t[-1]) != ("a", 5):
            if t[0] == "a":
                turn = t[2]
            else:
                inside[turn].append(t)
            t = plan.pop(0)
        attention(t[1], inside)
    red.finish()
    own_o.wait()
    swap_o.wait()
    own_g.wait()
    swap_g.wait()


def backward(w, cotf, outx, glob, lengths, bucket, saved, layers, fold):
    n = 6 * layers
    dma = pltpu.SemaphoreType.DMA
    shape = jax.ShapeDtypeStruct
    vm = pltpu.VMEM
    first, rest = Reduce.scratch(SLOTS, PART)
    return pl.pallas_call(
        functools.partial(backward_kernel, fold, layers),
        out_shape=[shape((2, S // 2, D), BF16), shape((2, S // 2, D), BF16), shape((n, 48, PART), F32),
                   shape((ROWS, D), F32), shape((8, D), F32)],
        in_specs=[ANY, ANY, ANY, VMEM, SMEM, SMEM] + [ANY] * 11,
        out_specs=[ANY, ANY, VMEM, VMEM, VMEM],
        scratch_shapes=[
            vm((2, 2, 4, 2, 2, 48, UNITS), BF16), vm((S, D), F32), vm((S, D), F32), vm((S, D), F32), vm((S, 128), F32),
            vm((S, D), BF16), vm((2, S, UNITS), BF16), vm((2, S, UNITS), BF16), vm((S, D), BF16),
            vm((2, S, HALF), BF16), vm((2, S, 3 * HALF), BF16), vm((12, 1, S), F32), vm((S, D), BF16), vm((2, S, HALF), BF16),
            vm((2, S, 3 * HALF), BF16), vm((2, 2, 1, HALF), F32),
            dma((2,)), dma((11,)), dma((7,)), *first, *rest, *Total.scratch(ROWS), *Total.scratch(8)],
        compiler_params=pltpu.CompilerParams(collective_id=2, has_side_effects=True, vmem_limit_bytes=62 * 2**20),
    )(w, cotf, outx, glob, lengths, bucket, *saved)


def pack(w_qkv, w_out, w_up, w_down):
    parts = []
    for l in range(w_qkv.shape[0]):
        parts.append(jnp.concatenate([w_qkv[l, 0], w_qkv[l, 1], w_qkv[l, 2], w_out[l].T], 1))
        parts.append(w_up[l])
        parts.append(w_down[l].T)
    return jnp.stack(parts)


def per_device(layer_input, cotangent, lengths, bucket, w_qkv, bias_qv, w_out, bias_out, ln_gain, ln_bias, w_up, bias_up, w_down):
    layers = w_qkv.shape[0]
    fold = lax.axis_size("dp") // GROUPS
    members = [[g * fold + i for i in range(fold)] for g in range(GROUPS)]
    packed = pack(w_qkv, w_out, w_up, w_down)
    if fold > 1:
        packed = lax.all_gather(packed, "dp", axis=1, tiled=True, axis_index_groups=members)
    qv = jnp.pad(bias_qv.reshape(layers, 2 * HALF), ((0, 0), (0, UNITS - 2 * HALF)))
    vec = jnp.concatenate([bias_up, qv], 0).astype(F32)
    vec = jnp.pad(vec, ((0, 8 - vec.shape[0]), (0, 0)))
    glob = jnp.concatenate([bias_out, ln_gain, ln_bias], 1).astype(F32).reshape(6 * layers, D)
    glob = jnp.pad(glob, ((0, 16 - 6 * layers), (0, 0)))
    w, cotf, out, *saved = forward(packed, layer_input, cotangent, vec, glob, lengths, bucket, layers, fold)
    output, ingrad, shards, early, late = backward(
        w, cotf.reshape(S, D), out.reshape(2, S // 2, D), glob, lengths, bucket, saved, layers, fold)
    if fold > 1:
        shards = lax.psum_scatter(shards, "dp", scatter_dimension=1, tiled=True, axis_index_groups=members)
        early, late = lax.psum((early, late), "dp", axis_index_groups=members)
    rows = shards.shape[1]
    part = lax.axis_index("mp")
    shards = jnp.flip(shards.reshape(layers, 6, rows, PART), 0)
    down, up, vo, qk = shards[:, 0:2], shards[:, 2:4], shards[:, 4], shards[:, 5]
    grad_qkv = jnp.stack([qk[..., :HALF], qk[..., HALF:], vo[..., :HALF]], 1)
    grad_out = vo[..., HALF:].transpose(0, 2, 1)
    grad_up = up.transpose(0, 2, 1, 3).reshape(layers, rows, UNITS)
    grad_down = down.transpose(0, 1, 3, 2).reshape(layers, UNITS, rows)
    vecs = jnp.flip(early.reshape(layers, 12, D), 0)
    gain, shift, bias = vecs[:, 0:2], vecs[:, 2:4], vecs[:, 4:6]
    grad_bias_up = lax.dynamic_slice_in_dim(vecs[:, 6:10].reshape(layers, 2, UNITS), part, 1, 1)[:, 0]
    qv = jnp.concatenate([late[None, 0:2], vecs[1:, 10:12]], 0)
    qv = lax.dynamic_slice_in_dim(qv, part * HALF, HALF, 2)
    return output, ingrad, grad_qkv, qv, grad_out, bias, gain, shift, grad_up, grad_bias_up, grad_down


def solution(mesh):
    in_specs = (
        P("dp", "mp", None),
        P("dp", "mp", None),
        P("dp", None),
        P("dp"),
        P(None, None, "dp", "mp"),
        P(None, None, "mp"),
        P(None, "mp", "dp"),
        P(),
        P(),
        P(),
        P(None, "dp", "mp"),
        P(None, "mp"),
        P(None, "mp", "dp"),
    )
    out_specs = (
        P("dp", "mp", None),
        P("dp", "mp", None),
        P(None, None, "dp", "mp"),
        P(None, None, "mp"),
        P(None, "mp", "dp"),
        P(),
        P(),
        P(),
        P(None, "dp", "mp"),
        P(None, "mp"),
        P(None, "mp", "dp"),
    )
    return jax.shard_map(
        per_device, mesh=mesh, in_specs=in_specs, out_specs=out_specs, check_vma=False
    )
```

time: 377 us -> 318 us (0.84)
  Pallas kernels: 352 us -> 293 us
    pallas_call x1, Pallas kernels: 171 us -> 139 us  [forward(): pl.pallas_call(functools.partial(forward_kernel, fold, layers), out_shape...]
    pallas_call x1, Pallas kernels: 181 us -> 154 us  [backward(): pl.pallas_call(functools.partial(backward_kernel, fold, layers), out_shap...]
where the time goes in v3:
time: 318 us; the launch traced here: 315 us
  Pallas kernels  293 us (92%)
  local copies, waits for them, and re-layouts  17 us (5%)
  other arithmetic  3.49 us (1%)
    pallas_call x1, Pallas kernels, backward(): pl.pallas_call(functools.partial(backward_kernel, fold, layers), out_shap...  154 us
    pallas_call x1, Pallas kernels, forward(): pl.pallas_call(functools.partial(forward_kernel, fold, layers), out_shape...  139 us
    unnamed x18, local copies, waits for them, and re-layouts  7.8 us

profile of v3, /device:TPU:0, one launch (start us, length us, event | category | flops | bytes accessed | tf_op | source)
XLA Modules:
  0.0 314.6 jit_solution(17616816263648837001)
XLA Ops:
  0.6 0.9 slice_bitcast_fusion.9
  1.5 0.8 slice_bitcast_fusion.6
  2.3 0.9 slice_dynamic-update-slice_fusion.1
  3.3 0.9 bitcast_dynamic-update-slice_fusion.1
  4.2 0.9 slice_dynamic-update-slice_fusion
  5.2 0.9 bitcast_dynamic-update-slice_fusion.packed
  6.1 0.0 copy-start
  6.1 0.9 pad_maximum_fusion.1
  7.0 0.6 pad_convert_fusion.glob
  7.6 0.7 copy.39
  8.3 0.7 fusion.3
  9.0 0.6 pad_convert_fusion.1.vec
  9.6 0.0 copy-done
  9.6 138.6 %shard_map.212 = (bf16[6,2,4,2,2,48,1536]{6,5,4,3,2,1,0:T(8,128)(2,1)}, bf16[2,256,768]{2,1,0:T(8,128)(2,1)}, bf16[512,768]{1,0:T(8,128)(2,1)}, bf16[2,512,768]{...) custom-call(bf16[6,48,1536]{2,1,0:T(8,128)(2,1)} %copy-done, ...), custom_call_target="tpu_custom_call" | custom-call | tf_op jit(solution)/shard_map/pallas_call | solution.py:486
  148.3 154.4 %shard_map.213 = (bf16[2,256,768]{2,1,0:T(8,128)(2,1)}, bf16[2,256,768]{2,1,0:T(8,128)(2,1)}, f32[12,48,768]{2,1,0:T(8,128)}, f32[24,768]{1,0:T(8,128)}, f32[8,768]{1,0:T(8,128)}) custom-call(bf16[6,2,4,2,2,48,1536]{6,5,4,3,2,1,0:T(8,128)(2,1)} %get-tuple-element.30.w, bf16[512,768]{1,0:T(8,128)(2,1)} %bitcast.76, bf16[2,256,768]{2,1,0:T(8,128)(2,1)} %bitcast.77, ...), custom_call_target="tpu_custom_call" | custom-call | tf_op jit(solution)/shard_map/pallas_call | solution.py:916
  302.7 0.0 copy-start.3
  302.7 1.4 fusion.5
  304.1 0.1 reverse_bitcast_fusion
  304.2 0.9 copy.37
  305.0 0.9 copy.38
  305.9 0.0 copy-done.3
  305.9 0.8 slice_bitcast_fusion.14
  306.7 0.6 fusion.4
  307.3 1.1 slice_bitcast_fusion.1
  308.5 0.7 slice_bitcast_fusion.2
  309.2 0.8 copy.33
  310.1 0.6 copy.41
  310.7 0.6 slice.126
  311.3 0.6 slice.128
  311.9 0.6 slice.130
  312.5 0.9 copy.49
  313.4 0.9 copy.50
  (17 shorter events, 0.2 us)
Async XLA Ops:
  6.1 3.6 %copy-start = (bf16[6,48,1536]{2,1,0:T(8,128)(2,1)}, bf16[6,48,1536]{2,1,0:T(8,128)(2,1)S(1)}, u32[]{:S(2)}) copy-start(bf16[6,48,1536]{2,1,0:T(8,128)(2,1)S(1)} %bitcast_dynamic-update-slice_fusion.packed) | copy-start | bytes 2654212
  302.7 3.2 %copy-start.3 = (f32[24,768]{1,0:T(8,128)S(1)}, f32[24,768]{1,0:T(8,128)}, u32[]{:S(2)}) copy-start(f32[24,768]{1,0:T(8,128)} %get-tuple-element.48) | copy-start | bytes 221188
  305.9 6.6 %copy-start.2 = (bf16[2,256,768]{2,1,0:T(8,128)(2,1)S(1)}, bf16[2,256,768]{2,1,0:T(8,128)(2,1)}, u32[]{:S(2)}) copy-start(bf16[2,256,768]{2,1,0:T(8,128)(2,1)} %get-tuple-element.105) | copy-start | bytes 2359300
  308.4 5.0 %copy-start.1 = (bf16[2,256,768]{2,1,0:T(8,128)(2,1)S(1)}, bf16[2,256,768]{2,1,0:T(8,128)(2,1)}, u32[]{:S(2)}) copy-start(bf16[2,256,768]{2,1,0:T(8,128)(2,1)} %get-tuple-element.106) | copy-start | bytes 2359300

commit v4 on v3

--- a/solution.py
+++ b/solution.py
@@ -61,10 +61,11 @@
         return {"dp": (z * 4 + xc) * self.fold + self.member, "mp": y}
 
     def greet(self):
-        barrier = pltpu.get_barrier_semaphore()
         for device in (*self.to_z[1:], self.to_x, self.to_y, self.to_c):
-            pl.semaphore_signal(barrier, inc=1, device_id=device, device_id_type=MESH)
-        pl.semaphore_wait(barrier, 6)
+            pl.semaphore_signal(pltpu.get_barrier_semaphore(), inc=1, device_id=device, device_id_type=MESH)
+
+    def greeted(self):
+        pl.semaphore_wait(pltpu.get_barrier_semaphore(), 6)
 
 
 class Gather:
@@ -288,19 +289,19 @@
 
 
 PLAN = (
-    ("TS",), ("S", 0), ("S", 4), ("TF", 0), ("L", 0, 1), ("S", 2), ("L", 4, 1), ("L", 2, 1), ("S", 1), ("L", 0, 2),
-    ("XY", 0, 1), ("XY", 0, 2), ("L", 2, 2), ("L", 0, 3), ("XY", 0, 3), ("F", 0, 0), ("L", 1, 1), ("L", 1, 2), ("S", 5),
-    ("L", 2, 3), ("XY", 2, 2), ("CY", 0), ("F", 0, 1), ("F", 0, 2), ("L", 1, 3), ("F", 0, 3), ("TF", 1), ("L", 4, 2),
-    ("CX", 0), ("SX",), ("L", 5, 1), ("L", 5, 2), ("XY", 1, 3), ("XY", 1, 1), ("XY", 1, 2), ("SH", 0), ("F", 2, 2),
-    ("TL", 0), ("F", 1, 3), ("AR", 0), ("F", 1, 0), ("XY", 2, 1), ("CX", 1), ("XY", 2, 3), ("L", 4, 3), ("F", 1, 1),
-    ("CY", 1), ("F", 1, 2), ("XY", 4, 3), ("L", 5, 3), ("F", 2, 3), ("SH", 1), ("F", 2, 0), ("TL", 1), ("CX", 2),
-    ("TL", 2), ("F", 2, 1), ("XY", 4, 1), ("AR", 1), ("F", 4, 0), ("CY", 2), ("XY", 4, 2), ("SH", 2), ("XY", 5, 2),
-    ("XY", 5, 1), ("XY", 5, 3), ("F", 4, 1), ("TL", 3), ("CY", 4), ("F", 4, 2), ("AR", 2), ("CX", 4), ("F", 5, 2),
-    ("F", 5, 1), ("AR", 3), ("CX", 5), ("F", 5, 0), ("F", 4, 3), ("CY", 5), ("F", 5, 3), ("SH", 4), ("SC",), ("SH", 5),
-    ("AR", 4), ("AR", 5),
+    ("S", 0), ("TS",), ("S", 1), ("S", 2), ("L", 0, 1), ("L", 1, 1), ("XY", 0, 1), ("L", 0, 2), ("L", 2, 1), ("S", 4),
+    ("TF", 0), ("L", 0, 3), ("TF", 1), ("XY", 0, 3), ("L", 1, 2), ("F", 0, 0), ("XY", 0, 2), ("XY", 1, 1), ("F", 0, 1),
+    ("L", 1, 3), ("TL", 0), ("F", 0, 3), ("F", 0, 2), ("XY", 1, 3), ("SX",), ("XY", 1, 2), ("S", 5), ("L", 4, 1),
+    ("L", 2, 2), ("XY", 2, 1), ("XY", 2, 2), ("F", 4, 0), ("SH", 0), ("CX", 0), ("CY", 0), ("F", 1, 0), ("TL", 1),
+    ("L", 2, 3), ("F", 1, 3), ("L", 5, 1), ("F", 1, 1), ("TL", 2), ("AR", 0), ("XY", 2, 3), ("XY", 5, 1), ("F", 1, 2),
+    ("CY", 1), ("F", 2, 0), ("CX", 1), ("F", 2, 1), ("TL", 3), ("XY", 4, 1), ("CX", 2), ("AR", 3), ("F", 2, 3),
+    ("L", 4, 2), ("SH", 1), ("L", 4, 3), ("F", 2, 2), ("XY", 4, 2), ("L", 5, 2), ("F", 4, 1), ("XY", 5, 2),
+    ("XY", 4, 3), ("AR", 1), ("CY", 2), ("SH", 2), ("AR", 2), ("L", 5, 3), ("F", 4, 2), ("XY", 5, 3), ("F", 4, 3),
+    ("F", 5, 0), ("CX", 4), ("CY", 4), ("CX", 5), ("F", 5, 2), ("F", 5, 1), ("SH", 4), ("F", 5, 3), ("AR", 4),
+    ("CY", 5), ("SC",), ("SH", 5), ("AR", 5),
 )
 TURNED = 3
-VIA_X = ((1, 0, 0, 1), (0, 1, 1, 0), (1, 1, 1, 0), (0, 1, 0, 1), (0, 0, 1, 0), (1, 1, 1, 0))
+VIA_X = ((1, 1, 1, 0), (1, 0, 1, 1), (0, 1, 1, 0), (0, 1, 1, 0), (0, 1, 0, 1), (1, 0, 0, 1))
 
 
 def forward_kernel(fold, layers, packed, xin, cot, vec, glob, lengths, bucket,
@@ -461,10 +462,11 @@
         "TL": g.turned_line, "SX": lambda: (swap_v.start(), swap_x.start()), "SC": lambda: swap_c.start()}
     plan = [lambda t=t: steps[t[0]](*t[1:]) for t in PLAN]
 
+    p.greet()
     own_x.start()
     own_v.start()
     own_c.start()
-    p.greet()
+    p.greeted()
     run(plan)
     own_c.wait()
     swap_c.wait()
@@ -681,20 +683,20 @@
 
 
 BACKWARD = (
-    ("SO",), ("n2", 0), ("t", 0), ("SUB", 0), ("t", 1), ("ST1", 0), ("g", 0, 0), ("SUB", 1), ("t", 2), ("ST1", 1),
-    ("g", 0, 1), ("SUB", 2), ("t", 3), ("ST1", 2), ("gy", 0), ("ST2Y", 0), ("n1", 0), ("ST2X", 0), ("to", 4),
-    ("SUB", 3), ("ST2Y", 1), ("gc", 0), ("ST1", 3), ("a", 0, 0), ("a", 0, 1), ("a", 0, 2), ("ST3", 0), ("a", 0, 3),
-    ("ST2X", 1), ("a", 0, 4), ("ST2X", 2), ("ST2Y", 2), ("a", 0, 5), ("ST4", 0), ("tv", 4), ("ST3", 1), ("SUB", 4),
-    ("ST2X", 3), ("ST2Y", 3), ("t", 5), ("ST3", 2), ("SUB", 5), ("ST1", 4), ("ST1", 5), ("gx", 0), ("n2", 1),
-    ("ST4", 1), ("ST2Y", 4), ("t", 6), ("ST3", 3), ("ST2X", 4), ("ST4", 2), ("t", 7), ("SUB", 7), ("ST2X", 5),
-    ("ST2Y", 5), ("g", 1, 0), ("ST1", 7), ("ST3", 4), ("ST4", 3), ("SUB", 6), ("ST1", 6), ("t", 8), ("SUB", 8),
-    ("g", 1, 1), ("ST3", 5), ("ST4", 4), ("t", 9), ("ST2Y", 7), ("ST2X", 7), ("gy", 1), ("n1", 1), ("ST2Y", 6),
-    ("ST4", 5), ("ST2X", 6), ("E", 0), ("SUB", 9), ("to", 10), ("E", 1), ("gc", 1), ("ST1", 8), ("ST3", 7), ("a", 1, 0),
-    ("a", 1, 1), ("ST3", 6), ("E", 2), ("ST1", 9), ("a", 1, 2), ("a", 1, 3), ("E", 3), ("ST2Y", 8), ("a", 1, 4),
-    ("ST2X", 8), ("a", 1, 5), ("tv", 10), ("V", 0), ("ST2X", 9), ("V", 1), ("ST4", 6), ("SUB", 10), ("ST2Y", 9),
-    ("V", 2), ("ST3", 8), ("ST1", 10), ("t", 11), ("V", 3), ("SUB", 11), ("gx", 1), ("ST1", 11), ("ST2Y", 10),
-    ("ST3", 9), ("ST2X", 10), ("ST2X", 11), ("ST3", 10), ("E", 4), ("ST2Y", 11), ("ST4", 9), ("ST3", 11), ("ST4", 8),
-    ("ST4", 7), ("ST4", 10), ("V", 4), ("ST4", 11),
+    ("SO",), ("n2", 0), ("t", 0), ("SUB", 0), ("t", 1), ("SUB", 1), ("ST1", 0), ("g", 0, 0), ("ST1", 1), ("t", 2),
+    ("SUB", 2), ("g", 0, 1), ("t", 3), ("ST1", 2), ("gy", 0), ("n1", 0), ("ST2X", 0), ("to", 4), ("gc", 0), ("a", 0, 0),
+    ("SUB", 3), ("ST2Y", 0), ("a", 0, 1), ("ST1", 3), ("a", 0, 2), ("ST2Y", 1), ("ST2X", 1), ("ST3", 0), ("a", 0, 3),
+    ("a", 0, 4), ("ST2Y", 2), ("ST2X", 2), ("a", 0, 5), ("tv", 4), ("ST3", 1), ("ST2X", 3), ("ST2Y", 3), ("SUB", 4),
+    ("ST1", 4), ("ST4", 0), ("t", 5), ("ST3", 2), ("SUB", 5), ("ST1", 5), ("gx", 0), ("n2", 1), ("ST4", 1), ("t", 6),
+    ("ST4", 2), ("SUB", 6), ("ST3", 3), ("ST2X", 4), ("ST2Y", 4), ("t", 7), ("ST2Y", 5), ("ST2X", 5), ("ST1", 6),
+    ("ST3", 4), ("SUB", 7), ("g", 1, 0), ("ST4", 3), ("t", 8), ("ST1", 7), ("g", 1, 1), ("SUB", 8), ("ST3", 5),
+    ("ST4", 4), ("ST2X", 6), ("ST2Y", 6), ("ST1", 8), ("t", 9), ("gy", 1), ("n1", 1), ("SUB", 9), ("ST4", 5),
+    ("to", 10), ("ST3", 6), ("ST2X", 7), ("gc", 1), ("E", 0), ("ST2Y", 7), ("a", 1, 0), ("E", 1), ("a", 1, 1),
+    ("ST2Y", 8), ("ST2X", 8), ("ST1", 9), ("a", 1, 2), ("ST3", 7), ("a", 1, 3), ("ST3", 8), ("E", 2), ("a", 1, 4),
+    ("a", 1, 5), ("ST4", 6), ("ST2Y", 9), ("V", 0), ("ST4", 7), ("ST2X", 9), ("tv", 10), ("V", 1), ("SUB", 10),
+    ("E", 3), ("ST1", 10), ("t", 11), ("SUB", 11), ("V", 2), ("ST3", 9), ("ST4", 8), ("ST1", 11), ("ST2Y", 10),
+    ("ST2X", 10), ("E", 4), ("V", 3), ("ST2X", 11), ("gx", 1), ("ST3", 10), ("ST2Y", 11), ("ST4", 9), ("ST3", 11),
+    ("ST4", 10), ("V", 4), ("ST4", 11),
 )
 SPLIT = (3, 2, 2, 2, 2, 2, 2, 2, 2, 2, 2, 2)
 SLOTS = 5
@@ -708,6 +710,7 @@
                     wv, g, gh, n, r, low, act, dg, y1r, ctx, qkv, lse, xr, gc, gqkv, sums,
                     wsem, lsem, esem, *rest):
     p = Place(fold)
+    p.greet()
     m = p.y
     red = Reduce(p, 6 * layers, SLOTS, SPLIT, rest[0], shards, *rest[1:16])
     early = Total(p, *rest[16:19], rest[19:21])
@@ -876,21 +879,28 @@
     cload = pltpu.make_async_copy(cotf, low, esem.at[6])
     cload.start()
     begin(top, "n2", "r2", "act")
-    weights(0).start()
-    begin(top, "dg", "y1r")
-    weights(1).start()
-    begin(top, "ctx", "qkv", "lse", "xr")
     early.v[0] = jnp.zeros((ROWS, D), F32)
     late.v[0] = jnp.zeros((8, D), F32)
     cload.wait()
     g[...] = low[...].astype(F32)
     own_o.start()
-    p.greet()
     plan = list(BACKWARD)
+    met = False
     while plan:
         t = plan.pop(0)
         if t[0] != "a":
+            if t[0] in ("SO", "SUB") and not met:
+                p.greeted()
+                met = True
             steps[t[0]](*t[1:])
+            if t == ("SUB", 0):
+                begin(top, "dg")
+                weights(0).start()
+            elif t == ("SUB", 1):
+                begin(top, "y1r")
+                weights(1).start()
+            elif t == ("SUB", 2):
+                begin(top, "ctx", "qkv", "lse", "xr")
             continue
         inside = [[] for _ in range(6)]
         while (t[0], t[-1]) != ("a", 5):
@@ -929,47 +939,90 @@
     )(w, cotf, outx, glob, lengths, bucket, *saved)
 
 
-def pack(w_qkv, w_out, w_up, w_down):
-    parts = []
+def pack_kernel(w_qkv, w_out, w_up, w_down, bias_qv, bias_up, bias_out, ln_gain, ln_bias, packed, vec, glob):
+    vec[...] = jnp.zeros_like(vec)
+    glob[...] = jnp.zeros_like(glob)
     for l in range(w_qkv.shape[0]):
-        parts.append(jnp.concatenate([w_qkv[l, 0], w_qkv[l, 1], w_qkv[l, 2], w_out[l].T], 1))
-        parts.append(w_up[l])
-        parts.append(w_down[l].T)
-    return jnp.stack(parts)
+        for t in range(3):
+            packed[3 * l, :, HALF * t:HALF * t + HALF] = w_qkv[l, t]
+        packed[3 * l, :, 3 * HALF:] = w_out[l]
+        packed[3 * l + 1] = w_up[l]
+        packed[3 * l + 2] = w_down[l]
+        qv = bias_qv[l].astype(F32)
+        for t in range(2):
+            vec[2 + l:3 + l, HALF * t:HALF * t + HALF] = qv[t:t + 1]
+        for i, ref in enumerate((bias_out, ln_gain, ln_bias)):
+            glob[6 * l + 2 * i:6 * l + 2 * i + 2, :] = ref[l].astype(F32)
+    vec[0:2, :] = bias_up[...].astype(F32)
+
+
+def pack(*args):
+    layers = args[0].shape[0]
+    shape = jax.ShapeDtypeStruct
+    return pl.pallas_call(
+        pack_kernel,
+        out_shape=[shape((3 * layers, 48, UNITS), BF16), shape((8, UNITS), F32), shape((16, D), F32)],
+        in_specs=[VMEM] * len(args), out_specs=[VMEM] * 3,
+        compiler_params=pltpu.CompilerParams(vmem_limit_bytes=60 * 2**20))(*args)
+
+
+def unpack_kernel(layers, shards, early, late, out_in, ingrad_in,
+                  out, ingrad, qkv, qv, w_out, bias, gain, shift, up, bias_up, down):
+    m = lax.axis_index("mp")
+    mine = lambda a, b: jnp.where(m == 0, a, b)
+    out[...] = out_in[...]
+    ingrad[...] = ingrad_in[...]
+    for l in range(layers):
+        u = 6 * (layers - 1 - l)
+        base = 2 * u
+        for half in range(2):
+            cols = slice(PART * half, PART * half + PART)
+            down[l, :, cols] = shards[u + half]
+            up[l, :, cols] = shards[u + 2 + half]
+            bias_up[l:l + 1, cols] = mine(early[base + 6 + half:base + 7 + half, :], early[base + 8 + half:base + 9 + half, :])
+        qkv[l, 0] = shards[u + 5, :, :HALF]
+        qkv[l, 1] = shards[u + 5, :, HALF:]
+        qkv[l, 2] = shards[u + 4, :, :HALF]
+        w_out[l] = shards[u + 4, :, HALF:]
+        gain[l] = early[base:base + 2, :]
+        shift[l] = early[base + 2:base + 4, :]
+        bias[l] = early[base + 4:base + 6, :]
+        for t in range(2):
+            line = early[base + 10 + t:base + 11 + t, :] if l else late[t:t + 1, :]
+            qv[l, t:t + 1, :] = mine(line[:, :HALF], line[:, HALF:])
+
+
+def unpack(layers, *args):
+    shape = lambda *s: jax.ShapeDtypeStruct(s, F32)
+    rows = jax.ShapeDtypeStruct((2, S // 2, D), BF16)
+    return pl.pallas_call(
+        functools.partial(unpack_kernel, layers),
+        out_shape=[rows, rows, shape(layers, 3, 48, HALF), shape(layers, 2, HALF), shape(layers, 48, HALF), shape(layers, 2, D),
+                   shape(layers, 2, D), shape(layers, 2, D), shape(layers, 48, UNITS), shape(layers, UNITS),
+                   shape(layers, 48, UNITS)],
+        in_specs=[VMEM] * len(args), out_specs=[VMEM] * 11,
+        compiler_params=pltpu.CompilerParams(vmem_limit_bytes=60 * 2**20))(*args)
 
 
 def per_device(layer_input, cotangent, lengths, bucket, w_qkv, bias_qv, w_out, bias_out, ln_gain, ln_bias, w_up, bias_up, w_down):
     layers = w_qkv.shape[0]
     fold = lax.axis_size("dp") // GROUPS
     members = [[g * fold + i for i in range(fold)] for g in range(GROUPS)]
-    packed = pack(w_qkv, w_out, w_up, w_down)
     if fold > 1:
-        packed = lax.all_gather(packed, "dp", axis=1, tiled=True, axis_index_groups=members)
-    qv = jnp.pad(bias_qv.reshape(layers, 2 * HALF), ((0, 0), (0, UNITS - 2 * HALF)))
-    vec = jnp.concatenate([bias_up, qv], 0).astype(F32)
-    vec = jnp.pad(vec, ((0, 8 - vec.shape[0]), (0, 0)))
-    glob = jnp.concatenate([bias_out, ln_gain, ln_bias], 1).astype(F32).reshape(6 * layers, D)
-    glob = jnp.pad(glob, ((0, 16 - 6 * layers), (0, 0)))
+        join = lambda v, axis: lax.all_gather(v, "dp", axis=axis, tiled=True, axis_index_groups=members)
+        w_qkv, w_out, w_up, w_down = join(w_qkv, 2), join(w_out, 2), join(w_up, 1), join(w_down, 2)
+    turn = lambda v: v.transpose(0, 2, 1)
+    packed, vec, glob = pack(w_qkv, turn(w_out), w_up, turn(w_down), bias_qv, bias_up, bias_out, ln_gain, ln_bias)
     w, cotf, out, *saved = forward(packed, layer_input, cotangent, vec, glob, lengths, bucket, layers, fold)
     output, ingrad, shards, early, late = backward(
         w, cotf.reshape(S, D), out.reshape(2, S // 2, D), glob, lengths, bucket, saved, layers, fold)
+    output, ingrad, qkv, qv, w_out, bias, gain, shift, up, bias_up, down = unpack(layers, shards, early, late, output, ingrad)
+    w_out, down = turn(w_out), turn(down)
     if fold > 1:
-        shards = lax.psum_scatter(shards, "dp", scatter_dimension=1, tiled=True, axis_index_groups=members)
-        early, late = lax.psum((early, late), "dp", axis_index_groups=members)
-    rows = shards.shape[1]
-    part = lax.axis_index("mp")
-    shards = jnp.flip(shards.reshape(layers, 6, rows, PART), 0)
-    down, up, vo, qk = shards[:, 0:2], shards[:, 2:4], shards[:, 4], shards[:, 5]
-    grad_qkv = jnp.stack([qk[..., :HALF], qk[..., HALF:], vo[..., :HALF]], 1)
-    grad_out = vo[..., HALF:].transpose(0, 2, 1)
-    grad_up = up.transpose(0, 2, 1, 3).reshape(layers, rows, UNITS)
-    grad_down = down.transpose(0, 1, 3, 2).reshape(layers, UNITS, rows)
-    vecs = jnp.flip(early.reshape(layers, 12, D), 0)
-    gain, shift, bias = vecs[:, 0:2], vecs[:, 2:4], vecs[:, 4:6]
-    grad_bias_up = lax.dynamic_slice_in_dim(vecs[:, 6:10].reshape(layers, 2, UNITS), part, 1, 1)[:, 0]
-    qv = jnp.concatenate([late[None, 0:2], vecs[1:, 10:12]], 0)
-    qv = lax.dynamic_slice_in_dim(qv, part * HALF, HALF, 2)
-    return output, ingrad, grad_qkv, qv, grad_out, bias, gain, shift, grad_up, grad_bias_up, grad_down
+        part = lambda v, axis: lax.psum_scatter(v, "dp", scatter_dimension=axis, tiled=True, axis_index_groups=members)
+        qkv, w_out, up, down = part(qkv, 2), part(w_out, 2), part(up, 1), part(down, 2)
+        qv, bias, gain, shift, bias_up = lax.psum((qv, bias, gain, shift, bias_up), "dp", axis_index_groups=members)
+    return output, ingrad, qkv, qv, w_out, bias, gain, shift, up, bias_up, down
 
 
 def solution(mesh):

time: 318 us -> 286 us (0.90)
  local copies, waits for them, and re-layouts: 17 us -> 0 us
  Pallas kernels: 293 us -> 282 us
  other arithmetic: 3.49 us -> 0 us
    pallas_call x1, Pallas kernels: 154 us -> 143 us  [backward(): pl.pallas_call(functools.partial(backward_kernel, fold, layers), out_shap...]
    unnamed x18 -> x0, local copies, waits for them, and re-layouts: 7.8 us -> none
    pallas_call x0 -> x2, Pallas kernels: none -> 6.01 us  [the longest x1 3.77 us: unpack(): pl.pallas_call(functools.partial(unpack_kernel, layers), out_shape=[rows,...]
    pallas_call x1, Pallas kernels: 139 us -> 133 us  [forward(): pl.pallas_call(functools.partial(forward_kernel, fold, layers), out_shape...]
    slice x8 -> x0, local copies, waits for them, and re-layouts: 3.19 us -> none  [the longest x4 1.82 us: per_device(): gain, shift, bias = (vecs[:, 0:2], vecs[:, 2:4], vecs[:, 4:6])]
where the time goes in v4:
time: 286 us; the launch traced here: 283 us
  Pallas kernels  282 us (99%)
    pallas_call x1, Pallas kernels, backward(): pl.pallas_call(functools.partial(backward_kernel, fold, layers), out_shap...  143 us
    pallas_call x1, Pallas kernels, forward(): pl.pallas_call(functools.partial(forward_kernel, fold, layers), out_shape...  133 us

profile of v4, /device:TPU:0, one launch (start us, length us, event | category | flops | bytes accessed | tf_op | source)
XLA Modules:
  0.0 283.1 jit_solution(6540783447775248584)
XLA Ops:
  0.6 2.2 shard_map.212
  2.9 132.7 %shard_map.213 = (bf16[6,2,4,2,2,48,1536]{6,5,4,3,2,1,0:T(8,128)(2,1)}, bf16[2,256,768]{2,1,0:T(8,128)(2,1)}, bf16[512,768]{1,0:T(8,128)(2,1)}, bf16[2,512,768]{...) custom-call(bf16[6,48,1536]{2,1,0:T(8,128)(2,1)} %get-tuple-element., ...), custom_call_target="tpu_custom_call" | custom-call | tf_op jit(solution)/shard_map/pallas_call | solution.py:488
  135.6 143.5 %shard_map.214 = (bf16[2,256,768]{2,1,0:T(8,128)(2,1)}, bf16[2,256,768]{2,1,0:T(8,128)(2,1)}, f32[12,48,768]{2,1,0:T(8,128)}, f32[24,768]{1,0:T(8,128)}, f32[8,768]{1,0:T(8,128)}) custom-call(bf16[6,2,4,2,2,48,1536]{6,5,4,3,2,1,0:T(8,128)(2,1)} %get-tuple-element.47.w, bf16[512,768]{1,0:T(8,128)(2,1)} %bitcast.6, bf16[2,256,768]{2,1,0:T(8,128)(2,1)} %bitcast.7, ...), custom_call_target="tpu_custom_call" | custom-call | tf_op jit(solution)/shard_map/pallas_call | solution.py:926
  279.1 3.8 %shard_map.215 = (bf16[2,256,768]{2,1,0:T(8,128)(2,1)}, bf16[2,256,768]{2,1,0:T(8,128)(2,1)}, f32[2,3,48,384]{3,2,1,0:T(8,128)}, f32[2,2,384]{2,1,0:T(2,128)}, f...) custom-call(f32[12,48,768]{2,1,0:T(8,128)} %get-tuple-element.61.sha, ...), custom_call_target="tpu_custom_call" | custom-call | tf_op jit(solution)/shard_map/pallas_call | solution.py:998

commit v5 on v4

--- a/solution.py
+++ b/solution.py
@@ -683,20 +683,20 @@
 
 
 BACKWARD = (
-    ("SO",), ("n2", 0), ("t", 0), ("SUB", 0), ("t", 1), ("SUB", 1), ("ST1", 0), ("g", 0, 0), ("ST1", 1), ("t", 2),
-    ("SUB", 2), ("g", 0, 1), ("t", 3), ("ST1", 2), ("gy", 0), ("n1", 0), ("ST2X", 0), ("to", 4), ("gc", 0), ("a", 0, 0),
-    ("SUB", 3), ("ST2Y", 0), ("a", 0, 1), ("ST1", 3), ("a", 0, 2), ("ST2Y", 1), ("ST2X", 1), ("ST3", 0), ("a", 0, 3),
-    ("a", 0, 4), ("ST2Y", 2), ("ST2X", 2), ("a", 0, 5), ("tv", 4), ("ST3", 1), ("ST2X", 3), ("ST2Y", 3), ("SUB", 4),
-    ("ST1", 4), ("ST4", 0), ("t", 5), ("ST3", 2), ("SUB", 5), ("ST1", 5), ("gx", 0), ("n2", 1), ("ST4", 1), ("t", 6),
-    ("ST4", 2), ("SUB", 6), ("ST3", 3), ("ST2X", 4), ("ST2Y", 4), ("t", 7), ("ST2Y", 5), ("ST2X", 5), ("ST1", 6),
-    ("ST3", 4), ("SUB", 7), ("g", 1, 0), ("ST4", 3), ("t", 8), ("ST1", 7), ("g", 1, 1), ("SUB", 8), ("ST3", 5),
-    ("ST4", 4), ("ST2X", 6), ("ST2Y", 6), ("ST1", 8), ("t", 9), ("gy", 1), ("n1", 1), ("SUB", 9), ("ST4", 5),
-    ("to", 10), ("ST3", 6), ("ST2X", 7), ("gc", 1), ("E", 0), ("ST2Y", 7), ("a", 1, 0), ("E", 1), ("a", 1, 1),
-    ("ST2Y", 8), ("ST2X", 8), ("ST1", 9), ("a", 1, 2), ("ST3", 7), ("a", 1, 3), ("ST3", 8), ("E", 2), ("a", 1, 4),
-    ("a", 1, 5), ("ST4", 6), ("ST2Y", 9), ("V", 0), ("ST4", 7), ("ST2X", 9), ("tv", 10), ("V", 1), ("SUB", 10),
-    ("E", 3), ("ST1", 10), ("t", 11), ("SUB", 11), ("V", 2), ("ST3", 9), ("ST4", 8), ("ST1", 11), ("ST2Y", 10),
-    ("ST2X", 10), ("E", 4), ("V", 3), ("ST2X", 11), ("gx", 1), ("ST3", 10), ("ST2Y", 11), ("ST4", 9), ("ST3", 11),
-    ("ST4", 10), ("V", 4), ("ST4", 11),
+    ("SO",), ("n2", 0), ("t", 0), ("SUB", 0), ("t", 1), ("ST1", 0), ("g", 0, 0), ("SUB", 1), ("t", 2), ("g", 0, 1),
+    ("ST1", 1), ("t", 3), ("SUB", 3), ("SUB", 2), ("gy", 0), ("ST2Y", 0), ("ST2X", 0), ("n1", 0), ("ST1", 2), ("to", 4),
+    ("gc", 0), ("ST2Y", 1), ("a", 0, 0), ("ST3", 0), ("a", 0, 1), ("ST2X", 1), ("a", 0, 2), ("ST1", 3), ("ST2X", 2),
+    ("a", 0, 3), ("a", 0, 4), ("a", 0, 5), ("ST2Y", 2), ("tv", 4), ("ST4", 0), ("ST3", 1), ("ST2X", 3), ("SUB", 4),
+    ("ST2Y", 3), ("t", 5), ("ST3", 2), ("SUB", 5), ("ST1", 4), ("gx", 0), ("ST4", 1), ("ST3", 3), ("ST1", 5), ("n2", 1),
+    ("ST2Y", 4), ("t", 6), ("ST2X", 4), ("ST4", 2), ("t", 7), ("SUB", 7), ("g", 1, 0), ("ST2X", 5), ("SUB", 6),
+    ("ST4", 3), ("ST2Y", 5), ("ST3", 4), ("ST1", 6), ("ST1", 7), ("t", 8), ("g", 1, 1), ("ST3", 5), ("ST4", 4),
+    ("t", 9), ("gy", 1), ("ST2Y", 6), ("ST2X", 6), ("n1", 1), ("ST4", 5), ("E", 0), ("SUB", 9), ("to", 10), ("ST2X", 7),
+    ("E", 1), ("gc", 1), ("SUB", 8), ("ST2Y", 7), ("a", 1, 0), ("E", 2), ("ST1", 8), ("ST3", 6), ("a", 1, 1),
+    ("ST1", 9), ("ST3", 7), ("a", 1, 2), ("a", 1, 3), ("a", 1, 4), ("E", 3), ("a", 1, 5), ("ST2Y", 8), ("ST2X", 8),
+    ("ST4", 6), ("tv", 10), ("SUB", 10), ("ST2Y", 9), ("ST2X", 9), ("V", 0), ("t", 11), ("ST3", 8), ("V", 1),
+    ("ST1", 10), ("V", 2), ("SUB", 11), ("ST3", 9), ("ST4", 7), ("E", 4), ("ST1", 11), ("ST2X", 10), ("ST2Y", 10),
+    ("ST4", 8), ("V", 3), ("ST2X", 11), ("ST2Y", 11), ("ST3", 10), ("gx", 1), ("ST3", 11), ("ST4", 9), ("ST4", 10),
+    ("V", 4), ("ST4", 11),
 )
 SPLIT = (3, 2, 2, 2, 2, 2, 2, 2, 2, 2, 2, 2)
 SLOTS = 5

time: 286 us -> 285 us (level)
  no operation moved by 1% of the time
where the time goes in v5:
time: 285 us; the launch traced here: 281 us
  Pallas kernels  281 us (99%)
    pallas_call x1, Pallas kernels, backward(): pl.pallas_call(functools.partial(backward_kernel, fold, layers), out_shap...  142 us
    pallas_call x1, Pallas kernels, forward(): pl.pallas_call(functools.partial(forward_kernel, fold, layers), out_shape...  133 us

profile of v5, /device:TPU:0, one launch (start us, length us, event | category | flops | bytes accessed | tf_op | source)
XLA Modules:
  0.0 281.5 jit_solution(4228293621639169091)
XLA Ops:
  0.6 2.2 shard_map.212
  2.9 132.8 %shard_map.213 = (bf16[6,2,4,2,2,48,1536]{6,5,4,3,2,1,0:T(8,128)(2,1)}, bf16[2,256,768]{2,1,0:T(8,128)(2,1)}, bf16[512,768]{1,0:T(8,128)(2,1)}, bf16[2,512,768]{...) custom-call(bf16[6,48,1536]{2,1,0:T(8,128)(2,1)} %get-tuple-element., ...), custom_call_target="tpu_custom_call" | custom-call | tf_op jit(solution)/shard_map/pallas_call | solution.py:488
  135.7 141.7 %shard_map.214 = (bf16[2,256,768]{2,1,0:T(8,128)(2,1)}, bf16[2,256,768]{2,1,0:T(8,128)(2,1)}, f32[12,48,768]{2,1,0:T(8,128)}, f32[24,768]{1,0:T(8,128)}, f32[8,768]{1,0:T(8,128)}) custom-call(bf16[6,2,4,2,2,48,1536]{6,5,4,3,2,1,0:T(8,128)(2,1)} %get-tuple-element.47.w, bf16[512,768]{1,0:T(8,128)(2,1)} %bitcast.6, bf16[2,256,768]{2,1,0:T(8,128)(2,1)} %bitcast.7, ...), custom_call_target="tpu_custom_call" | custom-call | tf_op jit(solution)/shard_map/pallas_call | solution.py:926
  277.4 3.8 %shard_map.215 = (bf16[2,256,768]{2,1,0:T(8,128)(2,1)}, bf16[2,256,768]{2,1,0:T(8,128)(2,1)}, f32[2,3,48,384]{3,2,1,0:T(8,128)}, f32[2,2,384]{2,1,0:T(2,128)}, f...) custom-call(f32[12,48,768]{2,1,0:T(8,128)} %get-tuple-element.61.sha, ...), custom_call_target="tpu_custom_call" | custom-call | tf_op jit(solution)/shard_map/pallas_call | solution.py:998

commit v6 on v5

--- a/solution.py
+++ b/solution.py
@@ -649,19 +649,17 @@
     bias = key_bias(limits)
     lane = lax.broadcasted_iota(jnp.int32, (S, 128), 1)
     k2t = k2.T
-    gq, gk, gv = [], [], []
-    for half in range(2):
-        qm, km = with_mask(q2, k2, half, bias)
-        st = dot(km, qm, NT)
-        probs = jnp.exp(st - lse[pair * 2 + half])
-        vm = jnp.where((lane // 64) == half, v2, jnp.zeros_like(v2))
-        gp = dot(vm, c2, NT)
-        prod = probs * gp
-        total = jnp.sum(prod, axis=0, keepdims=True)
-        gs = (prod - probs * total).astype(BF16)
-        gv.append(dot(probs.astype(BF16), c2))
-        gk.append(dot(gs, q2))
-        gq.append(dot(k2t[64 * half:64 * half + 64], gs))
+    both = range(2)
+    masked = [with_mask(q2, k2, h, bias) for h in both]
+    st = [dot(km, qm, NT) for qm, km in masked]
+    gp = [dot(jnp.where((lane // 64) == h, v2, jnp.zeros_like(v2)), c2, NT) for h in both]
+    probs = [jnp.exp(st[h] - lse[pair * 2 + h]) for h in both]
+    gv = [dot(probs[h].astype(BF16), c2) for h in both]
+    prod = [probs[h] * gp[h] for h in both]
+    total = [jnp.sum(prod[h], axis=0, keepdims=True) for h in both]
+    gs = [(prod[h] - probs[h] * total[h]).astype(BF16) for h in both]
+    gk = [dot(gs[h], q2) for h in both]
+    gq = [dot(k2t[64 * h:64 * h + 64], gs[h]) for h in both]
     pick = lambda v: jnp.where(lane < 64, v[0], v[1])
     gqt = jnp.concatenate(gq, 0).T * 0.125
     gkt = pick(gk) * 0.125
@@ -707,7 +705,7 @@
 def backward_kernel(fold, layers, w, cotf, outx, glob, lengths, bucket,
                     xr_o, qkv_o, lse_o, ctx_o, n1_o, r1_o, y1r_o, act_o, dg_o, n2_o, r2_o,
                     output, ingrad, shards, vout, vlate,
-                    wv, g, gh, n, r, low, act, dg, y1r, ctx, qkv, lse, xr, gc, gqkv, sums,
+                    wv, g, gh, n, r, low, act, dg, y1r, ctx, qkv, lse, xr, gc, sums,
                     wsem, lsem, esem, *rest):
     p = Place(fold)
     p.greet()
@@ -716,6 +714,7 @@
     early = Total(p, *rest[16:19], rest[19:21])
     late = Total(p, *rest[21:24], rest[24:26])
     limits = bounds(lengths, bucket, m)
+    gqkv = qkv
     order = [3 * l + t for l in reversed(range(layers)) for t in (2, 1, 0)]
     full = slice(0, UNITS)
 
@@ -933,7 +932,7 @@
             vm((2, 2, 4, 2, 2, 48, UNITS), BF16), vm((S, D), F32), vm((S, D), F32), vm((S, D), F32), vm((S, 128), F32),
             vm((S, D), BF16), vm((2, S, UNITS), BF16), vm((2, S, UNITS), BF16), vm((S, D), BF16),
             vm((2, S, HALF), BF16), vm((2, S, 3 * HALF), BF16), vm((12, 1, S), F32), vm((S, D), BF16), vm((2, S, HALF), BF16),
-            vm((2, S, 3 * HALF), BF16), vm((2, 2, 1, HALF), F32),
+            vm((2, 2, 1, HALF), F32),
             dma((2,)), dma((11,)), dma((7,)), *first, *rest, *Total.scratch(ROWS), *Total.scratch(8)],
         compiler_params=pltpu.CompilerParams(collective_id=2, has_side_effects=True, vmem_limit_bytes=62 * 2**20),
     )(w, cotf, outx, glob, lengths, bucket, *saved)

time: 285 us -> 285 us (level)
  no operation moved by 1% of the time
where the time goes in v6:
time: 285 us; the launch traced here: 281 us
  Pallas kernels  281 us (99%)
    pallas_call x1, Pallas kernels, backward(): pl.pallas_call(functools.partial(backward_kernel, fold, layers), out_shap...  142 us
    pallas_call x1, Pallas kernels, forward(): pl.pallas_call(functools.partial(forward_kernel, fold, layers), out_shape...  133 us

profile of v6, /device:TPU:0, one launch (start us, length us, event | category | flops | bytes accessed | tf_op | source)
XLA Modules:
  0.0 281.5 jit_solution(16211169835423864153)
XLA Ops:
  0.6 2.2 shard_map.212
  2.9 132.8 %shard_map.213 = (bf16[6,2,4,2,2,48,1536]{6,5,4,3,2,1,0:T(8,128)(2,1)}, bf16[2,256,768]{2,1,0:T(8,128)(2,1)}, bf16[512,768]{1,0:T(8,128)(2,1)}, bf16[2,512,768]{...) custom-call(bf16[6,48,1536]{2,1,0:T(8,128)(2,1)} %get-tuple-element., ...), custom_call_target="tpu_custom_call" | custom-call | tf_op jit(solution)/shard_map/pallas_call | solution.py:488
  135.7 141.7 %shard_map.214 = (bf16[2,256,768]{2,1,0:T(8,128)(2,1)}, bf16[2,256,768]{2,1,0:T(8,128)(2,1)}, f32[12,48,768]{2,1,0:T(8,128)}, f32[24,768]{1,0:T(8,128)}, f32[8,768]{1,0:T(8,128)}) custom-call(bf16[6,2,4,2,2,48,1536]{6,5,4,3,2,1,0:T(8,128)(2,1)} %get-tuple-element.47.w, bf16[512,768]{1,0:T(8,128)(2,1)} %bitcast.6, bf16[2,256,768]{2,1,0:T(8,128)(2,1)} %bitcast.7, ...), custom_call_target="tpu_custom_call" | custom-call | tf_op jit(solution)/shard_map/pallas_call | solution.py:925
  277.4 3.8 %shard_map.215 = (bf16[2,256,768]{2,1,0:T(8,128)(2,1)}, bf16[2,256,768]{2,1,0:T(8,128)(2,1)}, f32[2,3,48,384]{3,2,1,0:T(8,128)}, f32[2,2,384]{2,1,0:T(2,128)}, f...) custom-call(f32[12,48,768]{2,1,0:T(8,128)} %get-tuple-element.61.sha, ...), custom_call_target="tpu_custom_call" | custom-call | tf_op jit(solution)/shard_map/pallas_call | solution.py:997
